TPU v7x, 32 devices: a whole 2x2x4 slice. The times are simulated.
32 devices in a mesh: prompts: 2 (over x), beam: 16 (over z, y, core).
Axes of the slice: x: 2, y: 2, z: 4, core: 2. Of those that a mesh axis runs over, the one named last changes fastest.
Arguments:
- queries: bfloat16 [128, 256, 4096], P(('prompts', 'beam')), parts along dimension 0, may hold values from -4.375 to 4.375
- new_keys: bfloat16 [128, 256, 1024], P(('prompts', 'beam')), parts along dimension 0, may hold values from -4.375 to 4.375
- new_values: bfloat16 [128, 256, 1024], P(('prompts', 'beam')), parts along dimension 0, may hold values from -6 to 6
- step_kv: bfloat16 [128, 2, 64, 1024], P(('prompts', 'beam')), parts along dimension 0, may hold values from -6 to 6
- prm_last: bfloat16 [128, 4096], P(('prompts', 'beam')), parts along dimension 0, may hold values from -6 to 6
- value_head: float32 [4096], replicated, may hold values from -0.09375 to 0.09375
- parents: int32 [128], P('prompts'), parts along dimension 0, may hold values from 0 to 63, as said below
Outputs:
- attended: bfloat16 [128, 256, 4096], P(('prompts', 'beam')), parts along dimension 0
- child_share: float32 [128], P(('prompts', 'beam')), parts along dimension 0
There are 2 independent parts, one for each index of `prompts`. A program takes and returns all parts, laid end to end along the dimension named above; an argument that names none is the same for every part. Nothing has to cross between parts.
Inputs may be any that keep to these rules, and one draw needn't show every extreme that they name: `parents`: on every device exactly 2 of its 4 beams are the parent of one or more children and the other beams of none.
All inputs are finite; a program needn't handle non-finite values.
Results may differ from a plain program's by a relative error of at most 0.008.
Values may be sent and summed in bfloat16 or wider, within the bound.
No kernel may reach another device: no remote copies, remote signals or barrier semaphores. Data moves between devices by JAX's collectives and lax.ppermute only.
A program may use at most 192 MiB of HBM per device.

v0:
```python
import jax
import jax.numpy as jnp
from jax import lax
from jax.sharding import PartitionSpec as P

HEAD_SIZE = 128
KEEP = 2


def attend_child(operands):
    query, keys, values = operands
    total_len = keys.shape[0]
    new_len = query.shape[0]
    step_len = total_len - new_len
    kv_width = keys.shape[1]
    kv_heads = kv_width // HEAD_SIZE
    group = query.shape[1] // kv_width
    query_head_rows = query.reshape(new_len, kv_heads, group, HEAD_SIZE)
    key_head_rows = keys.reshape(total_len, kv_heads, HEAD_SIZE)
    value_head_rows = values.reshape(total_len, kv_heads, HEAD_SIZE)
    attention_scores = jnp.einsum(
        "yfli,xfi->flyx", query_head_rows, key_head_rows, preferred_element_type=jnp.float32
    ) * HEAD_SIZE ** (-0.5)
    column = jnp.arange(total_len)[None, :]
    row_pos = jnp.arange(new_len)[:, None]
    visible = (column < step_len) | (column - step_len <= row_pos)
    attention_scores = jnp.where(visible, attention_scores, -jnp.inf)
    attention_weights = jax.nn.softmax(attention_scores, axis=-1).astype(jnp.bfloat16)
    attended_values = jnp.einsum(
        "fjip,pfa->ifja", attention_weights, value_head_rows, preferred_element_type=jnp.float32
    )
    return attended_values.reshape(new_len, -1).astype(jnp.bfloat16)


def body(queries, new_keys, new_values, step_kv, prm_last, value_head, parents):
    beam_count = lax.axis_size("beam")
    group_index = lax.axis_index("beam")
    local = queries.shape[0]
    children = parents.shape[0]
    step_len = step_kv.shape[2]
    kv_width = step_kv.shape[3]
    mine = lax.dynamic_slice_in_dim(parents, group_index * local, local)
    hidden = prm_last.astype(jnp.float32)
    square = jnp.mean(hidden * hidden, axis=-1, keepdims=True)
    normed = hidden * lax.rsqrt(square + 1e-05)
    score = jnp.dot(normed, value_head, precision=lax.Precision.HIGHEST)
    reward = jax.nn.sigmoid(score).astype(jnp.bfloat16)
    flat_kv = step_kv.reshape(local, -1)
    beams_all = beam_count * local
    hits = jnp.sum(
        (parents[None, :] == jnp.arange(beams_all, dtype=jnp.int32)[:, None]).astype(jnp.int32),
        axis=1,
    )
    kept = (hits > 0).astype(jnp.int32).reshape(beam_count, local)
    order = jnp.cumsum(kept, axis=1) - 1
    slot_rank = jnp.arange(KEEP, dtype=jnp.int32)
    slot_table = (kept[:, None, :] == 1) & (order[:, None, :] == slot_rank[None, :, None])
    local_pos = jnp.arange(local, dtype=jnp.int32)
    slot_beam = (
        jnp.arange(beam_count, dtype=jnp.int32)[:, None] * local
        + jnp.sum(slot_table.astype(jnp.int32) * local_pos[None, None, :], axis=-1)
    ).reshape(-1)
    own_slots = lax.dynamic_index_in_dim(slot_table, group_index, 0, keepdims=False)
    packed_kv = jnp.dot(
        own_slots.astype(jnp.bfloat16), flat_kv, preferred_element_type=jnp.float32
    ).astype(jnp.bfloat16)
    packed_reward = jnp.dot(own_slots.astype(jnp.float32), reward.astype(jnp.float32)).astype(
        jnp.bfloat16
    )
    block = lax.all_gather(packed_kv, "beam", axis=0, tiled=True)
    marks = lax.all_gather(packed_reward, "beam", axis=0, tiled=True)
    match = mine[:, None] == slot_beam[None, :]
    copied = jnp.dot(match.astype(jnp.bfloat16), block, preferred_element_type=jnp.float32)
    picked = jnp.dot(match.astype(jnp.float32), marks.astype(jnp.float32))
    copied, child_reward = (copied, picked)
    total = lax.psum(jnp.sum(child_reward), "beam")
    child_share = children * child_reward / total
    copied_kv = copied.astype(jnp.bfloat16).reshape(local, 2, step_len, kv_width)
    keys_all = jnp.concatenate([copied_kv[:, 0], new_keys], axis=1)
    values_all = jnp.concatenate([copied_kv[:, 1], new_values], axis=1)
    attended = lax.map(attend_child, (queries, keys_all, values_all))
    return (attended, child_share)


def solution(mesh):
    in_specs = (
        P(("prompts", "beam"), None, None),
        P(("prompts", "beam"), None, None),
        P(("prompts", "beam"), None, None),
        P(("prompts", "beam"), None, None, None),
        P(("prompts", "beam"), None),
        P(),
        P("prompts"),
    )
    out_specs = (P(("prompts", "beam"), None, None), P(("prompts", "beam")))
    return jax.shard_map(body, mesh=mesh, in_specs=in_specs, out_specs=out_specs, check_vma=False)
```

profile of v0, /device:TPU:0, one launch (start us, length us, event | category | flops | bytes accessed | tf_op | source)
XLA Modules:
  0.0 220.7 jit_solution(13043537023212435444)
XLA Ops:
  8.3 2.0 copy.47
  10.7 1.5 fusion.20
  14.5 35.8 %all-reduce = bf16[32]{0:T(256)(128)(2,1)S(1)} all-reduce(bf16[32]{0:T(256)(128)(2,1)S(1)} %dynamic-update-slice), channel_id=1, replica_groups=mesh['prompts'=2,'beam'=16] {'beam'}, use_global_device_ids=true, to_apply=%add | all-reduce | flops 32 | bytes 128
  51.3 31.2 %psum.7 = f32[]{:T(128)} all-reduce(f32[]{:T(128)} %get-tuple-element.109), channel_id=1, replica_groups=mesh['prompts'=2,'beam'=16] {'beam'}, use_global_device_ids=true, to_apply=%region_9.10 | all-reduce | flops 1 | bytes 8 | tf_op jit(solution)/shard_map/psum | solution.py:76
  83.7 7.1 %all-gather.3.cloned.1.call-done = bf16[16,2,131072]{2,1,0:T(2,128)(2,1)} async-done(((bf16[1,2,131072]{2,1,0:T(2,128)(2,1)}), bf16[16,2,131072]{2,1,0:T(2,128)(2,1)}) %all-gather.3.cloned.1.call-update) | async-done | bytes 8388624 | tf_op jit(solution)/shard_map/all_gather | solution.py:70
  90.8 8.4 %reshape.120 = bf16[32,131072]{1,0:T(8,128)(2,1)} reshape(bf16[16,2,131072]{2,1,0:T(2,128)(2,1)} %all-gather.3.cloned.1.call-done) | data formatting | bytes 16777216
  99.2 4.6 %convolution_convert_fusion = bf16[4,131072]{1,0:T(4,128)(2,1)S(1)} fusion(bf16[32,131072]{1,0:T(8,128)(2,1)} %reshape.120, s32[32]{0:T(128)S(1)} %add.58, s32[4]{0:T(128)S(1)} %dynamic_slice.27), kind=kOutput, calls=%fused_computation.25 | convolution fusion | flops 34078848 | bytes 9437328 | tf_op jit(solution)/shard_map/dot_general | solution.py:73
  106.1 2.6 %pad_maximum_fusion = (bf16[4,320,1024]{2,1,0:T(8,128)(2,1)}, bf16[4,320,1024]{2,1,0:T(8,128)(2,1)}) fusion(bf16[4,256,1024]{2,1,0:T(8,128)(2,1)S(1)} %copy-done.2, bf16[4,64,1024]{2,1,0:T(8,128)(2,1)S(1)} %get-tuple-element.108, bf16[4,256,1024]{2,1,0:T(8,128)(2,1)S(1)} %copy-done.3, bf16[4,64,1024]{2,1,0:T(8,128)(2,1)S(1)} %get-tuple-element.107), kind=kLoop, calls=%fused_computation.28 | loop fusion | flops 10485760 | bytes 10485760 | tf_op jit(solution)/shard_map/concatenate | solution.py:80
  108.7 104.4 %while.12 = (s32[]{:T(128)}, bf16[4,256,4096]{2,1,0:T(8,128)(2,1)}, bf16[4,320,1024]{2,1,0:T(8,128)(2,1)}, bf16[4,320,1024]{2,1,0:T(8,128)(2,1)}, bf16[4,256,4096]{2,1,0:T(8,128)(2,1)}, /*index=5*/s32[]{:T(128)}) while((s32[]{:T(128)}, bf16[4,256,4096]{2,1,0:T(8,128)(2,1)}, bf16[4,320,1024]{2,1,0:T(8,128)(2,1)}, ...), condition=%wide.region_6.7_spmd, body=%wide.region_3.0_spmd.sunk | while | flops 1359119360 | bytes 48729304 | solution.py:81
  110.5 1.7 constant_dynamic-slice_fusion.2
  112.3 2.5 %copy.71 = bf16[1,256,4096]{1,2,0:T(8,128)(2,1)} copy(bf16[1,256,4096]{2,1,0:T(8,128)(2,1)S(1)} %constant_dynamic-slice_fusion.2) | data formatting | bytes 4194304 | tf_op jit(solution)/shard_map/while/body/jit(dynamic_index_in_dim)/dynamic_slice | solution.py:81
  114.8 9.1 %fusion.59 = (f32[8,4,256]{2,1,0:T(4,128)S(1)}, f32[8,4,256,320]{2,3,1,0:T(8,128)}) fusion(pred[256,320]{0,1:T(8,128)(4,1)S(1)} %fusion.58, bf16[256,8,4,128]{0,3,2,1:T(8,128)(2,1)} %bitcast.97, bf16[320,8,128,1]{2,1,0,3:T(8,128)(2,1)S(1)} %bitcast.100), kind=kOutput, calls=%fused_computation.65.clone.1 | convolution fusion | flops 681574720 | bytes 13352960 | tf_op jit(solution)/shard_map/while/body/eval_jaxpr/sub | solution.py:28
  123.8 6.6 %fusion.60 = bf16[8,128,4,256]{3,1,2,0:T(8,128)(2,1)} fusion(f32[8,4,256,320]{2,3,1,0:T(8,128)} %get-tuple-element.149, f32[8,4,256]{2,1,0:T(4,128)S(1)} %get-tuple-element.150, bf16[320,8,128,1]{2,1,0,3:T(8,128)(2,1)S(1)} %bitcast.99), kind=kOutput, calls=%fused_computation.9.clone.1 | convolution fusion | flops 677380096 | bytes 13271040 | tf_op jit(solution)/shard_map/while/body/eval_jaxpr/fjip,pfa->ifja/dot_general | solution.py:29
  130.4 2.9 %copy.74 = bf16[1,256,4096]{2,1,0:T(8,128)(2,1)S(1)} copy(bf16[1,256,4096]{1,2,0:T(8,128)(2,1)} %bitcast.98) | data formatting | bytes 4194304 | tf_op jit(solution)/shard_map/while/body/jit(dynamic_update_index_in_dim)/dynamic_update_slice | solution.py:81
  133.4 1.5 constant_dynamic-update-slice_fusion.2
  136.6 1.7 constant_dynamic-slice_fusion.2
  138.4 2.5 %copy.71 = bf16[1,256,4096]{1,2,0:T(8,128)(2,1)} copy(bf16[1,256,4096]{2,1,0:T(8,128)(2,1)S(1)} %constant_dynamic-slice_fusion.2) | data formatting | bytes 4194304 | tf_op jit(solution)/shard_map/while/body/jit(dynamic_index_in_dim)/dynamic_slice | solution.py:81
  140.9 9.1 %fusion.59 = (f32[8,4,256]{2,1,0:T(4,128)S(1)}, f32[8,4,256,320]{2,3,1,0:T(8,128)}) fusion(pred[256,320]{0,1:T(8,128)(4,1)S(1)} %fusion.58, bf16[256,8,4,128]{0,3,2,1:T(8,128)(2,1)} %bitcast.97, bf16[320,8,128,1]{2,1,0,3:T(8,128)(2,1)S(1)} %bitcast.100), kind=kOutput, calls=%fused_computation.65.clone.1 | convolution fusion | flops 681574720 | bytes 13352960 | tf_op jit(solution)/shard_map/while/body/eval_jaxpr/sub | solution.py:28
  150.0 6.6 %fusion.60 = bf16[8,128,4,256]{3,1,2,0:T(8,128)(2,1)} fusion(f32[8,4,256,320]{2,3,1,0:T(8,128)} %get-tuple-element.149, f32[8,4,256]{2,1,0:T(4,128)S(1)} %get-tuple-element.150, bf16[320,8,128,1]{2,1,0,3:T(8,128)(2,1)S(1)} %bitcast.99), kind=kOutput, calls=%fused_computation.9.clone.1 | convolution fusion | flops 677380096 | bytes 13271040 | tf_op jit(solution)/shard_map/while/body/eval_jaxpr/fjip,pfa->ifja/dot_general | solution.py:29
  156.6 2.9 %copy.74 = bf16[1,256,4096]{2,1,0:T(8,128)(2,1)S(1)} copy(bf16[1,256,4096]{1,2,0:T(8,128)(2,1)} %bitcast.98) | data formatting | bytes 4194304 | tf_op jit(solution)/shard_map/while/body/jit(dynamic_update_index_in_dim)/dynamic_update_slice | solution.py:81
  159.5 1.5 constant_dynamic-update-slice_fusion.2
  162.7 1.7 constant_dynamic-slice_fusion.2
  164.5 2.5 %copy.71 = bf16[1,256,4096]{1,2,0:T(8,128)(2,1)} copy(bf16[1,256,4096]{2,1,0:T(8,128)(2,1)S(1)} %constant_dynamic-slice_fusion.2) | data formatting | bytes 4194304 | tf_op jit(solution)/shard_map/while/body/jit(dynamic_index_in_dim)/dynamic_slice | solution.py:81
  167.0 9.1 %fusion.59 = (f32[8,4,256]{2,1,0:T(4,128)S(1)}, f32[8,4,256,320]{2,3,1,0:T(8,128)}) fusion(pred[256,320]{0,1:T(8,128)(4,1)S(1)} %fusion.58, bf16[256,8,4,128]{0,3,2,1:T(8,128)(2,1)} %bitcast.97, bf16[320,8,128,1]{2,1,0,3:T(8,128)(2,1)S(1)} %bitcast.100), kind=kOutput, calls=%fused_computation.65.clone.1 | convolution fusion | flops 681574720 | bytes 13352960 | tf_op jit(solution)/shard_map/while/body/eval_jaxpr/sub | solution.py:28
  176.1 6.6 %fusion.60 = bf16[8,128,4,256]{3,1,2,0:T(8,128)(2,1)} fusion(f32[8,4,256,320]{2,3,1,0:T(8,128)} %get-tuple-element.149, f32[8,4,256]{2,1,0:T(4,128)S(1)} %get-tuple-element.150, bf16[320,8,128,1]{2,1,0,3:T(8,128)(2,1)S(1)} %bitcast.99), kind=kOutput, calls=%fused_computation.9.clone.1 | convolution fusion | flops 677380096 | bytes 13271040 | tf_op jit(solution)/shard_map/while/body/eval_jaxpr/fjip,pfa->ifja/dot_general | solution.py:29
  182.7 2.9 %copy.74 = bf16[1,256,4096]{2,1,0:T(8,128)(2,1)S(1)} copy(bf16[1,256,4096]{1,2,0:T(8,128)(2,1)} %bitcast.98) | data formatting | bytes 4194304 | tf_op jit(solution)/shard_map/while/body/jit(dynamic_update_index_in_dim)/dynamic_update_slice | solution.py:81
  185.6 1.5 constant_dynamic-update-slice_fusion.2
  188.9 1.7 constant_dynamic-slice_fusion.2
  190.6 2.5 %copy.71 = bf16[1,256,4096]{1,2,0:T(8,128)(2,1)} copy(bf16[1,256,4096]{2,1,0:T(8,128)(2,1)S(1)} %constant_dynamic-slice_fusion.2) | data formatting | bytes 4194304 | tf_op jit(solution)/shard_map/while/body/jit(dynamic_index_in_dim)/dynamic_slice | solution.py:81
  193.1 9.1 %fusion.59 = (f32[8,4,256]{2,1,0:T(4,128)S(1)}, f32[8,4,256,320]{2,3,1,0:T(8,128)}) fusion(pred[256,320]{0,1:T(8,128)(4,1)S(1)} %fusion.58, bf16[256,8,4,128]{0,3,2,1:T(8,128)(2,1)} %bitcast.97, bf16[320,8,128,1]{2,1,0,3:T(8,128)(2,1)S(1)} %bitcast.100), kind=kOutput, calls=%fused_computation.65.clone.1 | convolution fusion | flops 681574720 | bytes 13352960 | tf_op jit(solution)/shard_map/while/body/eval_jaxpr/sub | solution.py:28
  202.2 6.6 %fusion.60 = bf16[8,128,4,256]{3,1,2,0:T(8,128)(2,1)} fusion(f32[8,4,256,320]{2,3,1,0:T(8,128)} %get-tuple-element.149, f32[8,4,256]{2,1,0:T(4,128)S(1)} %get-tuple-element.150, bf16[320,8,128,1]{2,1,0,3:T(8,128)(2,1)S(1)} %bitcast.99), kind=kOutput, calls=%fused_computation.9.clone.1 | convolution fusion | flops 677380096 | bytes 13271040 | tf_op jit(solution)/shard_map/while/body/eval_jaxpr/fjip,pfa->ifja/dot_general | solution.py:29
  208.8 2.9 %copy.74 = bf16[1,256,4096]{2,1,0:T(8,128)(2,1)S(1)} copy(bf16[1,256,4096]{1,2,0:T(8,128)(2,1)} %bitcast.98) | data formatting | bytes 4194304 | tf_op jit(solution)/shard_map/while/body/jit(dynamic_update_index_in_dim)/dynamic_update_slice | solution.py:81
  (64 shorter events, 16.7 us)
Async XLA Ops:
  7.2 6.5 %copy-start = (f32[4096]{0:T(1024)S(1)}, f32[4096]{0:T(1024)}, u32[]{:S(2)}) copy-start(f32[4096]{0:T(1024)} %param.14) | copy-start | bytes 49156
  7.2 5.1 %copy-start.6 = (u32[32]{0:T(128)S(1)}, u32[32]{0:T(128)}, u32[]{:S(2)}) copy-start(u32[32]{0:T(128)} %constant.91) | copy-start | bytes 388
  7.2 43.1 %copy-start.5 = (s32[64]{0:T(128)S(1)}, s32[64]{0:T(128)}, u32[]{:S(2)}) copy-start(s32[64]{0:T(128)} %param.15) | copy-start | bytes 772
  7.2 6.3 %copy-start.4 = (bf16[4,4096]{1,0:T(4,128)(2,1)S(1)}, bf16[4,4096]{1,0:T(4,128)(2,1)}, u32[]{:S(2)}) copy-start(bf16[4,4096]{1,0:T(4,128)(2,1)} %param.13) | copy-start | bytes 98308
  7.2 83.6 %all-gather.3.cloned.1.call-start = ((), (), s32[]{:S(2)}) async-start(), calls=%async_computation | async-start | bytes 8912896 | tf_op jit(solution)/shard_map/all_gather | solution.py:70
  103.9 1.6 copy-start.2
  103.9 2.2 %copy-start.3 = (bf16[4,256,1024]{2,1,0:T(8,128)(2,1)S(1)}, bf16[4,256,1024]{2,1,0:T(8,128)(2,1)}, u32[]{:S(2)}) copy-start(bf16[4,256,1024]{2,1,0:T(8,128)(2,1)} %param.10) | copy-start | bytes 6291460
  213.1 0.7 copy-start.1
Sparse Core Ops, SparseCore 0:
  12.4 78.3 all-gather.2
where the time goes:
time: 222 us; the launch traced here: 221 us
  matrix products  70.2 us (32%)
  blocking collectives  67 us (30%)
  local copies, waits for them, and re-layouts  55.4 us (25%)
  between operations  14.8 us (7%)
  waiting for transfers between devices  7.12 us (3%)
  other arithmetic  5.94 us (3%)
    sub x4, matrix products, attend_child(): jax.nn.softmax(attention_scores, axis=-1).astype(jnp.bfloat16)  36.2 us
    unnamed x1, blocking collectives  35.8 us
    psum x1, blocking collectives, body(): total = lax.psum(jnp.sum(child_reward), 'beam')  31.2 us
    dot_general x4, matrix products, attend_child(): jnp.einsum('fjip,pfa->ifja', attention_weights, value_head_rows, preferre...  26.4 us
    dynamic_update_slice x8, local copies, waits for them, and re-layouts, body(): attended = lax.map(attend_child, (queries, keys_all, values_all))  17.5 us
    dynamic_slice x8, local copies, waits for them, and re-layouts, body(): attended = lax.map(attend_child, (queries, keys_all, values_all))  17 us
    unnamed x20, local copies, waits for them, and re-layouts  14.1 us
    all_gather x1, waiting for transfers between devices, body(): block = lax.all_gather(packed_kv, 'beam', axis=0, tiled=True)  7.11 us
  transfers between devices with their start and end apart: 1, of which 1 were waited for; matrix products, arithmetic and copies ran while one was open for 2% of the time, Pallas kernels for 0%

commit v1 on v0

v1 whole, which is shorter than its diff:
```python
import functools
import math

import jax
import jax.numpy as jnp
from jax import lax
from jax.experimental import pallas as pl
from jax.experimental.pallas import tpu as pltpu
from jax.sharding import PartitionSpec as P

HEAD = 128
KEEP = 2
MARK = 16
LOG2E = math.log2(math.e)
MIB = 1 << 20
NT = (((1,), (1,)), ((), ()))
NN = (((1,), (0,)), ((), ()))


def mm(a, b, dims=NN):
    return lax.dot_general(a, b, dims, preferred_element_type=jnp.float32)


def kept_pair(parents, base, local):
    own = (parents >= base) & (parents < base + local)
    first = jnp.min(jnp.where(own, parents - base, local))
    last = jnp.max(jnp.where(own, parents - base, -1))
    return first, last


def pack_keys(parents_ref, kv_ref, last_ref, value_ref, out_ref):
    local, _, step, width = kv_ref.shape
    heads = width // HEAD
    base = lax.axis_index("beam") * local
    kept = kept_pair(parents_ref[...], base, local)
    hidden = last_ref[...].astype(jnp.float32)
    square = jnp.mean(hidden * hidden, axis=-1, keepdims=True)
    normed = hidden * lax.rsqrt(square + 1e-05)
    score = jnp.sum(normed * value_ref[...], axis=-1, keepdims=True)
    reward = jax.nn.sigmoid(score)
    row = lax.broadcasted_iota(jnp.int32, reward.shape, 0)
    marks = [jnp.sum(jnp.where(row == k, reward, 0.0)) for k in kept]
    tile = lax.broadcasted_iota(jnp.int32, (MARK, HEAD), 0)
    tile = jnp.where(tile < MARK // 2, marks[0], marks[1]).astype(jnp.bfloat16)
    for d in range(out_ref.shape[0]):
        out_ref[d, KEEP * step :, :] = tile
    for r, k in enumerate(kept):
        for f in range(heads):
            piece = kv_ref[k, 0, :, f * HEAD : (f + 1) * HEAD]
            for d in range(f, out_ref.shape[0], heads):
                out_ref[d, r * step : (r + 1) * step, :] = piece


def pack_values(parents_ref, kv_ref, out_ref):
    local, _, step, width = kv_ref.shape
    heads = width // HEAD
    base = lax.axis_index("beam") * local
    kept = kept_pair(parents_ref[...], base, local)
    for r, k in enumerate(kept):
        for f in range(heads):
            piece = kv_ref[k, 0, :, f * HEAD : (f + 1) * HEAD]
            for d in range(f, out_ref.shape[0], heads):
                out_ref[d, r * step : (r + 1) * step, :] = piece


def pick_pieces(step, item_ref, table_ref, out_ref):
    heads = out_ref.shape[0]
    local = out_ref.shape[1] // step
    for d in range(heads):
        for i in range(local):
            item = item_ref[d * local + i]
            start = pl.multiple_of((item % KEEP) * step, step)
            piece = table_ref[item // KEEP, pl.ds(start, step), :]
            out_ref[d, i * step : (i + 1) * step, :] = piece


def attend_new(q_ref, k_ref, v_ref, out_ref, lse_ref):
    new = q_ref.shape[1]
    half = new // 2
    heads = k_ref.shape[2] // HEAD
    group = q_ref.shape[2] // k_ref.shape[2]
    scale = HEAD**-0.5 * LOG2E
    ones = jnp.ones((new, HEAD), jnp.bfloat16)
    low = lax.broadcasted_iota(jnp.int32, (half, HEAD), 1) < HEAD // 2
    row = lax.broadcasted_iota(jnp.int32, (half, half), 0)
    column = lax.broadcasted_iota(jnp.int32, (half, half), 1)
    bias = jnp.where(column <= row, 0.0, -jnp.inf)
    bias = jnp.concatenate([bias] * group, axis=0)
    for f in range(heads):
        keys = k_ref[0, :, f * HEAD : (f + 1) * HEAD]
        values = jnp.concatenate([v_ref[0, :, f * HEAD : (f + 1) * HEAD], ones], axis=1)
        for r in range(2):
            seen = (r + 1) * half
            rows = slice(r * half, (r + 1) * half)
            columns = [slice((f * group + h) * HEAD, (f * group + h + 1) * HEAD) for h in range(group)]
            query = jnp.concatenate([q_ref[0, rows, c] for c in columns], axis=0)
            logits = mm(query, keys[:seen], NT) * scale
            masked = logits[:, seen - half :] + bias
            if r == 0:
                logits = masked
                top = jnp.max(logits, axis=1, keepdims=True)
            else:
                free = logits[:, :half]
                top = jnp.max(jnp.maximum(free, masked), axis=1, keepdims=True)
                logits = jnp.concatenate([free, masked], axis=1)
            weights = jnp.exp2(logits - top).astype(jnp.bfloat16)
            both = mm(weights, values[:seen])
            total = both[:, HEAD:]
            part = both[:, :HEAD] / total
            lse = top + jnp.log2(total)
            for h in range(group):
                out_ref[0, rows, columns[h]] = part[h * half : (h + 1) * half].astype(jnp.bfloat16)
            for h in range(0, group, 2):
                pair = jnp.where(low, lse[h * half : (h + 1) * half], lse[(h + 1) * half : (h + 2) * half])
                start = (f * group + h) // 2 * HEAD
                lse_ref[0, rows, start : start + HEAD] = pair


def block_pair(a):
    zero = jnp.zeros_like(a)
    return jnp.concatenate([jnp.concatenate([a, zero], axis=1), jnp.concatenate([zero, a], axis=1)], axis=0)


def weigh_step(q_ref, k_ref, lse_ref, new_ref, weights_ref, out_ref):
    heads = k_ref.shape[0]
    step = k_ref.shape[1]
    pairs = lse_ref.shape[2] // HEAD
    new = q_ref.shape[1]
    scale = HEAD**-0.5 * LOG2E
    low = lax.broadcasted_iota(jnp.int32, (new, HEAD), 1) < step
    ones = block_pair(jnp.ones((step, HEAD), jnp.bfloat16))
    for f in range(heads):
        keys = block_pair(k_ref[f])
        for p in range(f * pairs // heads, (f + 1) * pairs // heads):
            wide = slice(p * 2 * HEAD, (p + 1) * 2 * HEAD)
            narrow = slice(p * HEAD, (p + 1) * HEAD)
            logits = mm(q_ref[0, :, wide], keys, NT) * scale - lse_ref[0, :, narrow]
            tops = [
                jnp.maximum(jnp.max(jnp.where(m, logits, 0.0), axis=1, keepdims=True), 0.0) for m in (low, ~low)
            ]
            weights = jnp.exp2(logits - jnp.where(low, tops[0], tops[1]))
            rest = [jnp.broadcast_to(jnp.exp2(-t), (new, HEAD)) for t in tops]
            total = mm(weights.astype(jnp.bfloat16), ones)
            shares = [1.0 / (rest[h] + total[:, h * HEAD : (h + 1) * HEAD]) for h in range(2)]
            weights_ref[0, :, narrow] = (weights * jnp.where(low, shares[0], shares[1])).astype(jnp.bfloat16)
            for h in range(2):
                c = slice((2 * p + h) * HEAD, (2 * p + h + 1) * HEAD)
                part = new_ref[0, :, c].astype(jnp.float32) * (shares[h] * rest[h])
                out_ref[0, :, c] = part.astype(jnp.bfloat16)


def add_step(v_ref, weights_ref, part_ref, out_ref):
    heads = v_ref.shape[0]
    pairs = weights_ref.shape[2] // HEAD
    for f in range(heads):
        values = block_pair(v_ref[f])
        for p in range(f * pairs // heads, (f + 1) * pairs // heads):
            wide = slice(p * 2 * HEAD, (p + 1) * 2 * HEAD)
            narrow = slice(p * HEAD, (p + 1) * HEAD)
            added = mm(weights_ref[0, :, narrow], values)
            out_ref[0, :, wide] = (part_ref[0, :, wide].astype(jnp.float32) + added).astype(jnp.bfloat16)


def params(mib):
    return pltpu.CompilerParams(vmem_limit_bytes=mib * MIB)


def body(queries, new_keys, new_values, step_kv, prm_last, value_head, parents):
    beam_count = lax.axis_size("beam")
    group_index = lax.axis_index("beam")
    local, new, width = queries.shape
    children = parents.shape[0]
    step = step_kv.shape[2]
    kv_width = step_kv.shape[3]
    heads = kv_width // HEAD
    groups = [list(range(g, g + heads)) for g in range(0, beam_count, heads)]
    vmem = pl.BlockSpec(memory_space=pltpu.VMEM)
    smem = pl.BlockSpec(memory_space=pltpu.SMEM)
    bf16 = jnp.bfloat16

    parent_row = parents.reshape(1, children)
    packed_keys = pl.pallas_call(
        pack_keys,
        grid=(1,),
        out_shape=jax.ShapeDtypeStruct((beam_count, KEEP * step + MARK, HEAD), bf16),
        in_specs=[
            pl.BlockSpec((1, children), lambda i: (0, 0)),
            pl.BlockSpec((local, 1, step, kv_width), lambda i: (0, 0, 0, 0)),
            pl.BlockSpec(prm_last.shape, lambda i: (0, 0)),
            pl.BlockSpec((1, value_head.shape[0]), lambda i: (0, 0)),
        ],
        out_specs=pl.BlockSpec((beam_count, KEEP * step + MARK, HEAD), lambda i: (0, 0, 0)),
        name="pack_keys",
    )(parent_row, step_kv, prm_last, value_head.reshape(1, -1))
    packed_values = pl.pallas_call(
        pack_values,
        grid=(1,),
        out_shape=jax.ShapeDtypeStruct((beam_count, KEEP * step, HEAD), bf16),
        in_specs=[
            pl.BlockSpec((1, children), lambda i: (0, 0)),
            pl.BlockSpec((local, 1, step, kv_width), lambda i: (0, 1, 0, 0)),
        ],
        out_specs=pl.BlockSpec((beam_count, KEEP * step, HEAD), lambda i: (0, 0, 0)),
        name="pack_values",
    )(parent_row, step_kv)

    owner = parents // local
    earlier = (owner[:, None] == owner[None, :]) & (parents[None, :] < parents[:, None])
    item = owner * KEEP + jnp.any(earlier, axis=1).astype(jnp.int32)
    near = lax.dynamic_slice_in_dim(item, group_index // heads * (heads * local), heads * local)

    def deliver(packed, name):
        table = lax.all_to_all(packed, "beam", 0, 0)
        picked = pl.pallas_call(
            functools.partial(pick_pieces, step),
            out_shape=jax.ShapeDtypeStruct((heads, local * step, HEAD), bf16),
            in_specs=[smem, vmem],
            out_specs=vmem,
            name=name,
        )(near, table)
        return table, lax.all_to_all(picked, "beam", 0, 0, axis_index_groups=groups)

    table, step_keys = deliver(packed_keys, "pick_keys")
    _, step_values = deliver(packed_values, "pick_values")

    marks = jnp.stack([table[:, KEEP * step, 0], table[:, KEEP * step + MARK // 2, 0]], axis=1).reshape(-1)
    match = item[:, None] == jnp.arange(beam_count * KEEP, dtype=jnp.int32)[None, :]
    picked = jnp.sum(jnp.where(match, marks.astype(jnp.float32)[None, :], 0.0), axis=1)
    mine = lax.dynamic_slice_in_dim(picked, group_index * local, local)
    child_share = children * mine / jnp.sum(picked)

    parts = 2
    cost = lambda f, t, b: pl.CostEstimate(flops=f, transcendentals=t, bytes_accessed=b)
    pair_width = width // 2
    part, lse = pl.pallas_call(
        attend_new,
        grid=(local, parts),
        out_shape=[
            jax.ShapeDtypeStruct((local, new, width), bf16),
            jax.ShapeDtypeStruct((local, new, pair_width), jnp.float32),
        ],
        in_specs=[
            pl.BlockSpec((1, new, width // parts), lambda i, j: (i, 0, j)),
            pl.BlockSpec((1, new, kv_width // parts), lambda i, j: (i, 0, j)),
            pl.BlockSpec((1, new, kv_width // parts), lambda i, j: (i, 0, j)),
        ],
        out_specs=[
            pl.BlockSpec((1, new, width // parts), lambda i, j: (i, 0, j)),
            pl.BlockSpec((1, new, pair_width // parts), lambda i, j: (i, 0, j)),
        ],
        compiler_params=params(24),
        cost_estimate=cost(4 * local * new * new * width, local * new * new * width // HEAD, 6 * local * new * width),
        name="attend_new",
    )(queries, new_keys, new_values)

    weights, part = pl.pallas_call(
        weigh_step,
        grid=(local, parts),
        out_shape=[
            jax.ShapeDtypeStruct((local, new, pair_width), bf16),
            jax.ShapeDtypeStruct((local, new, width), bf16),
        ],
        in_specs=[
            pl.BlockSpec((1, new, width // parts), lambda i, j: (i, 0, j)),
            pl.BlockSpec((heads // parts, step, HEAD), lambda i, j: (j, i, 0)),
            pl.BlockSpec((1, new, pair_width // parts), lambda i, j: (i, 0, j)),
            pl.BlockSpec((1, new, width // parts), lambda i, j: (i, 0, j)),
        ],
        out_specs=[
            pl.BlockSpec((1, new, pair_width // parts), lambda i, j: (i, 0, j)),
            pl.BlockSpec((1, new, width // parts), lambda i, j: (i, 0, j)),
        ],
        compiler_params=params(24),
        cost_estimate=cost(4 * local * new * step * width, local * new * step * width // HEAD, 6 * local * new * width),
        name="weigh_step",
    )(queries, step_keys, lse, part)

    attended = pl.pallas_call(
        add_step,
        grid=(local, parts),
        out_shape=jax.ShapeDtypeStruct((local, new, width), bf16),
        in_specs=[
            pl.BlockSpec((heads // parts, step, HEAD), lambda i, j: (j, i, 0)),
            pl.BlockSpec((1, new, pair_width // parts), lambda i, j: (i, 0, j)),
            pl.BlockSpec((1, new, width // parts), lambda i, j: (i, 0, j)),
        ],
        out_specs=pl.BlockSpec((1, new, width // parts), lambda i, j: (i, 0, j)),
        compiler_params=params(24),
        cost_estimate=cost(2 * local * new * step * width, 0, 5 * local * new * width),
        name="add_step",
    )(step_values, weights, part)
    return (attended, child_share)


def solution(mesh):
    in_specs = (
        P(("prompts", "beam"), None, None),
        P(("prompts", "beam"), None, None),
        P(("prompts", "beam"), None, None),
        P(("prompts", "beam"), None, None, None),
        P(("prompts", "beam"), None),
        P(),
        P("prompts"),
    )
    out_specs = (P(("prompts", "beam"), None, None), P(("prompts", "beam")))
    return jax.shard_map(body, mesh=mesh, in_specs=in_specs, out_specs=out_specs, check_vma=False)
```

time: 222 us -> 131 us (0.59)
  matrix products: 70.2 us -> 0 us
  blocking collectives: 67 us -> 0 us
  Pallas kernels: 0 us -> 45.8 us
  local copies, waits for them, and re-layouts: 55.4 us -> 31 us
  waiting for transfers between devices: 7.12 us -> 29.6 us
  starting transfers between devices: 0.04 us -> 18.8 us
  between operations: 14.8 us -> 0.77 us
    pallas_call x0 -> x7, Pallas kernels: none -> 45.8 us  [the longest x1 16.1 us: body(): pl.pallas_call(attend_new, grid=(local, parts), out_shape=[jax.ShapeDtype...]
    sub x4 -> x0, matrix products: 36.2 us -> none  [attend_child(): jax.nn.softmax(attention_scores, axis=-1).astype(jnp.bfloat16)]
    unnamed x1 -> x0, blocking collectives: 35.8 us -> none
    dot_general x9 -> x0, matrix products: 34 us -> none  [the longest x4 26.4 us: attend_child(): jnp.einsum('fjip,pfa->ifja', attention_weights, value_head_rows, preferre...]
    psum x1 -> x0, blocking collectives: 31.2 us -> none  [body(): total = lax.psum(jnp.sum(child_reward), 'beam')]
    all_to_all x0 -> x4, waiting for transfers between devices: none -> 29.6 us  [the longest x2 22.9 us: deliver(): table = lax.all_to_all(packed, 'beam', 0, 0)]
    all_to_all x0 -> x4, starting transfers between devices: none -> 18.8 us  [the longest x2 11.8 us: deliver(): table = lax.all_to_all(packed, 'beam', 0, 0)]
    dynamic_update_slice x8 -> x0, local copies, waits for them, and re-layouts: 17.5 us -> none  [body(): attended = lax.map(attend_child, (queries, keys_all, values_all))]
  transfers between devices with their start and end apart: 1 -> 4, of which waited for: 1 -> 3; matrix products, arithmetic and copies ran while one was open for 2% -> 5% of each run, Pallas kernels for 0% -> 28%
where the time goes in v1:
time: 131 us; the launch traced here: 130 us
  Pallas kernels  45.8 us (35%)
  local copies, waits for them, and re-layouts  31 us (24%)
  waiting for transfers between devices  29.6 us (23%)
  starting transfers between devices  18.8 us (14%)
  other arithmetic  4.2 us (3%)
    unnamed x26, local copies, waits for them, and re-layouts  29.3 us
    all_to_all x2, waiting for transfers between devices, deliver(): table = lax.all_to_all(packed, 'beam', 0, 0)  22.9 us
    pallas_call x1, Pallas kernels, body(): pl.pallas_call(attend_new, grid=(local, parts), out_shape=[jax.ShapeDtype...  16.1 us
    pallas_call x1, Pallas kernels, body(): pl.pallas_call(weigh_step, grid=(local, parts), out_shape=[jax.ShapeDtype...  14.4 us
    all_to_all x2, starting transfers between devices, deliver(): table = lax.all_to_all(packed, 'beam', 0, 0)  11.8 us
    all_to_all x2, starting transfers between devices, deliver(): lax.all_to_all(picked, 'beam', 0, 0, axis_index_groups=groups)  6.98 us
    all_to_all x2, waiting for transfers between devices, deliver(): lax.all_to_all(picked, 'beam', 0, 0, axis_index_groups=groups)  6.65 us
    pallas_call x1, Pallas kernels, body(): pl.pallas_call(add_step, grid=(local, parts), out_shape=jax.ShapeDtypeStr...  6.57 us
  transfers between devices with their start and end apart: 4, of which 3 were waited for; matrix products, arithmetic and copies ran while one was open for 5% of the time, Pallas kernels for 28%

profile of v1, /device:TPU:0, one launch (start us, length us, event | category | flops | bytes accessed | tf_op | source)
XLA Modules:
  0.0 130.1 jit_solution(9752454778491753668)
XLA Ops:
  0.6 2.4 %pack_keys.1 = bf16[16,144,128]{2,1,0:T(8,128)(2,1)} custom-call(s32[1,64]{1,0:T(1,128)} %bitcast.5, bf16[4,2,64,1024]{3,2,1,0:T(8,128)(2,1)} %kv_ref.3, bf16[4,4096]{1,0:T(4,128)(2,1)} %last_ref.1, f32[1,4096]{1,0:T(1,128)} %bitcast.4), custom_call_target="tpu_custom_call" | custom-call | tf_op jit(solution)/shard_map/pack_keys/pallas_call | solution.py:182
  3.1 7.4 %all-to-all-start.2 = ((bf16[16,144,128]{2,1,0:T(8,128)(2,1)}), bf16[16,144,128]{2,1,0:T(8,128)(2,1)S(1)}, u32[]{:S(2)}, u32[]{:S(2)}) async-start(bf16[16,144,128]{2,1,0:T(8,128)(2,1)} %pack_keys.1), calls=%async_computation.2 | async-start | bytes 1179648 | tf_op jit(solution)/shard_map/all_to_all | solution.py:213
  10.5 2.1 %pack_values.1 = bf16[16,128,128]{2,1,0:T(8,128)(2,1)} custom-call(s32[1,64]{1,0:T(1,128)} %bitcast.6, bf16[4,2,64,1024]{3,2,1,0:T(8,128)(2,1)} %kv_ref.3), custom_call_target="tpu_custom_call" | custom-call | tf_op jit(solution)/shard_map/pack_values/pallas_call | solution.py:195
  12.6 13.4 %all-to-all-done.2.table_ref = bf16[16,144,128]{2,1,0:T(8,128)(2,1)S(1)} async-done(((bf16[16,144,128]{2,1,0:T(8,128)(2,1)}), bf16[16,144,128]{2,1,0:T(8,128)(2,1)S(1)}, u32[]{:S(2)}, u32[]{:S(2)}) %all-to-all-start.2) | async-done | bytes 589856 | tf_op jit(solution)/shard_map/all_to_all | solution.py:213
  26.0 4.4 %all-to-all-start = ((bf16[16,128,128]{2,1,0:T(8,128)(2,1)}), bf16[16,128,128]{2,1,0:T(8,128)(2,1)S(1)}, u32[]{:S(2)}, u32[]{:S(2)}) async-start(bf16[16,128,128]{2,1,0:T(8,128)(2,1)} %pack_values.1), calls=%async_computation | async-start | bytes 1048576 | tf_op jit(solution)/shard_map/all_to_all | solution.py:213
  30.5 0.7 and_select_fusion
  31.1 0.9 and_reduce_fusion
  32.1 0.7 convert_add_fusion
  32.7 0.6 dynamic_slice.6.item_ref
  33.3 2.1 %pick_keys.1 = bf16[8,256,128]{2,1,0:T(8,128)(2,1)} custom-call(s32[32]{0:T(128)} %dynamic_slice.6.item_ref, bf16[16,144,128]{2,1,0:T(8,128)(2,1)} %copy-done.11), custom_call_target="tpu_custom_call" | custom-call | tf_op jit(solution)/shard_map/pick_keys/pallas_call | solution.py:214
  35.4 9.5 %all-to-all-done.table_ref = bf16[16,128,128]{2,1,0:T(8,128)(2,1)S(1)} async-done(((bf16[16,128,128]{2,1,0:T(8,128)(2,1)}), bf16[16,128,128]{2,1,0:T(8,128)(2,1)S(1)}, u32[]{:S(2)}, u32[]{:S(2)}) %all-to-all-start) | async-done | bytes 524320 | tf_op jit(solution)/shard_map/all_to_all | solution.py:213
  44.9 3.5 %all-to-all-start.3 = ((bf16[8,256,128]{2,1,0:T(8,128)(2,1)}), bf16[8,256,128]{2,1,0:T(8,128)(2,1)S(1)}, u32[]{:S(2)}, u32[]{:S(2)}) async-start(bf16[8,256,128]{2,1,0:T(8,128)(2,1)} %pick_keys.1), calls=%async_computation.3 | async-start | bytes 1048576 | tf_op jit(solution)/shard_map/all_to_all | solution.py:221
  48.4 2.1 %pick_values.1 = bf16[8,256,128]{2,1,0:T(8,128)(2,1)} custom-call(s32[32]{0:T(128)} %dynamic_slice.6.item_ref, bf16[16,128,128]{2,1,0:T(8,128)(2,1)} %copy-done.12), custom_call_target="tpu_custom_call" | custom-call | tf_op jit(solution)/shard_map/pick_values/pallas_call | solution.py:214
  50.5 6.6 %all-to-all-done.3.k_ref = bf16[8,256,128]{2,1,0:T(8,128)(2,1)S(1)} async-done(((bf16[8,256,128]{2,1,0:T(8,128)(2,1)}), bf16[8,256,128]{2,1,0:T(8,128)(2,1)S(1)}, u32[]{:S(2)}, u32[]{:S(2)}) %all-to-all-start.3) | async-done | bytes 524320 | tf_op jit(solution)/shard_map/all_to_all | solution.py:221
  57.2 3.5 %all-to-all-start.1 = ((bf16[8,256,128]{2,1,0:T(8,128)(2,1)}), bf16[8,256,128]{2,1,0:T(8,128)(2,1)S(1)}, u32[]{:S(2)}, u32[]{:S(2)}) async-start(bf16[8,256,128]{2,1,0:T(8,128)(2,1)} %pick_values.1), calls=%async_computation.1 | async-start | bytes 1048576 | tf_op jit(solution)/shard_map/all_to_all | solution.py:221
  60.7 3.4 %copy-done = bf16[4,256,4096]{2,1,0:T(8,128)(2,1)S(1)} copy-done((bf16[4,256,4096]{2,1,0:T(8,128)(2,1)S(1)}, bf16[4,256,4096]{2,1,0:T(8,128)(2,1)}, u32[]{:S(2)}) %copy-start) | copy-done | bytes 8388632
  64.1 1.6 %copy-done.10 = bf16[4,256,1024]{2,1,0:T(8,128)(2,1)S(1)} copy-done((bf16[4,256,1024]{2,1,0:T(8,128)(2,1)S(1)}, bf16[4,256,1024]{2,1,0:T(8,128)(2,1)}, u32[]{:S(2)}) %copy-start.10) | copy-done | bytes 2097176
  65.7 16.1 %attend_new.1 = (bf16[4,256,4096]{2,1,0:T(8,128)(2,1)S(1)}, f32[4,256,2048]{2,1,0:T(8,128)S(1)}) custom-call(bf16[4,256,4096]{2,1,0:T(8,128)(2,1)S(1)} %copy-done, bf16[4,256,1024]{2,1,0:T(8,128)(2,1)S(1)} %copy-done.9, bf16[4,256,1024]{2,1,0:T(8,128)(2,1)S(1)} %copy-done.10), custom_call_target="tpu_custom_call" | custom-call | flops 4294967296 | bytes 25165824 | tf_op jit(solution)/shard_map/attend_new/pallas_call | solution.py:235
  81.8 3.2 %copy-done.2 = bf16[4,256,4096]{2,1,0:T(8,128)(2,1)} copy-done((bf16[4,256,4096]{2,1,0:T(8,128)(2,1)}, bf16[4,256,4096]{2,1,0:T(8,128)(2,1)S(1)}, u32[]{:S(2)}) %copy-start.2) | copy-done | bytes 8388632
  85.0 3.4 %copy-done.3 = f32[4,256,2048]{2,1,0:T(8,128)} copy-done((f32[4,256,2048]{2,1,0:T(8,128)}, f32[4,256,2048]{2,1,0:T(8,128)S(1)}, u32[]{:S(2)}) %copy-start.3) | copy-done | bytes 8388632
  88.4 1.0 slice_reduce_fusion.1
  89.5 0.1 reshape.22
  89.6 0.7 select_reduce_fusion
  90.3 1.2 multiply_divide_fusion
  91.5 3.4 %copy-done.1 = bf16[4,256,4096]{2,1,0:T(8,128)(2,1)S(1)} copy-done((bf16[4,256,4096]{2,1,0:T(8,128)(2,1)S(1)}, bf16[4,256,4096]{2,1,0:T(8,128)(2,1)}, u32[]{:S(2)}) %copy-start.1) | copy-done | bytes 8388632
  94.9 3.4 %copy-done.4 = f32[4,256,2048]{2,1,0:T(8,128)S(1)} copy-done((f32[4,256,2048]{2,1,0:T(8,128)S(1)}, f32[4,256,2048]{2,1,0:T(8,128)}, u32[]{:S(2)}) %copy-start.4) | copy-done | bytes 8388632
  98.3 14.4 %weigh_step.1 = (bf16[4,256,2048]{2,1,0:T(8,128)(2,1)S(1)}, bf16[4,256,4096]{2,1,0:T(8,128)(2,1)S(1)}) custom-call(bf16[4,256,4096]{2,1,0:T(8,128)(2,1)S(1)} %copy-done.1, bf16[8,256,128]{2,1,0:T(8,128)(2,1)S(1)} %all-to-all-done.3.k_ref, f32[4,256,2048]{2,1,0:T(8,128)S(1)} %copy-done.4, bf16[4,256,4096]{2,1,0:T(8,128)(2,1)} %copy-done.2), custom_call_target="tpu_custom_call" | custom-call | flops 1073741824 | bytes 25165824 | tf_op jit(solution)/shard_map/weigh_step/pallas_call | solution.py:256
  112.7 3.4 %copy-done.5 = bf16[4,256,4096]{2,1,0:T(8,128)(2,1)} copy-done((bf16[4,256,4096]{2,1,0:T(8,128)(2,1)}, bf16[4,256,4096]{2,1,0:T(8,128)(2,1)S(1)}, u32[]{:S(2)}) %copy-start.5) | copy-done | bytes 8388632
  116.1 1.9 %copy-done.7 = bf16[4,256,2048]{2,1,0:T(8,128)(2,1)} copy-done((bf16[4,256,2048]{2,1,0:T(8,128)(2,1)}, bf16[4,256,2048]{2,1,0:T(8,128)(2,1)S(1)}, u32[]{:S(2)}) %copy-start.7) | copy-done | bytes 4194328
  118.0 3.4 %copy-done.6 = bf16[4,256,4096]{2,1,0:T(8,128)(2,1)S(1)} copy-done((bf16[4,256,4096]{2,1,0:T(8,128)(2,1)S(1)}, bf16[4,256,4096]{2,1,0:T(8,128)(2,1)}, u32[]{:S(2)}) %copy-start.6) | copy-done | bytes 8388632
  121.4 2.2 %copy-done.8 = bf16[4,256,2048]{2,1,0:T(8,128)(2,1)S(1)} copy-done((bf16[4,256,2048]{2,1,0:T(8,128)(2,1)S(1)}, bf16[4,256,2048]{2,1,0:T(8,128)(2,1)}, u32[]{:S(2)}) %copy-start.8) | copy-done | bytes 4194328
  123.6 6.6 %add_step.1 = bf16[4,256,4096]{2,1,0:T(8,128)(2,1)} custom-call(bf16[8,256,128]{2,1,0:T(8,128)(2,1)S(1)} %all-to-all-done.1.v_ref, bf16[4,256,2048]{2,1,0:T(8,128)(2,1)S(1)} %copy-done.8, bf16[4,256,4096]{2,1,0:T(8,128)(2,1)S(1)} %copy-done.6), custom_call_target="tpu_custom_call" | custom-call | flops 536870912 | bytes 20971520 | tf_op jit(solution)/shard_map/add_step/pallas_call | solution.py:278
  (19 shorter events, 0.1 us)
Async XLA Ops:
  0.6 60.1 %copy-start.9 = (bf16[4,256,1024]{2,1,0:T(8,128)(2,1)S(1)}, bf16[4,256,1024]{2,1,0:T(8,128)(2,1)}, u32[]{:S(2)}) copy-start(bf16[4,256,1024]{2,1,0:T(8,128)(2,1)} %k_ref.1) | copy-start | bytes 6291460
  3.1 22.9 %all-to-all-start.2 = ((bf16[16,144,128]{2,1,0:T(8,128)(2,1)}), bf16[16,144,128]{2,1,0:T(8,128)(2,1)S(1)}, u32[]{:S(2)}, u32[]{:S(2)}) async-start(bf16[16,144,128]{2,1,0:T(8,128)(2,1)} %pack_keys.1), calls=%async_computation.2 | async-start | bytes 1179648 | tf_op jit(solution)/shard_map/all_to_all | solution.py:213
  26.0 7.3 %copy-start.11 = (bf16[16,144,128]{2,1,0:T(8,128)(2,1)}, bf16[16,144,128]{2,1,0:T(8,128)(2,1)S(1)}, u32[]{:S(2)}) copy-start(bf16[16,144,128]{2,1,0:T(8,128)(2,1)S(1)} %all-to-all-done.2.table_ref) | copy-start | bytes 1769476
  26.0 18.9 %all-to-all-start = ((bf16[16,128,128]{2,1,0:T(8,128)(2,1)}), bf16[16,128,128]{2,1,0:T(8,128)(2,1)S(1)}, u32[]{:S(2)}, u32[]{:S(2)}) async-start(bf16[16,128,128]{2,1,0:T(8,128)(2,1)} %pack_values.1), calls=%async_computation | async-start | bytes 1048576 | tf_op jit(solution)/shard_map/all_to_all | solution.py:213
  44.9 3.5 %copy-start.12 = (bf16[16,128,128]{2,1,0:T(8,128)(2,1)}, bf16[16,128,128]{2,1,0:T(8,128)(2,1)S(1)}, u32[]{:S(2)}) copy-start(bf16[16,128,128]{2,1,0:T(8,128)(2,1)S(1)} %all-to-all-done.table_ref) | copy-start | bytes 1572868
  44.9 12.3 %all-to-all-start.3 = ((bf16[8,256,128]{2,1,0:T(8,128)(2,1)}), bf16[8,256,128]{2,1,0:T(8,128)(2,1)S(1)}, u32[]{:S(2)}, u32[]{:S(2)}) async-start(bf16[8,256,128]{2,1,0:T(8,128)(2,1)} %pick_keys.1), calls=%async_computation.3 | async-start | bytes 1048576 | tf_op jit(solution)/shard_map/all_to_all | solution.py:221
  57.2 60.8 %all-to-all-start.1 = ((bf16[8,256,128]{2,1,0:T(8,128)(2,1)}), bf16[8,256,128]{2,1,0:T(8,128)(2,1)S(1)}, u32[]{:S(2)}, u32[]{:S(2)}) async-start(bf16[8,256,128]{2,1,0:T(8,128)(2,1)} %pick_values.1), calls=%async_computation.1 | async-start | bytes 1048576 | tf_op jit(solution)/shard_map/all_to_all | solution.py:221
  60.7 3.4 %copy-start = (bf16[4,256,4096]{2,1,0:T(8,128)(2,1)S(1)}, bf16[4,256,4096]{2,1,0:T(8,128)(2,1)}, u32[]{:S(2)}) copy-start(bf16[4,256,4096]{2,1,0:T(8,128)(2,1)} %q_ref.3) | copy-start | bytes 25165828
  64.1 1.6 %copy-start.10 = (bf16[4,256,1024]{2,1,0:T(8,128)(2,1)S(1)}, bf16[4,256,1024]{2,1,0:T(8,128)(2,1)}, u32[]{:S(2)}) copy-start(bf16[4,256,1024]{2,1,0:T(8,128)(2,1)} %v_ref.1) | copy-start | bytes 6291460
  81.8 3.2 %copy-start.2 = (bf16[4,256,4096]{2,1,0:T(8,128)(2,1)}, bf16[4,256,4096]{2,1,0:T(8,128)(2,1)S(1)}, u32[]{:S(2)}) copy-start(bf16[4,256,4096]{2,1,0:T(8,128)(2,1)S(1)} %get-tuple-element.7.new_ref) | copy-start | bytes 25165828
  85.0 3.4 %copy-start.3 = (f32[4,256,2048]{2,1,0:T(8,128)}, f32[4,256,2048]{2,1,0:T(8,128)S(1)}, u32[]{:S(2)}) copy-start(f32[4,256,2048]{2,1,0:T(8,128)S(1)} %get-tuple-element.6.lse_ref) | copy-start | bytes 25165828
  91.5 3.4 %copy-start.1 = (bf16[4,256,4096]{2,1,0:T(8,128)(2,1)S(1)}, bf16[4,256,4096]{2,1,0:T(8,128)(2,1)}, u32[]{:S(2)}) copy-start(bf16[4,256,4096]{2,1,0:T(8,128)(2,1)} %q_ref.3) | copy-start | bytes 25165828
  94.9 3.4 %copy-start.4 = (f32[4,256,2048]{2,1,0:T(8,128)S(1)}, f32[4,256,2048]{2,1,0:T(8,128)}, u32[]{:S(2)}) copy-start(f32[4,256,2048]{2,1,0:T(8,128)} %copy-done.3) | copy-start | bytes 25165828
  112.7 3.4 %copy-start.5 = (bf16[4,256,4096]{2,1,0:T(8,128)(2,1)}, bf16[4,256,4096]{2,1,0:T(8,128)(2,1)S(1)}, u32[]{:S(2)}) copy-start(bf16[4,256,4096]{2,1,0:T(8,128)(2,1)S(1)} %get-tuple-element.9.part_ref) | copy-start | bytes 25165828
  116.1 1.9 %copy-start.7 = (bf16[4,256,2048]{2,1,0:T(8,128)(2,1)}, bf16[4,256,2048]{2,1,0:T(8,128)(2,1)S(1)}, u32[]{:S(2)}) copy-start(bf16[4,256,2048]{2,1,0:T(8,128)(2,1)S(1)} %get-tuple-element.8.weights_ref) | copy-start | bytes 12582916
  118.0 3.4 %copy-start.6 = (bf16[4,256,4096]{2,1,0:T(8,128)(2,1)S(1)}, bf16[4,256,4096]{2,1,0:T(8,128)(2,1)}, u32[]{:S(2)}) copy-start(bf16[4,256,4096]{2,1,0:T(8,128)(2,1)} %copy-done.5) | copy-start | bytes 25165828
  121.4 2.2 %copy-start.8 = (bf16[4,256,2048]{2,1,0:T(8,128)(2,1)S(1)}, bf16[4,256,2048]{2,1,0:T(8,128)(2,1)}, u32[]{:S(2)}) copy-start(bf16[4,256,2048]{2,1,0:T(8,128)(2,1)} %copy-done.7) | copy-start | bytes 12582916

commit v2 on v0

v2 whole, which is shorter than its diff:
```python
import functools
import math

import jax
import jax.numpy as jnp
from jax import lax
from jax.experimental import pallas as pl
from jax.experimental.pallas import tpu as pltpu
from jax.sharding import PartitionSpec as P

HEAD = 128
KEEP = 2
MARK = 16
WAIT = (0, 1, 2, 2)
LOG2E = math.log2(math.e)
MIB = 1 << 20
NT = (((1,), (1,)), ((), ()))
NN = (((1,), (0,)), ((), ()))


def mm(a, b, dims=NN):
    return lax.dot_general(a, b, dims, preferred_element_type=jnp.float32)


def kept_pair(parents, base, local):
    own = (parents >= base) & (parents < base + local)
    first = jnp.min(jnp.where(own, parents - base, local))
    last = jnp.max(jnp.where(own, parents - base, -1))
    return first, last


def pack(parents_ref, kv_ref, last_ref, value_ref, out_ref, held_ref, sems):
    local, _, step, width = kv_ref.shape
    heads = width // HEAD
    base = lax.axis_index("beam") * local
    kept = kept_pair(parents_ref[...], base, local)
    copies = [pltpu.make_async_copy(kv_ref.at[k], held_ref.at[r], sems.at[r]) for r, k in enumerate(kept)]
    for copy in copies:
        copy.start()
    hidden = last_ref[...].astype(jnp.float32)
    square = jnp.mean(hidden * hidden, axis=-1, keepdims=True)
    normed = hidden * lax.rsqrt(square + 1e-05)
    score = jnp.sum(normed * value_ref[...], axis=-1, keepdims=True)
    reward = jax.nn.sigmoid(score)
    row = lax.broadcasted_iota(jnp.int32, reward.shape, 0)
    marks = [jnp.sum(jnp.where(row == k, reward, 0.0)) for k in kept]
    tile = lax.broadcasted_iota(jnp.int32, (MARK, HEAD), 0)
    tile = jnp.where(tile < MARK // 2, marks[0], marks[1]).astype(jnp.bfloat16)
    for d in range(out_ref.shape[0]):
        out_ref[d, KEEP * 2 * step :, :] = tile
    for r, copy in enumerate(copies):
        copy.wait()
        for s in range(2):
            for f in range(heads):
                piece = held_ref[r, s, :, f * HEAD : (f + 1) * HEAD]
                start = (r * 2 + s) * step
                for d in range(f, out_ref.shape[0], heads):
                    out_ref[d, start : start + step, :] = piece


def pick(item_ref, table_ref, _, *out_refs):
    rows = (table_ref.shape[1] - MARK) // KEEP
    chips = len(out_refs)
    local = out_refs[0].shape[0] // (2 * rows)
    chip = lax.axis_index("beam") % (2 * chips) // 2
    core = lax.axis_index("beam") % 2
    for m in range(chips):
        for other in range(2):
            owner = (chip ^ m) * 2 + (core ^ other)
            for i in range(local):
                item = item_ref[owner * local + i]
                start = pl.multiple_of((item % KEEP) * rows, rows)
                to = (other * local + i) * rows
                out_refs[m][to : to + rows, :] = table_ref[item // KEEP, pl.ds(start, rows), :]


def share_rewards(item_ref, table_ref, _, out_ref):
    children, local = item_ref.shape[0], out_ref.shape[1]
    rows = table_ref.shape[1] - MARK
    mine = lax.axis_index("beam") * local
    upper = lax.broadcasted_iota(jnp.int32, (MARK, HEAD), 0) < MARK // 2
    lane = lax.broadcasted_iota(jnp.int32, (1, HEAD), 1)

    def reward(child):
        item = item_ref[child]
        tile = table_ref[item // KEEP, rows:, :].astype(jnp.float32)
        tile = jnp.where(upper == (item % KEEP == 0), tile, 0.0)
        return tile[:1, :] + tile[MARK // 2 : MARK // 2 + 1, :]

    total = jnp.zeros((1, HEAD), jnp.float32)
    for child in range(children):
        total = total + reward(child)
    picked = jnp.zeros((1, HEAD), jnp.float32)
    for i in range(local):
        picked = jnp.where(lane == i, reward(mine + i), picked)
    out_ref[...] = (children * picked / total)[:, :local]


def attend_new(q_ref, k_ref, v_ref, out_ref, stat_ref):
    new = q_ref.shape[1]
    half = new // 2
    heads = k_ref.shape[2] // HEAD
    group = q_ref.shape[2] // k_ref.shape[2]
    count = heads * group
    scale = HEAD**-0.5 * LOG2E
    ones = jnp.ones((new, HEAD), jnp.bfloat16)
    lane = lax.broadcasted_iota(jnp.int32, (half, HEAD), 1)
    row = lax.broadcasted_iota(jnp.int32, (half, half), 0)
    column = lax.broadcasted_iota(jnp.int32, (half, half), 1)
    bias = jnp.concatenate([jnp.where(column <= row, 0.0, -jnp.inf)] * group, axis=0)
    tops = [jnp.zeros((half, HEAD), jnp.float32) for _ in range(2)]
    sums = [jnp.ones((half, HEAD), jnp.float32) for _ in range(2)]
    for f in range(heads):
        keys = k_ref[0, :, f * HEAD : (f + 1) * HEAD]
        values = jnp.concatenate([v_ref[0, :, f * HEAD : (f + 1) * HEAD], ones], axis=1)
        columns = [slice((f * group + h) * HEAD, (f * group + h + 1) * HEAD) for h in range(group)]
        for r in range(2):
            seen = (r + 1) * half
            rows = slice(r * half, (r + 1) * half)
            query = jnp.concatenate([q_ref[0, rows, c] for c in columns], axis=0)
            logits = mm(query, keys[:seen], NT) * scale
            masked = logits[:, seen - half :] + bias
            if r == 0:
                logits = masked
                top = jnp.max(masked, axis=1, keepdims=True)
            else:
                free = logits[:, :half]
                logits = jnp.concatenate([free, masked], axis=1)
                top = jnp.max(jnp.maximum(free, masked), axis=1, keepdims=True)
            weights = jnp.exp2(logits - top).astype(jnp.bfloat16)
            both = mm(weights, values[:seen])
            total = both[:, HEAD:]
            part = both[:, :HEAD] * pltpu.reciprocal(total, approx=True)
            for h in range(group):
                s = slice(h * half, (h + 1) * half)
                out_ref[0, rows, columns[h]] = part[s].astype(jnp.bfloat16)
                here = lane == f * group + h
                tops[r] = jnp.where(here, top[s], tops[r])
                sums[r] = jnp.where(here, total[s], sums[r])
    for r in range(2):
        lse = (tops[r] + jnp.log2(sums[r])) * (-1.0 / scale)
        high = lse.astype(jnp.bfloat16).astype(jnp.float32)
        rest = pltpu.roll(lse - high, count, 1)
        both = jnp.where(lane < count, high, jnp.where(lane < 2 * count, rest, 0.0))
        stat_ref[0, r * half : (r + 1) * half, :] = both.astype(jnp.bfloat16)


def block_pair(a):
    zero = jnp.zeros_like(a)
    return jnp.concatenate([jnp.concatenate([a, zero], axis=1), jnp.concatenate([zero, a], axis=1)], axis=0)


def forward(sent_ref, _, out_ref):
    out_ref[...] = sent_ref[sent_ref.shape[0] - out_ref.shape[0] :, :]


def attend_block(q_ref, part_ref, stat_ref, own_ref, other_ref, out_ref, place, i, f, shifted):
    new, width = q_ref.shape[1:]
    rows = own_ref.shape[0] // (2 * q_ref.shape[0])
    step = rows // 2
    pairs = width // (2 * HEAD)
    core = lax.axis_index("beam") % 2
    scale = HEAD**-0.5 * LOG2E
    ones = block_pair(jnp.ones((step, HEAD), jnp.bfloat16))
    lane = lax.broadcasted_iota(jnp.int32, (new, HEAD), 1)
    pair_of_lane = lane % (HEAD // 4) // 2 - place * pairs
    odd_lane = lax.broadcasted_iota(jnp.int32, (rows, HEAD), 1) % 2
    spread = (odd_lane == lax.broadcasted_iota(jnp.int32, (rows, HEAD), 0) // step).astype(jnp.bfloat16)
    low = lax.broadcasted_iota(jnp.int32, (new * pairs // 2, HEAD), 1) < step

    here = pl.ds(pl.multiple_of(i * rows, rows), rows)
    piece = jnp.where(f == core, own_ref[here, :], other_ref[here, :])
    stat = stat_ref[i]
    keys = jnp.concatenate([block_pair(piece[:step]), spread], axis=1)
    values = jnp.concatenate([block_pair(piece[step:]), ones], axis=1)
    group = [f * (pairs // 2) + p for p in range(pairs // 2)]
    columns = [pl.ds(pl.multiple_of(p * 2 * HEAD, 2 * HEAD), 2 * HEAD) for p in group]
    shifts = [jnp.where(pair_of_lane == p, stat, jnp.zeros_like(stat)) for p in group]
    left = [jnp.concatenate([q_ref[i, :, c], t], axis=1) for c, t in zip(columns, shifts)]
    logits = mm(jnp.concatenate(left, axis=0), keys, NT) * scale
    part = jnp.concatenate([part_ref[i, :, c] for c in columns], axis=0).astype(jnp.float32)
    rest = 1.0
    most = None
    if shifted:
        tops = [jnp.maximum(jnp.max(jnp.where(k, logits, 0.0), axis=1, keepdims=True), 0.0) for k in (low, ~low)]
        logits = logits - jnp.where(low, tops[0], tops[1])
        rest = jnp.concatenate([jnp.broadcast_to(jnp.exp2(-t), low.shape) for t in tops], axis=1)
        part = part * rest
    else:
        most = jnp.max(logits.reshape(-1, 8, HEAD), axis=0)
    both = mm(jnp.exp2(logits).astype(jnp.bfloat16), values)
    share = pltpu.reciprocal(rest + both[:, 2 * HEAD :], approx=True)
    result = ((part + both[:, : 2 * HEAD]) * share).astype(jnp.bfloat16)
    for n, c in enumerate(columns):
        out_ref[i, :, c] = result[n * new : (n + 1) * new]
    return most


def attend_blocks(q_ref, part_ref, stat_ref, own_ref, other_ref, held_ref, out_ref, sems, place, ready):
    local, _, width = q_ref.shape
    lanes = pl.ds(pl.multiple_of(place * width, width), width)
    refs = (q_ref, part_ref, stat_ref, own_ref, other_ref, held_ref, place)

    def send(i):
        return pltpu.make_async_copy(held_ref.at[i], out_ref.at[i, :, lanes], sems.at[i])

    def work(i, most):
        ready(i)
        most = jnp.maximum(most, jnp.maximum(attend_block(*refs, i, 0, False), attend_block(*refs, i, 1, False)))
        send(i).start()
        return most

    most = lax.fori_loop(0, local, work, jnp.full((8, HEAD), -jnp.inf, jnp.float32))
    for i in range(local):
        send(i).wait()

    @pl.when(jnp.max(most) > 100.0)
    def _():
        lax.fori_loop(0, 2 * local, lambda t, c: (attend_block(*refs, t // 2, t % 2, True), c)[1], 0)
        for i in range(local):
            send(i).start()
        for i in range(local):
            send(i).wait()


def attend_first(q_ref, part_ref, stat_ref, own_ref, other_ref, *refs):
    out_ref, later_q, later_part, later_stat, token_ref, held_q, held_part, held, sems, stat_sem, out_sems = refs
    stat_copy = pltpu.make_async_copy(stat_ref, later_stat, stat_sem)
    stat_copy.start()
    token_ref[...] = jnp.zeros_like(token_ref)
    local, _, width = held.shape
    chips = later_q.shape[0] + 1
    chip = lax.axis_index("beam") % (2 * chips) // 2

    def copy(k, m, i, to):
        lanes = pl.ds(pl.multiple_of((chip ^ m) * width, width), width)
        return pltpu.make_async_copy((q_ref, part_ref)[k].at[i, :, lanes], to.at[i], sems.at[k, m, i])

    targets = [(held_q, held_part)] + [(later_q.at[m], later_part.at[m]) for m in range(chips - 1)]
    for m in range(chips):
        for i in range(local):
            for k in range(2):
                copy(k, m, i, targets[m][k]).start()

    def ready(i):
        for k in range(2):
            copy(k, 0, i, targets[0][k]).wait()

    stat_copy.wait()
    attend_blocks(held_q, held_part, later_stat, own_ref, other_ref, held, out_ref, out_sems, chip, ready)
    for m in range(1, chips):
        for i in range(local):
            for k in range(2):
                copy(k, m, i, targets[m][k]).wait()


def attend_later(m, q_ref, part_ref, stat_ref, own_ref, other_ref, _, out_ref, token_ref, held, sems):
    chips = q_ref.shape[0] + 1
    place = lax.axis_index("beam") % (2 * chips) // 2 ^ m
    token_ref[...] = jnp.zeros_like(token_ref)
    views = (q_ref.at[m - 1], part_ref.at[m - 1])
    attend_blocks(*views, stat_ref, own_ref, other_ref, held, out_ref, sems, place, lambda i: None)


def params(mib):
    return pltpu.CompilerParams(vmem_limit_bytes=mib * MIB)


def swap(a, distance):
    count = lax.axis_size("beam")
    return lax.ppermute(a, "beam", [(i, i ^ distance) for i in range(count)])


def body(queries, new_keys, new_values, step_kv, prm_last, value_head, parents):
    beam_count = lax.axis_size("beam")
    group_index = lax.axis_index("beam")
    local, new, width = queries.shape
    children = parents.shape[0]
    step = step_kv.shape[2]
    kv_width = step_kv.shape[3]
    heads = kv_width // HEAD
    chips = heads // 2
    vmem = pl.BlockSpec(memory_space=pltpu.VMEM)
    smem = pl.BlockSpec(memory_space=pltpu.SMEM)
    bf16 = jnp.bfloat16

    rows = 2 * step
    in_hbm = lambda a: pltpu.with_memory_space_constraint(a, pltpu.HBM)
    in_vmem = lambda a: pltpu.with_memory_space_constraint(a, pltpu.VMEM)
    packed = pl.pallas_call(
        pack,
        out_shape=jax.ShapeDtypeStruct((beam_count, KEEP * rows + MARK, HEAD), bf16),
        in_specs=[vmem, pl.BlockSpec(memory_space=pl.ANY), vmem, vmem],
        out_specs=vmem,
        scratch_shapes=[pltpu.VMEM((KEEP, 2, step, kv_width), bf16), pltpu.SemaphoreType.DMA((KEEP,))],
        name="pack",
    )(parents.reshape(1, children), step_kv, prm_last, value_head.reshape(1, -1))
    table = lax.all_to_all(packed, "beam", 0, 0)

    cost = lambda f, t, b: pl.CostEstimate(flops=f, transcendentals=t, bytes_accessed=b)
    whole = lambda w: pl.BlockSpec((1, new, w), lambda i: (i, 0, 0))
    part, stat = pl.pallas_call(
        attend_new,
        grid=(local,),
        out_shape=[
            jax.ShapeDtypeStruct((local, new, width), bf16),
            jax.ShapeDtypeStruct((local, new, HEAD), bf16),
        ],
        in_specs=[whole(width), whole(kv_width), whole(kv_width)],
        out_specs=[whole(width), whole(HEAD)],
        compiler_params=params(56),
        cost_estimate=cost(4 * local * new * new * width, local * new * new * width // HEAD, 6 * local * new * width),
        name="attend_new",
    )(queries, new_keys, new_values)

    owner = parents // local
    earlier = (owner[:, None] == owner[None, :]) & (parents[None, :] < parents[:, None])
    item = owner * KEEP + jnp.any(earlier, axis=1).astype(jnp.int32)
    near = lax.dynamic_slice_in_dim(item, group_index // heads * (heads * local), heads * local)
    pieces = pl.pallas_call(
        pick,
        out_shape=[jax.ShapeDtypeStruct((2 * local * rows, HEAD), bf16)] * chips,
        in_specs=[smem, vmem, pl.BlockSpec(memory_space=pl.ANY)],
        out_specs=[vmem] * chips,
        compiler_params=params(4),
        name="pick",
    )(near, table, in_hbm(stat))

    anywhere = pl.BlockSpec(memory_space=pl.ANY)
    hbm = pl.BlockSpec(memory_space=pltpu.HBM)
    wide = width // chips
    own = [pieces[0]] + [swap(pieces[m], 2 * m) for m in range(1, chips)]
    done = [near]
    step_cost = cost(local * new * step * width, local * new * step * width // HEAD, 3 * local * new * width)
    result = jax.ShapeDtypeStruct((local, new, width), bf16)
    later = pltpu.VMEM((chips - 1, local, new, wide), bf16)
    held = pltpu.VMEM((local, new, wide), bf16)
    for m in range(chips):
        passed = pl.pallas_call(
            forward,
            out_shape=jax.ShapeDtypeStruct((local * rows, HEAD), bf16),
            in_specs=[vmem, anywhere],
            out_specs=vmem,
            compiler_params=params(2),
            name="forward",
        )(own[m], done[WAIT[m]])
        other = swap(passed, 1)
        if m == 0:
            attended, later_q, later_part, later_stat, token = pl.pallas_call(
                attend_first,
                out_shape=[result, later, later, pltpu.VMEM(stat.shape, bf16), jax.ShapeDtypeStruct((8, HEAD), jnp.float32)],
                in_specs=[hbm, hbm, hbm, vmem, vmem],
                out_specs=[hbm] + [vmem] * 4,
                scratch_shapes=[held] * 3
                + [pltpu.SemaphoreType.DMA((2, chips, local)), pltpu.SemaphoreType.DMA, pltpu.SemaphoreType.DMA((local,))],
                compiler_params=params(16),
                cost_estimate=step_cost,
                name="attend_first",
            )(in_hbm(queries), in_hbm(part), in_hbm(stat), own[m], other)
            done.append(token)
        else:
            attended, token = pl.pallas_call(
                functools.partial(attend_later, m),
                out_shape=[result, jax.ShapeDtypeStruct((8, HEAD), jnp.float32)],
                in_specs=[vmem] * 5 + [hbm],
                out_specs=[hbm, vmem],
                scratch_shapes=[held, pltpu.SemaphoreType.DMA((local,))],
                input_output_aliases={5: 0},
                compiler_params=params(12),
                cost_estimate=step_cost,
                name="attend_later",
            )(in_vmem(later_q), in_vmem(later_part), in_vmem(later_stat), own[m], other, attended)
            done.append(token)

    child_share = pl.pallas_call(
        share_rewards,
        out_shape=jax.ShapeDtypeStruct((1, local), jnp.float32),
        in_specs=[smem, vmem, vmem],
        out_specs=vmem,
        compiler_params=params(2),
        name="share_rewards",
    )(item, table, done[1]).reshape(local)
    return (attended, child_share)


def solution(mesh):
    in_specs = (
        P(("prompts", "beam"), None, None),
        P(("prompts", "beam"), None, None),
        P(("prompts", "beam"), None, None),
        P(("prompts", "beam"), None, None, None),
        P(("prompts", "beam"), None),
        P(),
        P("prompts"),
    )
    out_specs = (P(("prompts", "beam"), None, None), P(("prompts", "beam")))
    return jax.shard_map(body, mesh=mesh, in_specs=in_specs, out_specs=out_specs, check_vma=False)
```

time: 222 us -> 68.3 us (0.31)
  matrix products: 70.2 us -> 0 us
  blocking collectives: 67 us -> 0 us
  local copies, waits for them, and re-layouts: 55.4 us -> 0.08 us
  Pallas kernels: 0 us -> 44.4 us
  starting transfers between devices: 0.04 us -> 14.1 us
  between operations: 14.8 us -> 0.76 us
  other arithmetic: 5.94 us -> 2.26 us
    pallas_call x0 -> x12, Pallas kernels: none -> 44.4 us  [the longest x1 16.4 us: body(): pl.pallas_call(attend_new, grid=(local,), out_shape=[jax.ShapeDtypeStruct...]
    sub x4 -> x0, matrix products: 36.2 us -> none  [attend_child(): jax.nn.softmax(attention_scores, axis=-1).astype(jnp.bfloat16)]
    unnamed x1 -> x0, blocking collectives: 35.8 us -> none
    dot_general x9 -> x0, matrix products: 34 us -> none  [the longest x4 26.4 us: attend_child(): jnp.einsum('fjip,pfa->ifja', attention_weights, value_head_rows, preferre...]
    psum x1 -> x0, blocking collectives: 31.2 us -> none  [body(): total = lax.psum(jnp.sum(child_reward), 'beam')]
    dynamic_update_slice x8 -> x0, local copies, waits for them, and re-layouts: 17.5 us -> none  [body(): attended = lax.map(attend_child, (queries, keys_all, values_all))]
    dynamic_slice x9 -> x1, local copies, waits for them, and re-layouts: 17.1 us -> 0.08 us  [body(): lax.dynamic_slice_in_dim(item, group_index // heads * (heads * local), he...]
    unnamed x20 -> x0, local copies, waits for them, and re-layouts: 14.1 us -> none
  transfers between devices with their start and end apart: 1 -> 8, of which waited for: 1 -> 2; matrix products, arithmetic and copies ran while one was open for 2% -> 3% of each run, Pallas kernels for 0% -> 53%
where the time goes in v2:
time: 68.3 us; the launch traced here: 68 us
  Pallas kernels  44.4 us (65%)
  starting transfers between devices  14.1 us (21%)
  waiting for transfers between devices  6.43 us (9%)
  other arithmetic  2.26 us (3%)
  between operations  0.76 us (1%)
    pallas_call x1, Pallas kernels, body(): pl.pallas_call(attend_new, grid=(local,), out_shape=[jax.ShapeDtypeStruct...  16.4 us
    pallas_call x3, Pallas kernels, body(): pl.pallas_call(functools.partial(attend_later, m), out_shape=[result, jax...  12.5 us
    pallas_call x1, Pallas kernels, body(): pl.pallas_call(attend_first, out_shape=[result, later, later, pltpu.VMEM(...  9.98 us
    all_to_all x1, starting transfers between devices, body(): table = lax.all_to_all(packed, 'beam', 0, 0)  7.4 us
    ppermute x7, starting transfers between devices, swap(): return lax.ppermute(a, 'beam', [(i, i ^ distance) for i in range(count)])  6.65 us
    all_to_all x1, waiting for transfers between devices, body(): table = lax.all_to_all(packed, 'beam', 0, 0)  5.23 us
    pallas_call x1, Pallas kernels, body(): pl.pallas_call(pack, out_shape=jax.ShapeDtypeStruct((beam_count, KEEP * r...  3.1 us
    pallas_call x1, Pallas kernels, body(): pl.pallas_call(share_rewards, out_shape=jax.ShapeDtypeStruct((1, local),...  1.56 us
  transfers between devices with their start and end apart: 8, of which 2 were waited for; matrix products, arithmetic and copies ran while one was open for 3% of the time, Pallas kernels for 53%

profile of v2, /device:TPU:0, one launch (start us, length us, event | category | flops | bytes accessed | tf_op | source)
XLA Modules:
  0.0 68.0 jit_solution(16613010584114554737)
XLA Ops:
  0.6 3.1 %pack.1 = bf16[16,272,128]{2,1,0:T(8,128)(2,1)} custom-call(s32[1,64]{1,0:T(1,128)} %bitcast.4, bf16[4,2,64,1024]{3,2,1,0:T(8,128)(2,1)} %kv_ref.1, bf16[4,4096]{1,0:T(4,128)(2,1)} %last_ref.1, f32[1,4096]{1,0:T(1,128)} %bitcast.3), custom_call_target="tpu_custom_call" | custom-call | tf_op jit(solution)/shard_map/pack/pallas_call | solution.py:290
  3.7 7.4 %all-to-all-start = ((bf16[16,272,128]{2,1,0:T(8,128)(2,1)}), bf16[16,272,128]{2,1,0:T(8,128)(2,1)S(1)}, u32[]{:S(2)}, u32[]{:S(2)}) async-start(bf16[16,272,128]{2,1,0:T(8,128)(2,1)} %pack.1), calls=%async_computation | async-start | bytes 2228224 | tf_op jit(solution)/shard_map/all_to_all | solution.py:298
  11.2 0.7 and_select_fusion
  11.8 0.9 %and_reduce_fusion = pred[64]{0:T(512)(128)(4,1)S(1)} fusion(s32[64]{0:T(128)} %param.13, s32[64]{0:T(128)S(1)} %and_select_fusion), kind=kLoop, calls=%fused_computation | loop fusion | flops 16320 | bytes 576 | tf_op jit(solution)/shard_map/reduce_or | solution.py:318
  12.7 0.7 convert_add_fusion.item_ref
  13.4 0.1 dynamic_slice.3.item_ref._
  13.5 16.4 %attend_new.1 = (bf16[4,256,4096]{2,1,0:T(8,128)(2,1)}, bf16[4,256,128]{2,1,0:T(8,128)(2,1)}) custom-call(bf16[4,256,4096]{2,1,0:T(8,128)(2,1)} %q_ref.3, bf16[4,256,1024]{2,1,0:T(8,128)(2,1)} %k_ref.1, bf16[4,256,1024]{2,1,0:T(8,128)(2,1)} %v_ref.1), custom_call_target="tpu_custom_call" | custom-call | flops 4294967296 | bytes 25165824 | tf_op jit(solution)/shard_map/attend_new/pallas_call | solution.py:302
  29.9 5.2 %all-to-all-done.table_ref = bf16[16,272,128]{2,1,0:T(8,128)(2,1)S(1)} async-done(((bf16[16,272,128]{2,1,0:T(8,128)(2,1)}), bf16[16,272,128]{2,1,0:T(8,128)(2,1)S(1)}, u32[]{:S(2)}, u32[]{:S(2)}) %all-to-all-start) | async-done | bytes 1114144 | tf_op jit(solution)/shard_map/all_to_all | solution.py:298
  35.2 0.8 %pick.1 = (bf16[1024,128]{1,0:T(8,128)(2,1)S(1)}, bf16[1024,128]{1,0:T(8,128)(2,1)S(1)}, bf16[1024,128]{1,0:T(8,128)(2,1)S(1)}, bf16[1024,128]{1,0:T(8,128)(2,1)S(1)}) custom-call(s32[32]{0:T(128)S(1)} %dynamic_slice.3.item_ref._, bf16[16,272,128]{2,1,0:T(8,128)(2,1)S(1)} %all-to-all-done.table_ref, bf16[4,256,128]{2,1,0:T(8,128)(2,1)} %get-tuple-element.18._.stat_ref), custom_call_target="tpu_custom_call" | custom-call | tf_op jit(solution)/shard_map/pick/pallas_call | solution.py:320
  36.0 2.1 %collective-permute-start.2 = (bf16[1024,128]{1,0:T(8,128)(2,1)S(1)}, bf16[1024,128]{1,0:T(8,128)(2,1)S(1)}, u32[]{:S(2)}, u32[]{:S(2)}) collective-permute-start(bf16[1024,128]{1,0:T(8,128)(2,1)S(1)} %get-tuple-element.24), channel_id=1, source_target_pairs={{0,2},{1,3},{2,0},{3,1},{4,6},{5,7},{6,4},{7,5},{8,10},{9,11},{10,... | collective-permute-start | bytes 786440 | tf_op jit(solution)/shard_map/ppermute | solution.py:271
  38.1 0.6 collective-permute-start
  38.6 3.1 %collective-permute-start.5 = (bf16[1024,128]{1,0:T(8,128)(2,1)S(1)}, bf16[1024,128]{1,0:T(8,128)(2,1)S(1)}, u32[]{:S(2)}, u32[]{:S(2)}) collective-permute-start(bf16[1024,128]{1,0:T(8,128)(2,1)S(1)} %get-tuple-element.28), channel_id=1, source_target_pairs={{0,4},{1,5},{2,6},{3,7},{4,0},{5,1},{6,2},{7,3},{8,12},{9,13},{10,... | collective-permute-start | bytes 786440 | tf_op jit(solution)/shard_map/ppermute | solution.py:271
  41.8 0.0 collective-permute-start.1
  41.8 0.0 collective-permute-done.other_ref
  41.8 10.0 %attend_first.1 = (bf16[4,256,4096]{2,1,0:T(8,128)(2,1)}, bf16[3,4,256,1024]{3,2,1,0:T(8,128)(2,1)S(1)}, bf16[3,4,256,1024]{3,2,1,0:T(8,128)(2,1)S(1)}, bf16[4,256,128]{2,1,0:T(8,128)(2,1)S(1)}, f32[8,128]{1,0:T(8,128)S(1)}) custom-call(bf16[4,256,4096]{2,1,0:T(8,128)(2,1)} %q_ref.3, bf16[4,256,4096]{2,1,0:T(8,128)(2,1)} %get-tuple-element.17.part_ref, ...), custom_call_target="tpu_custom_call" | custom-call | flops 268435456 | bytes 12582912 | tf_op jit(solution)/shard_map/attend_first/pallas_call | solution.py:349
  51.8 0.0 collective-permute-done.2.sent_ref.own_ref
  51.8 0.2 collective-permute-start.3
  52.0 1.2 %collective-permute-done.3.other_ref = bf16[512,128]{1,0:T(8,128)(2,1)S(1)} collective-permute-done((bf16[512,128]{1,0:T(8,128)(2,1)S(1)}, bf16[512,128]{1,0:T(8,128)(2,1)S(1)}, u32[]{:S(2)}, u32[]{:S(2)}) %collective-permute-start.3) | collective-permute-done | bytes 131104 | tf_op jit(solution)/shard_map/ppermute | solution.py:271
  53.2 3.8 %attend_later.3 = (bf16[4,256,4096]{2,1,0:T(8,128)(2,1)}, f32[8,128]{1,0:T(8,128)S(1)}) custom-call(bf16[3,4,256,1024]{3,2,1,0:T(8,128)(2,1)S(1)} %get-tuple-element.20.q_ref, bf16[3,4,256,1024]{3,2,1,0:T(8,128)(2,1)S(1)} %get-tuple-element.21.part_ref, bf16[4,256,128]{2,1,0:T(8,128)(2,1)S(1)} %get-tuple-element.22.stat_ref, ...), custom_call_target="tpu_custom_call", output_to_operand_aliasing={{0}: (5, {})} | custom-call | flops 268435456 | bytes 12582912 | tf_op jit(solution)/shard_map/attend_later/pallas_call | solution.py:362
  57.0 0.0 collective-permute-done.5.sent_ref.own_ref
  57.0 0.2 collective-permute-start.6
  57.2 0.0 collective-permute-done.1.sent_ref.own_ref
  57.3 0.4 collective-permute-start.4
  57.7 1.6 %share_rewards.1 = f32[1,4]{1,0:T(1,128)} custom-call(s32[64]{0:T(128)S(1)} %convert_add_fusion.item_ref, bf16[16,272,128]{2,1,0:T(8,128)(2,1)S(1)} %all-to-all-done.table_ref, f32[8,128]{1,0:T(8,128)S(1)} %get-tuple-element.25._), custom_call_target="tpu_custom_call" | custom-call | tf_op jit(solution)/shard_map/share_rewards/pallas_call | solution.py:375
  59.2 0.0 collective-permute-done.6.other_ref
  59.2 4.4 %attend_later.4 = (bf16[4,256,4096]{2,1,0:T(8,128)(2,1)}, f32[8,128]{1,0:T(8,128)}) custom-call(bf16[3,4,256,1024]{3,2,1,0:T(8,128)(2,1)S(1)} %get-tuple-element.20.q_ref, bf16[3,4,256,1024]{3,2,1,0:T(8,128)(2,1)S(1)} %get-tuple-element.21.part_ref, bf16[4,256,128]{2,1,0:T(8,128)(2,1)S(1)} %get-tuple-element.22.stat_ref, ...), custom_call_target="tpu_custom_call", output_to_operand_aliasing={{0}: (5, {})} | custom-call | flops 268435456 | bytes 12582912 | tf_op jit(solution)/shard_map/attend_later/pallas_call | solution.py:362
  63.6 0.0 collective-permute-done.4.other_ref
  63.6 4.4 %attend_later.5 = (bf16[4,256,4096]{2,1,0:T(8,128)(2,1)}, f32[8,128]{1,0:T(8,128)}) custom-call(bf16[3,4,256,1024]{3,2,1,0:T(8,128)(2,1)S(1)} %get-tuple-element.20.q_ref, bf16[3,4,256,1024]{3,2,1,0:T(8,128)(2,1)S(1)} %get-tuple-element.21.part_ref, bf16[4,256,128]{2,1,0:T(8,128)(2,1)S(1)} %get-tuple-element.22.stat_ref, ...), custom_call_target="tpu_custom_call", output_to_operand_aliasing={{0}: (5, {})} | custom-call | flops 268435456 | bytes 12582912 | tf_op jit(solution)/shard_map/attend_later/pallas_call | solution.py:362
  (4 shorter events, 0.0 us)
Async XLA Ops:
  3.7 31.4 %all-to-all-start = ((bf16[16,272,128]{2,1,0:T(8,128)(2,1)}), bf16[16,272,128]{2,1,0:T(8,128)(2,1)S(1)}, u32[]{:S(2)}, u32[]{:S(2)}) async-start(bf16[16,272,128]{2,1,0:T(8,128)(2,1)} %pack.1), calls=%async_computation | async-start | bytes 2228224 | tf_op jit(solution)/shard_map/all_to_all | solution.py:298
  36.0 15.8 %collective-permute-start.2 = (bf16[1024,128]{1,0:T(8,128)(2,1)S(1)}, bf16[1024,128]{1,0:T(8,128)(2,1)S(1)}, u32[]{:S(2)}, u32[]{:S(2)}) collective-permute-start(bf16[1024,128]{1,0:T(8,128)(2,1)S(1)} %get-tuple-element.24), channel_id=1, source_target_pairs={{0,2},{1,3},{2,0},{3,1},{4,6},{5,7},{6,4},{7,5},{8,10},{9,11},{10,... | collective-permute-start | bytes 786440 | tf_op jit(solution)/shard_map/ppermute | solution.py:271
  38.1 3.7 %collective-permute-start = (bf16[512,128]{1,0:T(8,128)(2,1)S(1)}, bf16[512,128]{1,0:T(8,128)(2,1)S(1)}, u32[]{:S(2)}, u32[]{:S(2)}) collective-permute-start(bf16[512,128]{1,0:T(8,128)(2,1)S(1)} %forward.4), channel_id=1, source_target_pairs={{0,1},{1,0},{2,3},{3,2},{4,5},{5,4},{6,7},{7,6},{8,9},{9,8},{10,11... | collective-permute-start | bytes 393224 | tf_op jit(solution)/shard_map/ppermute | solution.py:271
  38.6 18.4 %collective-permute-start.5 = (bf16[1024,128]{1,0:T(8,128)(2,1)S(1)}, bf16[1024,128]{1,0:T(8,128)(2,1)S(1)}, u32[]{:S(2)}, u32[]{:S(2)}) collective-permute-start(bf16[1024,128]{1,0:T(8,128)(2,1)S(1)} %get-tuple-element.28), channel_id=1, source_target_pairs={{0,4},{1,5},{2,6},{3,7},{4,0},{5,1},{6,2},{7,3},{8,12},{9,13},{10,... | collective-permute-start | bytes 786440 | tf_op jit(solution)/shard_map/ppermute | solution.py:271
  41.8 15.5 %collective-permute-start.1 = (bf16[1024,128]{1,0:T(8,128)(2,1)S(1)}, bf16[1024,128]{1,0:T(8,128)(2,1)S(1)}, u32[]{:S(2)}, u32[]{:S(2)}) collective-permute-start(bf16[1024,128]{1,0:T(8,128)(2,1)S(1)} %get-tuple-element.23), channel_id=1, source_target_pairs={{0,6},{1,7},{2,4},{3,5},{4,2},{5,3},{6,0},{7,1},{8,14},{9,15},{10,... | collective-permute-start | bytes 786440 | tf_op jit(solution)/shard_map/ppermute | solution.py:271
  51.8 1.4 %collective-permute-start.3 = (bf16[512,128]{1,0:T(8,128)(2,1)S(1)}, bf16[512,128]{1,0:T(8,128)(2,1)S(1)}, u32[]{:S(2)}, u32[]{:S(2)}) collective-permute-start(bf16[512,128]{1,0:T(8,128)(2,1)S(1)} %forward.5), channel_id=1, source_target_pairs={{0,1},{1,0},{2,3},{3,2},{4,5},{5,4},{6,7},{7,6},{8,9},{9,8},{10,11... | collective-permute-start | bytes 393224 | tf_op jit(solution)/shard_map/ppermute | solution.py:271
  57.0 2.2 %collective-permute-start.6 = (bf16[512,128]{1,0:T(8,128)(2,1)S(1)}, bf16[512,128]{1,0:T(8,128)(2,1)S(1)}, u32[]{:S(2)}, u32[]{:S(2)}) collective-permute-start(bf16[512,128]{1,0:T(8,128)(2,1)S(1)} %forward.7), channel_id=1, source_target_pairs={{0,1},{1,0},{2,3},{3,2},{4,5},{5,4},{6,7},{7,6},{8,9},{9,8},{10,11... | collective-permute-start | bytes 393224 | tf_op jit(solution)/shard_map/ppermute | solution.py:271
  57.3 6.3 %collective-permute-start.4 = (bf16[512,128]{1,0:T(8,128)(2,1)S(1)}, bf16[512,128]{1,0:T(8,128)(2,1)S(1)}, u32[]{:S(2)}, u32[]{:S(2)}) collective-permute-start(bf16[512,128]{1,0:T(8,128)(2,1)S(1)} %forward.6), channel_id=1, source_target_pairs={{0,1},{1,0},{2,3},{3,2},{4,5},{5,4},{6,7},{7,6},{8,9},{9,8},{10,11... | collective-permute-start | bytes 393224 | tf_op jit(solution)/shard_map/ppermute | solution.py:271

commit v3 on v2

v3 whole, which is shorter than its diff:
```python
import functools
import math

import jax
import jax.numpy as jnp
from jax import lax
from jax.experimental import pallas as pl
from jax.experimental.pallas import tpu as pltpu
from jax.sharding import PartitionSpec as P

HEAD = 128
KEEP = 2
MARK = 16
LIMIT = 100.0
LOG2E = math.log2(math.e)
MIB = 1 << 20
NT = (((1,), (1,)), ((), ()))
NN = (((1,), (0,)), ((), ()))


def mm(a, b, dims=NN):
    return lax.dot_general(a, b, dims, preferred_element_type=jnp.float32)


def kept_pair(parents, base, local):
    own = (parents >= base) & (parents < base + local)
    first = jnp.min(jnp.where(own, parents - base, local))
    last = jnp.max(jnp.where(own, parents - base, -1))
    return first, last


def pack(parents_ref, kv_ref, last_ref, value_ref, out_ref, held_ref, sems):
    local, _, step, width = kv_ref.shape
    heads = width // HEAD
    base = lax.axis_index("beam") * local
    kept = kept_pair(parents_ref[...], base, local)
    copies = [pltpu.make_async_copy(kv_ref.at[k], held_ref.at[r], sems.at[r]) for r, k in enumerate(kept)]
    for copy in copies:
        copy.start()
    hidden = last_ref[...].astype(jnp.float32)
    square = jnp.mean(hidden * hidden, axis=-1, keepdims=True)
    normed = hidden * lax.rsqrt(square + 1e-05)
    score = jnp.sum(normed * value_ref[...], axis=-1, keepdims=True)
    reward = jax.nn.sigmoid(score)
    row = lax.broadcasted_iota(jnp.int32, reward.shape, 0)
    marks = [jnp.sum(jnp.where(row == k, reward, 0.0)) for k in kept]
    tile = lax.broadcasted_iota(jnp.int32, (MARK, HEAD), 0)
    tile = jnp.where(tile < MARK // 2, marks[0], marks[1]).astype(jnp.bfloat16)
    for d in range(out_ref.shape[0]):
        out_ref[d, KEEP * 2 * step :, :] = tile
    for r, copy in enumerate(copies):
        copy.wait()
        for s in range(2):
            for f in range(heads):
                piece = held_ref[r, s, :, f * HEAD : (f + 1) * HEAD]
                start = (r * 2 + s) * step
                for d in range(f, out_ref.shape[0], heads):
                    out_ref[d, start : start + step, :] = piece


def pick(chips, ms, item_ref, table_ref, _, *out_refs):
    rows = (table_ref.shape[1] - MARK) // KEEP
    local = out_refs[0].shape[0] // (2 * rows)
    chip = lax.axis_index("beam") % (2 * chips) // 2
    core = lax.axis_index("beam") % 2
    for n, m in enumerate(ms):
        for other in range(2):
            owner = (chip ^ m) * 2 + (core ^ other)
            for i in range(local):
                item = item_ref[owner * local + i]
                start = pl.multiple_of((item % KEEP) * rows, rows)
                to = (other * local + i) * rows
                out_refs[n][to : to + rows, :] = table_ref[item // KEEP, pl.ds(start, rows), :]


def share_rewards(item_ref, table_ref, out_ref):
    children, local = item_ref.shape[0], out_ref.shape[1]
    rows = table_ref.shape[1] - MARK
    mine = lax.axis_index("beam") * local
    upper = lax.broadcasted_iota(jnp.int32, (MARK, HEAD), 0) < MARK // 2
    lane = lax.broadcasted_iota(jnp.int32, (1, HEAD), 1)

    def reward(child):
        item = item_ref[child]
        tile = table_ref[item // KEEP, rows:, :].astype(jnp.float32)
        tile = jnp.where(upper == (item % KEEP == 0), tile, 0.0)
        return tile[:1, :] + tile[MARK // 2 : MARK // 2 + 1, :]

    total = jnp.zeros((1, HEAD), jnp.float32)
    for child in range(children):
        total = total + reward(child)
    picked = jnp.zeros((1, HEAD), jnp.float32)
    for i in range(local):
        picked = jnp.where(lane == i, reward(mine + i), picked)
    out_ref[...] = (children * picked / total)[:, :local]


def attend_new(q_ref, k_ref, v_ref, out_ref, stat_ref, sums_ref, tops_ref):
    new = q_ref.shape[1]
    half = new // 2
    heads = k_ref.shape[2] // HEAD
    group = q_ref.shape[2] // k_ref.shape[2]
    count = heads * group
    scale = HEAD**-0.5 * LOG2E
    ones = jnp.ones((new, HEAD), jnp.bfloat16)
    lane = lax.broadcasted_iota(jnp.int32, (half, HEAD), 1)
    row = lax.broadcasted_iota(jnp.int32, (half, half), 0)
    column = lax.broadcasted_iota(jnp.int32, (half, half), 1)
    hidden = jnp.concatenate([jnp.where(column <= row, 0.0, -jnp.inf)] * group, axis=0)
    sums_ref[...] = jnp.ones_like(sums_ref)
    tops_ref[...] = jnp.zeros_like(tops_ref)

    def block(f, shifted):
        lanes = lambda n: pl.ds(pl.multiple_of(n * HEAD, HEAD), HEAD)
        keys = k_ref[0, :, lanes(f)]
        values = jnp.concatenate([v_ref[0, :, lanes(f)], ones], axis=1)
        columns = [lanes(f * group + h) for h in range(group)]
        most = None
        for r in range(2):
            seen = (r + 1) * half
            rows = slice(r * half, (r + 1) * half)
            query = jnp.concatenate([q_ref[0, rows, c] for c in columns], axis=0)
            logits = mm(query, keys[:seen], NT) * scale
            blocks = [logits[:, n * half : (n + 1) * half] for n in range(r + 1)]
            if not shifted:
                for a in blocks:
                    size = jnp.max(jnp.abs(a).reshape(-1, 8, half), axis=0)
                    most = size if most is None else jnp.maximum(most, size)
            blocks[r] = blocks[r] + hidden
            if shifted:
                top = functools.reduce(jnp.maximum, [jnp.max(a, axis=1, keepdims=True) for a in blocks])
                top = top.astype(jnp.bfloat16).astype(jnp.float32)
                blocks = [a - top for a in blocks]
            weights = jnp.concatenate([jnp.exp2(a).astype(jnp.bfloat16) for a in blocks], axis=1)
            both = mm(weights, values[:seen])
            for h in range(group):
                s = slice(h * half, (h + 1) * half)
                out_ref[0, rows, columns[h]] = both[s, :HEAD].astype(jnp.bfloat16)
                here = lane == f * group + h
                sums_ref[rows, :] = jnp.where(here, both[s, HEAD:], sums_ref[rows, :])
                if shifted:
                    tops_ref[rows, :] = jnp.where(here, top[s], tops_ref[rows, :])
        return most

    most = functools.reduce(jnp.maximum, [block(f, False) for f in range(heads)])

    @pl.when(jnp.max(most) > LIMIT)
    def _():
        lax.fori_loop(0, heads, lambda f, c: (block(f, True), c)[1], 0)

    sums = sums_ref[...]
    high = sums.astype(jnp.bfloat16).astype(jnp.float32)
    rest = pltpu.roll(sums - high, count, 1)
    tops = pltpu.roll(tops_ref[...], 2 * count, 1)
    lane = lax.broadcasted_iota(jnp.int32, (new, HEAD), 1)
    stat = jnp.where(lane < count, high, jnp.where(lane < 2 * count, rest, jnp.where(lane < 3 * count, tops, 0.0)))
    stat_ref[0] = stat.astype(jnp.bfloat16)


def block_pair(a):
    zero = jnp.zeros_like(a)
    return jnp.concatenate([jnp.concatenate([a, zero], axis=1), jnp.concatenate([zero, a], axis=1)], axis=0)


def forward(sent_ref, _, out_ref):
    out_ref[...] = sent_ref[sent_ref.shape[0] - out_ref.shape[0] :, :]


class Block:
    def __init__(self, q_ref, part_ref, stat_ref, own_ref, other_ref, out_ref, count, place, i, f):
        new, width = q_ref.shape[1:]
        rows = own_ref.shape[0] // (2 * q_ref.shape[0])
        self.step = rows // 2
        pairs = width // (2 * HEAD)
        core = lax.axis_index("beam") % 2
        here = pl.ds(pl.multiple_of(i * rows, rows), rows)
        self.piece = jnp.where(f == core, own_ref[here, :], other_ref[here, :])
        group = [f * (pairs // 2) + p for p in range(pairs // 2)]
        self.columns = [pl.ds(pl.multiple_of(p * 2 * HEAD, 2 * HEAD), 2 * HEAD) for p in group]
        self.heads = [(place * pairs + p) * 2 for p in group]
        self.q_ref, self.part_ref, self.stat_ref, self.out_ref = q_ref, part_ref, stat_ref, out_ref
        self.i, self.count, self.new = i, count, new

    def logits(self):
        keys = block_pair(self.piece[: self.step])
        queries = jnp.concatenate([self.q_ref[self.i, :, c] for c in self.columns], axis=0)
        return mm(queries, keys, NT) * (HEAD**-0.5 * LOG2E)

    def tail(self):
        lane = lax.broadcasted_iota(jnp.int32, (self.new, HEAD), 1)
        pair_of_lane = jnp.where(lane < 2 * self.count, lane % self.count // 2 * 2, -1)
        stat = self.stat_ref[self.i]
        sums = jnp.concatenate([jnp.where(pair_of_lane == h, stat, jnp.zeros_like(stat)) for h in self.heads], axis=0)
        part = jnp.concatenate([self.part_ref[self.i, :, c] for c in self.columns], axis=0).astype(jnp.float32)
        values = block_pair(self.piece[self.step :])
        ones = block_pair(jnp.ones((self.step, HEAD), jnp.bfloat16))
        odd = lax.broadcasted_iota(jnp.int32, (HEAD, 2 * HEAD), 0) % 2
        spread = (odd == lax.broadcasted_iota(jnp.int32, (HEAD, 2 * HEAD), 1) // HEAD).astype(jnp.bfloat16)
        return values, ones, spread, sums, part

    def store(self, added, total):
        result = (added * pltpu.reciprocal(total, approx=True)).astype(jnp.bfloat16)
        for n, c in enumerate(self.columns):
            self.out_ref[self.i, :, c] = result[n * self.new : (n + 1) * self.new]

    def weigh(self):
        logits = self.logits()
        return jnp.exp2(logits).astype(jnp.bfloat16), jnp.max(logits.reshape(-1, 8, HEAD), axis=0)

    def finish(self, weights):
        part = jnp.concatenate([self.part_ref[self.i, :, c] for c in self.columns], axis=0).astype(jnp.float32)
        added = mm(weights, block_pair(self.piece[self.step :]))
        lane = lax.broadcasted_iota(jnp.int32, (self.new, HEAD), 1)
        low = lax.broadcasted_iota(jnp.int32, weights.shape, 1) < self.step
        stat = self.stat_ref[self.i].astype(jnp.float32)
        here = jnp.where(lane < 2 * self.count, lane % self.count, -1)
        wide = weights.astype(jnp.float32)
        totals = []
        for n, k in enumerate((low, ~low)):
            sums = jnp.concatenate([jnp.where(here == h + n, stat, 0.0) for h in self.heads], axis=0)
            total = jnp.sum(jnp.where(k, wide, 0.0) + sums, axis=1, keepdims=True)
            totals.append(jnp.broadcast_to(pltpu.reciprocal(total, approx=True), low.shape))
        result = ((part + added) * jnp.concatenate(totals, axis=1)).astype(jnp.bfloat16)
        for n, c in enumerate(self.columns):
            self.out_ref[self.i, :, c] = result[n * self.new : (n + 1) * self.new]

    def shifted(self):
        logits = self.logits()
        low = lax.broadcasted_iota(jnp.int32, logits.shape, 1) < self.step
        lane = lax.broadcasted_iota(jnp.int32, (self.new, HEAD), 1) - 2 * self.count
        stat = self.stat_ref[self.i].astype(jnp.float32)
        shift = lambda h: jnp.sum(jnp.where(lane == h, stat, 0.0), axis=1, keepdims=True)
        shifts = [jnp.concatenate([shift(h + n) for h in self.heads], axis=0) for n in range(2)]
        logits = logits - jnp.where(low, shifts[0], shifts[1])
        tops = [jnp.maximum(jnp.max(jnp.where(k, logits, 0.0), axis=1, keepdims=True), 0.0) for k in (low, ~low)]
        weights = jnp.exp2(logits - jnp.where(low, tops[0], tops[1])).astype(jnp.bfloat16)
        rest = jnp.concatenate([jnp.broadcast_to(jnp.exp2(-t), low.shape) for t in tops], axis=1)
        values, ones, spread, sums, part = self.tail()
        self.store(part * rest + mm(weights, values), mm(weights, ones) + mm(sums, spread) * rest)


def attend_blocks(works, stat_ref, held_ref, out_ref, sems, ready):
    local, _, width = works[0][0].shape
    count = out_ref.shape[2] // HEAD

    def block(n, i, f):
        q_ref, part_ref, own_ref, other_ref, place = works[n]
        return Block(q_ref, part_ref, stat_ref, own_ref, other_ref, held_ref.at[n], count, place, i, f)

    def send(n, i):
        lanes = pl.ds(pl.multiple_of(works[n][4] * width, width), width)
        return pltpu.make_async_copy(held_ref.at[n, i], out_ref.at[i, :, lanes], sems.at[n, i])

    lane = lax.broadcasted_iota(jnp.int32, stat_ref.shape[1:], 1)

    def work(n, i, carry):
        most, weights = carry
        later, top = block(n, i, 1).weigh()
        block(n, i, 0).finish(weights)
        most = jnp.maximum(most, top)
        following = jnp.minimum(i + 1, local - 1)
        ready(following, i + 1 < local)
        weights, top = block(n, following, 0).weigh()
        block(n, i, 1).finish(later)
        send(n, i).start()
        return jnp.maximum(most, top), weights

    def moved(i, most):
        tops = jnp.where(lane >= 2 * count, stat_ref[i].astype(jnp.float32), 0.0)
        tops = jnp.where(tops == 0.0, -jnp.inf, jnp.inf)
        return jnp.maximum(most, jnp.max(tops.reshape(-1, 8, HEAD), axis=0))

    most = jnp.full((8, HEAD), -jnp.inf, jnp.float32)
    ready(0, True)
    for n in range(len(works)):
        weights, top = block(n, 0, 0).weigh()
        most, _ = lax.fori_loop(0, local, functools.partial(work, n), (jnp.maximum(most, top), weights))
    most = lax.fori_loop(0, local, moved, most)
    every = [(n, i) for n in range(len(works)) for i in range(local)]
    for n, i in every:
        send(n, i).wait()

    @pl.when(jnp.max(most) > LIMIT)
    def _():
        for n in range(len(works)):
            lax.fori_loop(0, 2 * local, lambda t, c: (block(n, t // 2, t % 2).shifted(), c)[1], 0)
        for n, i in every:
            send(n, i).start()
        for n, i in every:
            send(n, i).wait()


def stage(q_ref, part_ref, m, i, to_q, to_part, sems, chips):
    width = to_q.shape[2]
    place = lax.axis_index("beam") % (2 * chips) // 2 ^ m
    lanes = pl.ds(pl.multiple_of(place * width, width), width)
    pairs = ((q_ref, to_q), (part_ref, to_part))
    return [pltpu.make_async_copy(a.at[i, :, lanes], to.at[i], sems.at[k, i]) for k, (a, to) in enumerate(pairs)]


def attend_first(chips, item_ref, table_ref, q_ref, part_ref, stat_ref, own_ref, other_ref, *refs):
    out_ref, share_ref, next_q, next_part, stat_out, token_ref = refs[:6]
    held_q, held_part, held, sems, next_sems, stat_sem, out_sems = refs[6:]
    local = held_q.shape[0]
    chip = lax.axis_index("beam") % (2 * chips) // 2
    mine = lambda i: stage(q_ref, part_ref, 0, i, held_q, held_part, sems, chips)
    following = lambda i: stage(q_ref, part_ref, 1, i, next_q, next_part, next_sems, chips)
    stat_copy = pltpu.make_async_copy(stat_ref, stat_out, stat_sem)
    stat_copy.start()
    for i in range(local):
        for copy in mine(i):
            copy.start()
    token_ref[...] = jnp.zeros_like(token_ref)
    share_rewards(item_ref, table_ref, share_ref)

    def ready(i, due):
        @pl.when(due)
        def _():
            for copy in mine(i):
                copy.wait()
            for copy in following(i):
                copy.start()

    stat_copy.wait()
    attend_blocks([(held_q, held_part, own_ref, other_ref, chip)], stat_out, held, out_ref, out_sems, ready)
    for i in range(local):
        for copy in following(i):
            copy.wait()


def attend_second(chips, q_ref, part_ref, next_q, next_part, stat_ref, own_ref, other_ref, _, *refs):
    out_ref, token_ref, *later = refs[: 2 + 2 * (chips - 2)]
    held, sems, next_sems = refs[2 + 2 * (chips - 2) :]
    local = held.shape[1]
    chip = lax.axis_index("beam") % (2 * chips) // 2

    def staged():
        for n, m in enumerate(range(2, chips)):
            for i in range(local):
                yield from stage(q_ref, part_ref, m, i, later[2 * n], later[2 * n + 1], next_sems.at[n], chips)

    for copy in staged():
        copy.start()
    token_ref[...] = jnp.zeros_like(token_ref)
    works = [(next_q, next_part, own_ref, other_ref, chip ^ 1)]
    attend_blocks(works, stat_ref, held, out_ref, sems, lambda i, due: None)
    for copy in staged():
        copy.wait()


def attend_last(chips, stat_ref, *refs):
    operands, (_, out_ref, held, sems) = refs[: 4 * (chips - 2)], refs[4 * (chips - 2) :]
    chip = lax.axis_index("beam") % (2 * chips) // 2
    works = [(*operands[4 * n : 4 * n + 4], chip ^ m) for n, m in enumerate(range(2, chips))]
    attend_blocks(works, stat_ref, held, out_ref, sems, lambda i, due: None)


def params(mib):
    return pltpu.CompilerParams(vmem_limit_bytes=mib * MIB)


def swap(a, distance):
    count = lax.axis_size("beam")
    return lax.ppermute(a, "beam", [(i, i ^ distance) for i in range(count)])


def body(queries, new_keys, new_values, step_kv, prm_last, value_head, parents):
    beam_count = lax.axis_size("beam")
    group_index = lax.axis_index("beam")
    local, new, width = queries.shape
    children = parents.shape[0]
    step = step_kv.shape[2]
    kv_width = step_kv.shape[3]
    heads = kv_width // HEAD
    chips = heads // 2
    vmem = pl.BlockSpec(memory_space=pltpu.VMEM)
    smem = pl.BlockSpec(memory_space=pltpu.SMEM)
    bf16 = jnp.bfloat16

    rows = 2 * step
    in_hbm = lambda a: pltpu.with_memory_space_constraint(a, pltpu.HBM)
    in_vmem = lambda a: pltpu.with_memory_space_constraint(a, pltpu.VMEM)
    packed = pl.pallas_call(
        pack,
        out_shape=jax.ShapeDtypeStruct((beam_count, KEEP * rows + MARK, HEAD), bf16),
        in_specs=[vmem, pl.BlockSpec(memory_space=pl.ANY), vmem, vmem],
        out_specs=vmem,
        scratch_shapes=[pltpu.VMEM((KEEP, 2, step, kv_width), bf16), pltpu.SemaphoreType.DMA((KEEP,))],
        name="pack",
    )(parents.reshape(1, children), step_kv, prm_last, value_head.reshape(1, -1))
    table = lax.all_to_all(packed, "beam", 0, 0)

    cost = lambda f, t, b: pl.CostEstimate(flops=f, transcendentals=t, bytes_accessed=b)
    small = cost(1024, 0, 1024)
    whole = lambda w: pl.BlockSpec((1, new, w), lambda i: (i, 0, 0))
    part, stat = pl.pallas_call(
        attend_new,
        grid=(local,),
        out_shape=[
            jax.ShapeDtypeStruct((local, new, width), bf16),
            jax.ShapeDtypeStruct((local, new, HEAD), bf16),
        ],
        in_specs=[whole(width), whole(kv_width), whole(kv_width)],
        out_specs=[whole(width), whole(HEAD)],
        scratch_shapes=[pltpu.VMEM((new, HEAD), jnp.float32)] * 2,
        compiler_params=params(56),
        cost_estimate=cost(4 * local * new * new * width, local * new * new * width // HEAD, 6 * local * new * width),
        name="attend_new",
    )(queries, new_keys, new_values)

    owner = parents // local
    earlier = (owner[:, None] == owner[None, :]) & (parents[None, :] < parents[:, None])
    item = owner * KEEP + jnp.any(earlier, axis=1).astype(jnp.int32)
    near = lax.dynamic_slice_in_dim(item, group_index // heads * (heads * local), heads * local)
    anywhere = pl.BlockSpec(memory_space=pl.ANY)
    hbm = pl.BlockSpec(memory_space=pltpu.HBM)

    def picked(ms, after):
        return pl.pallas_call(
            functools.partial(pick, chips, ms),
            out_shape=[jax.ShapeDtypeStruct((2 * local * rows, HEAD), bf16)] * len(ms),
            in_specs=[smem, vmem, anywhere],
            out_specs=[vmem] * len(ms),
            compiler_params=params(4),
            cost_estimate=small,
            name="pick",
        )(near, table, after)

    def pass_on(piece, after):
        passed = pl.pallas_call(
            forward,
            out_shape=jax.ShapeDtypeStruct((local * rows, HEAD), bf16),
            in_specs=[vmem, anywhere],
            out_specs=vmem,
            compiler_params=params(2),
            cost_estimate=small,
            name="forward",
        )(piece, after)
        return swap(passed, 1)

    far = tuple(range(2, chips))
    pieces = picked(far, in_hbm(stat))
    pieces = picked((0, 1), pieces[0]) + pieces
    own = [pieces[0]] + [swap(pieces[m], 2 * m) for m in range(1, chips)]
    wide = width // chips
    result = jax.ShapeDtypeStruct((local, new, width), bf16)
    token = jax.ShapeDtypeStruct((8, HEAD), jnp.float32)
    later = pltpu.VMEM((local, new, wide), bf16)
    held = lambda n: pltpu.VMEM((n, local, new, wide), bf16)
    many = pltpu.SemaphoreType.DMA
    attended, child_share, next_q, next_part, stat_held, done = pl.pallas_call(
        functools.partial(attend_first, chips),
        out_shape=[
            result,
            jax.ShapeDtypeStruct((1, local), jnp.float32),
            later,
            later,
            pltpu.VMEM(stat.shape, bf16),
            token,
        ],
        in_specs=[smem, vmem, hbm, hbm, hbm, vmem, vmem],
        out_specs=[hbm] + [vmem] * 5,
        scratch_shapes=[later] * 2 + [held(1), many((2, local)), many((2, local)), many, many((1, local))],
        compiler_params=params(16),
        cost_estimate=small,
        name="attend_first",
    )(item, table, in_hbm(queries), in_hbm(part), in_hbm(stat), own[0], pass_on(own[0], near))
    attended, done, *staged = pl.pallas_call(
        functools.partial(attend_second, chips),
        out_shape=[result, token] + [later] * (2 * len(far)),
        in_specs=[hbm, hbm] + [vmem] * 5 + [hbm],
        out_specs=[hbm, vmem] + [vmem] * (2 * len(far)),
        scratch_shapes=[held(1), many((1, local)), many((len(far), 2, local))],
        input_output_aliases={7: 0},
        compiler_params=params(12),
        cost_estimate=small,
        name="attend_second",
    )(
        in_hbm(queries),
        in_hbm(part),
        in_vmem(next_q),
        in_vmem(next_part),
        in_vmem(stat_held),
        own[1],
        pass_on(own[1], done),
        attended,
    )
    operands = []
    for n, m in enumerate(far):
        operands += [in_vmem(staged[2 * n]), in_vmem(staged[2 * n + 1]), own[m], pass_on(own[m], done)]
    attended = pl.pallas_call(
        functools.partial(attend_last, chips),
        out_shape=result,
        in_specs=[vmem] * (1 + len(operands)) + [hbm],
        out_specs=hbm,
        scratch_shapes=[held(len(far)), many((len(far), local))],
        input_output_aliases={1 + len(operands): 0},
        compiler_params=params(12),
        cost_estimate=small,
        name="attend_last",
    )(in_vmem(stat_held), *operands, attended)
    child_share = child_share.reshape(local)
    return (attended, child_share)


def solution(mesh):
    in_specs = (
        P(("prompts", "beam"), None, None),
        P(("prompts", "beam"), None, None),
        P(("prompts", "beam"), None, None),
        P(("prompts", "beam"), None, None, None),
        P(("prompts", "beam"), None),
        P(),
        P("prompts"),
    )
    out_specs = (P(("prompts", "beam"), None, None), P(("prompts", "beam")))
    return jax.shard_map(body, mesh=mesh, in_specs=in_specs, out_specs=out_specs, check_vma=False)
```

time: 68.3 us -> 107 us (1.57)
  Pallas kernels: 44.4 us -> 91.9 us
  waiting for transfers between devices: 6.43 us -> 2.32 us
  starting transfers between devices: 14.1 us -> 11.8 us
  other arithmetic: 2.26 us -> 0.2 us
    pallas_call x10 -> x9, Pallas kernels: 24.9 us -> 55.2 us  [the longest x1 24.1 us: body(): pl.pallas_call(functools.partial(attend_last, chips), out_shape=result, i...]
    pallas_call x1, Pallas kernels: 16.4 us -> 33.6 us  [body(): pl.pallas_call(attend_new, grid=(local,), out_shape=[jax.ShapeDtypeStruct...]
    all_to_all x1, waiting for transfers between devices: 5.23 us -> 0.01 us  [body(): table = lax.all_to_all(packed, 'beam', 0, 0)]
    ppermute x7, starting transfers between devices: 6.65 us -> 4.45 us  [swap(): return lax.ppermute(a, 'beam', [(i, i ^ distance) for i in range(count)])]
    ppermute x7, waiting for transfers between devices: 1.2 us -> 2.31 us  [swap(): return lax.ppermute(a, 'beam', [(i, i ^ distance) for i in range(count)])]
  transfers between devices with their start and end apart: 8 -> 8, of which waited for: 2 -> 3; matrix products, arithmetic and copies ran while one was open for 3% -> 0% of each run, Pallas kernels for 53% -> 59%
where the time goes in v3:
time: 107 us
  Pallas kernels  91.9 us (86%)
  starting transfers between devices  11.8 us (11%)
  waiting for transfers between devices  2.32 us (2%)
    pallas_call x1, Pallas kernels, body(): pl.pallas_call(attend_new, grid=(local,), out_shape=[jax.ShapeDtypeStruct...  33.6 us
    pallas_call x1, Pallas kernels, body(): pl.pallas_call(functools.partial(attend_last, chips), out_shape=result, i...  24.1 us
    pallas_call x1, Pallas kernels, body(): pl.pallas_call(functools.partial(attend_first, chips), out_shape=[result,...  16.7 us
    pallas_call x1, Pallas kernels, body(): pl.pallas_call(functools.partial(attend_second, chips), out_shape=[result...  13 us
    all_to_all x1, starting transfers between devices, body(): table = lax.all_to_all(packed, 'beam', 0, 0)  7.4 us
    ppermute x7, starting transfers between devices, swap(): return lax.ppermute(a, 'beam', [(i, i ^ distance) for i in range(count)])  4.45 us
    pallas_call x1, Pallas kernels, body(): pl.pallas_call(pack, out_shape=jax.ShapeDtypeStruct((beam_count, KEEP * r...  3.1 us
    ppermute x7, waiting for transfers between devices, swap(): return lax.ppermute(a, 'beam', [(i, i ^ distance) for i in range(count)])  2.31 us
  transfers between devices with their start and end apart: 8, of which 3 were waited for; matrix products, arithmetic and copies ran while one was open for 0% of the time, Pallas kernels for 59%

profile of v3, /device:TPU:0, one launch (start us, length us, event | category | flops | bytes accessed | tf_op | source)
XLA Modules:
  0.0 107.1 jit_solution(695487642983725720)
XLA Ops:
  0.6 0.0 copy-start
  0.6 3.1 %pack.1 = bf16[16,272,128]{2,1,0:T(8,128)(2,1)} custom-call(s32[1,64]{1,0:T(1,128)} %bitcast.4, bf16[4,2,64,1024]{3,2,1,0:T(8,128)(2,1)} %kv_ref.1, bf16[4,4096]{1,0:T(4,128)(2,1)} %last_ref.1, f32[1,4096]{1,0:T(1,128)} %bitcast.3), custom_call_target="tpu_custom_call" | custom-call | tf_op jit(solution)/shard_map/pack/pallas_call | solution.py:383
  3.7 7.4 %all-to-all-start = ((bf16[16,272,128]{2,1,0:T(8,128)(2,1)}), bf16[16,272,128]{2,1,0:T(8,128)(2,1)S(1)}, u32[]{:S(2)}, u32[]{:S(2)}) async-start(bf16[16,272,128]{2,1,0:T(8,128)(2,1)} %pack.1), calls=%async_computation | async-start | bytes 2228224 | tf_op jit(solution)/shard_map/all_to_all | solution.py:391
  11.2 0.0 copy-done
  11.2 0.2 and_reduce_fusion
  11.4 0.1 dynamic_slice.3.item_ref._
  11.5 33.6 %attend_new.1 = (bf16[4,256,4096]{2,1,0:T(8,128)(2,1)}, bf16[4,256,128]{2,1,0:T(8,128)(2,1)}) custom-call(bf16[4,256,4096]{2,1,0:T(8,128)(2,1)} %q_ref.5, bf16[4,256,1024]{2,1,0:T(8,128)(2,1)} %k_ref.1, bf16[4,256,1024]{2,1,0:T(8,128)(2,1)} %v_ref.1), custom_call_target="tpu_custom_call" | custom-call | flops 4294967296 | bytes 25165824 | tf_op jit(solution)/shard_map/attend_new/pallas_call | solution.py:396
  45.1 0.0 all-to-all-done.table_ref
  45.1 0.7 pick.2
  45.8 0.7 pick.3
  46.4 2.0 %collective-permute-start.1 = (bf16[1024,128]{1,0:T(8,128)(2,1)S(1)}, bf16[1024,128]{1,0:T(8,128)(2,1)S(1)}, u32[]{:S(2)}, u32[]{:S(2)}) collective-permute-start(bf16[1024,128]{1,0:T(8,128)(2,1)S(1)} %get-tuple-element.27), channel_id=1, source_target_pairs={{0,2},{1,3},{2,0},{3,1},{4,6},{5,7},{6,4},{7,5},{8,10},{9,11},{10,... | collective-permute-start | bytes 786440 | tf_op jit(solution)/shard_map/ppermute | solution.py:364
  48.4 0.1 collective-permute-start
  48.5 1.5 %collective-permute-start.3 = (bf16[1024,128]{1,0:T(8,128)(2,1)S(1)}, bf16[1024,128]{1,0:T(8,128)(2,1)S(1)}, u32[]{:S(2)}, u32[]{:S(2)}) collective-permute-start(bf16[1024,128]{1,0:T(8,128)(2,1)S(1)} %get-tuple-element.22._), channel_id=1, source_target_pairs={{0,4},{1,5},{2,6},{3,7},{4,0},{5,1},{6,2},{7,3},{8,12},{9,13},{10,... | collective-permute-start | bytes 786440 | tf_op jit(solution)/shard_map/ppermute | solution.py:364
  50.0 0.1 collective-permute-start.5
  50.2 0.0 collective-permute-done.other_ref
  50.2 16.7 %attend_first.1 = (bf16[4,256,4096]{2,1,0:T(8,128)(2,1)}, f32[1,4]{1,0:T(1,128)}, bf16[4,256,1024]{2,1,0:T(8,128)(2,1)S(1)}, bf16[4,256,1024]{2,1,0:T(8,128)(2,1...) custom-call(s32[64]{0:T(128)S(1)} %convert_add_fusion.item_ref, ...), custom_call_target="tpu_custom_call" | custom-call | flops 1024 | bytes 1024 | tf_op jit(solution)/shard_map/attend_first/pallas_call | solution.py:451
  66.9 0.0 collective-permute-done.1.sent_ref.own_ref
  67.0 0.1 collective-permute-start.2
  67.1 1.3 %collective-permute-done.2.other_ref = bf16[512,128]{1,0:T(8,128)(2,1)S(1)} collective-permute-done((bf16[512,128]{1,0:T(8,128)(2,1)S(1)}, bf16[512,128]{1,0:T(8,128)(2,1)S(1)}, u32[]{:S(2)}, u32[]{:S(2)}) %collective-permute-start.2) | collective-permute-done | bytes 131104 | tf_op jit(solution)/shard_map/ppermute | solution.py:364
  68.4 13.0 %attend_second.1 = (bf16[4,256,4096]{2,1,0:T(8,128)(2,1)}, f32[8,128]{1,0:T(8,128)S(1)}, bf16[4,256,1024]{2,1,0:T(8,128)(2,1)S(1)}, bf16[4,256,1024]{2,1,0:T(8,1...) custom-call(bf16[4,256,4096]{2,1,0:T(8,128)(2,1)} %q_ref.5, ...), custom_call_target="tpu_custom_call", output_to_operand_aliasing={{0}: (7, {})} | custom-call | flops 1024 | bytes 1024 | tf_op jit(solution)/shard_map/attend_second/pallas_call | solution.py:468
  81.4 0.0 collective-permute-done.3.sent_ref.refs_2_
  81.4 0.2 collective-permute-start.4
  81.6 0.0 collective-permute-done.5.sent_ref.refs_6_
  81.6 0.4 collective-permute-start.6
  82.1 0.8 collective-permute-done.4.refs_3_
  82.8 0.2 collective-permute-done.6.refs_7_
  83.0 24.1 %attend_last.1 = bf16[4,256,4096]{2,1,0:T(8,128)(2,1)} custom-call(bf16[4,256,128]{2,1,0:T(8,128)(2,1)S(1)} %get-tuple-element.24.stat_ref, bf16[4,256,1024]{2,1,0:T(8,128)(2,1)S(1)} %get-tuple-element.30.refs_0_, bf16[4,256,1024]{2,1,0:T(8,128)(2,1)S(1)} %get-tuple-element.31.refs_1_, ...), custom_call_target="tpu_custom_call", output_to_operand_aliasing={{}: (9, {})} | custom-call | flops 1024 | bytes 1024 | tf_op jit(solution)/shard_map/attend_last/pallas_call | solution.py:491
  (6 shorter events, 0.1 us)
Async XLA Ops:
  0.6 10.5 %copy-start = (s32[64]{0:T(128)S(1)}, s32[64]{0:T(128)}, u32[]{:S(2)}) copy-start(s32[64]{0:T(128)} %param.13) | copy-start | bytes 772
  3.7 41.3 %all-to-all-start = ((bf16[16,272,128]{2,1,0:T(8,128)(2,1)}), bf16[16,272,128]{2,1,0:T(8,128)(2,1)S(1)}, u32[]{:S(2)}, u32[]{:S(2)}) async-start(bf16[16,272,128]{2,1,0:T(8,128)(2,1)} %pack.1), calls=%async_computation | async-start | bytes 2228224 | tf_op jit(solution)/shard_map/all_to_all | solution.py:391
  46.4 20.5 %collective-permute-start.1 = (bf16[1024,128]{1,0:T(8,128)(2,1)S(1)}, bf16[1024,128]{1,0:T(8,128)(2,1)S(1)}, u32[]{:S(2)}, u32[]{:S(2)}) collective-permute-start(bf16[1024,128]{1,0:T(8,128)(2,1)S(1)} %get-tuple-element.27), channel_id=1, source_target_pairs={{0,2},{1,3},{2,0},{3,1},{4,6},{5,7},{6,4},{7,5},{8,10},{9,11},{10,... | collective-permute-start | bytes 786440 | tf_op jit(solution)/shard_map/ppermute | solution.py:364
  48.4 1.8 %collective-permute-start = (bf16[512,128]{1,0:T(8,128)(2,1)S(1)}, bf16[512,128]{1,0:T(8,128)(2,1)S(1)}, u32[]{:S(2)}, u32[]{:S(2)}) collective-permute-start(bf16[512,128]{1,0:T(8,128)(2,1)S(1)} %forward.4), channel_id=1, source_target_pairs={{0,1},{1,0},{2,3},{3,2},{4,5},{5,4},{6,7},{7,6},{8,9},{9,8},{10,11... | collective-permute-start | bytes 393224 | tf_op jit(solution)/shard_map/ppermute | solution.py:364
  48.5 32.9 %collective-permute-start.3 = (bf16[1024,128]{1,0:T(8,128)(2,1)S(1)}, bf16[1024,128]{1,0:T(8,128)(2,1)S(1)}, u32[]{:S(2)}, u32[]{:S(2)}) collective-permute-start(bf16[1024,128]{1,0:T(8,128)(2,1)S(1)} %get-tuple-element.22._), channel_id=1, source_target_pairs={{0,4},{1,5},{2,6},{3,7},{4,0},{5,1},{6,2},{7,3},{8,12},{9,13},{10,... | collective-permute-start | bytes 786440 | tf_op jit(solution)/shard_map/ppermute | solution.py:364
  50.0 31.6 %collective-permute-start.5 = (bf16[1024,128]{1,0:T(8,128)(2,1)S(1)}, bf16[1024,128]{1,0:T(8,128)(2,1)S(1)}, u32[]{:S(2)}, u32[]{:S(2)}) collective-permute-start(bf16[1024,128]{1,0:T(8,128)(2,1)S(1)} %get-tuple-element.35), channel_id=1, source_target_pairs={{0,6},{1,7},{2,4},{3,5},{4,2},{5,3},{6,0},{7,1},{8,14},{9,15},{10,... | collective-permute-start | bytes 786440 | tf_op jit(solution)/shard_map/ppermute | solution.py:364
  67.0 1.4 %collective-permute-start.2 = (bf16[512,128]{1,0:T(8,128)(2,1)S(1)}, bf16[512,128]{1,0:T(8,128)(2,1)S(1)}, u32[]{:S(2)}, u32[]{:S(2)}) collective-permute-start(bf16[512,128]{1,0:T(8,128)(2,1)S(1)} %forward.5), channel_id=1, source_target_pairs={{0,1},{1,0},{2,3},{3,2},{4,5},{5,4},{6,7},{7,6},{8,9},{9,8},{10,11... | collective-permute-start | bytes 393224 | tf_op jit(solution)/shard_map/ppermute | solution.py:364
  81.4 1.4 %collective-permute-start.4 = (bf16[512,128]{1,0:T(8,128)(2,1)S(1)}, bf16[512,128]{1,0:T(8,128)(2,1)S(1)}, u32[]{:S(2)}, u32[]{:S(2)}) collective-permute-start(bf16[512,128]{1,0:T(8,128)(2,1)S(1)} %forward.6), channel_id=1, source_target_pairs={{0,1},{1,0},{2,3},{3,2},{4,5},{5,4},{6,7},{7,6},{8,9},{9,8},{10,11... | collective-permute-start | bytes 393224 | tf_op jit(solution)/shard_map/ppermute | solution.py:364
  81.6 1.4 %collective-permute-start.6 = (bf16[512,128]{1,0:T(8,128)(2,1)S(1)}, bf16[512,128]{1,0:T(8,128)(2,1)S(1)}, u32[]{:S(2)}, u32[]{:S(2)}) collective-permute-start(bf16[512,128]{1,0:T(8,128)(2,1)S(1)} %forward.7), channel_id=1, source_target_pairs={{0,1},{1,0},{2,3},{3,2},{4,5},{5,4},{6,7},{7,6},{8,9},{9,8},{10,11... | collective-permute-start | bytes 393224 | tf_op jit(solution)/shard_map/ppermute | solution.py:364

commit v4 on v3

--- a/solution.py
+++ b/solution.py
@@ -29,33 +29,41 @@
     return first, last
 
 
-def pack(parents_ref, kv_ref, last_ref, value_ref, out_ref, held_ref, sems):
-    local, _, step, width = kv_ref.shape
+def pack(parents_hbm, kv_hbm, last_hbm, value_hbm, out_ref, parents_ref, held_ref, last_ref, value_ref, piece_ref, *sems):
+    local, _, step, width = kv_hbm.shape
     heads = width // HEAD
-    base = lax.axis_index("beam") * local
-    kept = kept_pair(parents_ref[...], base, local)
-    copies = [pltpu.make_async_copy(kv_ref.at[k], held_ref.at[r], sems.at[r]) for r, k in enumerate(kept)]
-    for copy in copies:
+    kv_sems, sems, out_sems = sems
+    small = [(parents_hbm, parents_ref), (last_hbm, last_ref), (value_hbm, value_ref)]
+    small = [pltpu.make_async_copy(a, to, sems.at[n]) for n, (a, to) in enumerate(small)]
+    copies = [pltpu.make_async_copy(kv_hbm.at[i], held_ref.at[i], kv_sems.at[i]) for i in range(local)]
+    for copy in small + copies:
         copy.start()
+    small[0].wait()
+    kept = kept_pair(parents_ref[...], lax.axis_index("beam") * local, local)
+    small[1].wait()
+    small[2].wait()
     hidden = last_ref[...].astype(jnp.float32)
     square = jnp.mean(hidden * hidden, axis=-1, keepdims=True)
     normed = hidden * lax.rsqrt(square + 1e-05)
-    score = jnp.sum(normed * value_ref[...], axis=-1, keepdims=True)
-    reward = jax.nn.sigmoid(score)
+    reward = jax.nn.sigmoid(jnp.sum(normed * value_ref[...], axis=-1, keepdims=True))
     row = lax.broadcasted_iota(jnp.int32, reward.shape, 0)
-    marks = [jnp.sum(jnp.where(row == k, reward, 0.0)) for k in kept]
+    marks = [jnp.sum(jnp.where(row == k, reward, 0.0), axis=0, keepdims=True) for k in kept]
     tile = lax.broadcasted_iota(jnp.int32, (MARK, HEAD), 0)
     tile = jnp.where(tile < MARK // 2, marks[0], marks[1]).astype(jnp.bfloat16)
-    for d in range(out_ref.shape[0]):
-        out_ref[d, KEEP * 2 * step :, :] = tile
-    for r, copy in enumerate(copies):
+    for copy in copies:
         copy.wait()
-        for s in range(2):
-            for f in range(heads):
-                piece = held_ref[r, s, :, f * HEAD : (f + 1) * HEAD]
+    sends = []
+    for f in range(heads):
+        for r, k in enumerate(kept):
+            for s in range(2):
                 start = (r * 2 + s) * step
-                for d in range(f, out_ref.shape[0], heads):
-                    out_ref[d, start : start + step, :] = piece
+                piece_ref[f, start : start + step, :] = held_ref[k, s, :, f * HEAD : (f + 1) * HEAD]
+        piece_ref[f, KEEP * 2 * step :, :] = tile
+        for d in range(f, out_ref.shape[0], heads):
+            sends.append(pltpu.make_async_copy(piece_ref.at[f], out_ref.at[d], out_sems.at[d]))
+            sends[-1].start()
+    for send in sends:
+        send.wait()
 
 
 def pick(chips, ms, item_ref, table_ref, _, *out_refs):
@@ -162,8 +170,11 @@
     return jnp.concatenate([jnp.concatenate([a, zero], axis=1), jnp.concatenate([zero, a], axis=1)], axis=0)
 
 
-def forward(sent_ref, _, out_ref):
-    out_ref[...] = sent_ref[sent_ref.shape[0] - out_ref.shape[0] :, :]
+def forward(*refs):
+    *sent_refs, _, out_ref = refs
+    rows = out_ref.shape[0] // len(sent_refs)
+    for n, sent_ref in enumerate(sent_refs):
+        out_ref[n * rows : (n + 1) * rows, :] = sent_ref[rows:, :]
 
 
 class Block:
@@ -300,18 +311,21 @@
 
 def attend_first(chips, item_ref, table_ref, q_ref, part_ref, stat_ref, own_ref, other_ref, *refs):
     out_ref, share_ref, next_q, next_part, stat_out, token_ref = refs[:6]
-    held_q, held_part, held, sems, next_sems, stat_sem, out_sems = refs[6:]
+    items, held_q, held_part, held, sems, next_sems, stat_sem, item_sem, out_sems = refs[6:]
     local = held_q.shape[0]
     chip = lax.axis_index("beam") % (2 * chips) // 2
     mine = lambda i: stage(q_ref, part_ref, 0, i, held_q, held_part, sems, chips)
     following = lambda i: stage(q_ref, part_ref, 1, i, next_q, next_part, next_sems, chips)
     stat_copy = pltpu.make_async_copy(stat_ref, stat_out, stat_sem)
     stat_copy.start()
+    item_copy = pltpu.make_async_copy(item_ref, items, item_sem)
+    item_copy.start()
     for i in range(local):
         for copy in mine(i):
             copy.start()
     token_ref[...] = jnp.zeros_like(token_ref)
-    share_rewards(item_ref, table_ref, share_ref)
+    item_copy.wait()
+    share_rewards(items, table_ref, share_ref)
 
     def ready(i, due):
         @pl.when(due)
@@ -349,9 +363,13 @@
 
 
 def attend_last(chips, stat_ref, *refs):
-    operands, (_, out_ref, held, sems) = refs[: 4 * (chips - 2)], refs[4 * (chips - 2) :]
+    *operands, other_ref, _, out_ref, held, sems = refs
+    count = other_ref.shape[0] // (chips - 2)
     chip = lax.axis_index("beam") % (2 * chips) // 2
-    works = [(*operands[4 * n : 4 * n + 4], chip ^ m) for n, m in enumerate(range(2, chips))]
+    works = [
+        (*operands[3 * n : 3 * n + 3], other_ref.at[pl.ds(n * count, count), :], chip ^ m)
+        for n, m in enumerate(range(2, chips))
+    ]
     attend_blocks(works, stat_ref, held, out_ref, sems, lambda i, due: None)
 
 
@@ -375,19 +393,30 @@
     chips = heads // 2
     vmem = pl.BlockSpec(memory_space=pltpu.VMEM)
     smem = pl.BlockSpec(memory_space=pltpu.SMEM)
+    hbm = pl.BlockSpec(memory_space=pltpu.HBM)
     bf16 = jnp.bfloat16
 
     rows = 2 * step
     in_hbm = lambda a: pltpu.with_memory_space_constraint(a, pltpu.HBM)
     in_vmem = lambda a: pltpu.with_memory_space_constraint(a, pltpu.VMEM)
+    message = KEEP * rows + MARK
     packed = pl.pallas_call(
         pack,
-        out_shape=jax.ShapeDtypeStruct((beam_count, KEEP * rows + MARK, HEAD), bf16),
-        in_specs=[vmem, pl.BlockSpec(memory_space=pl.ANY), vmem, vmem],
-        out_specs=vmem,
-        scratch_shapes=[pltpu.VMEM((KEEP, 2, step, kv_width), bf16), pltpu.SemaphoreType.DMA((KEEP,))],
+        out_shape=jax.ShapeDtypeStruct((beam_count, message, HEAD), bf16),
+        in_specs=[hbm] * 4,
+        out_specs=hbm,
+        scratch_shapes=[
+            pltpu.VMEM((1, children), jnp.int32),
+            pltpu.VMEM((local, 2, step, kv_width), bf16),
+            pltpu.VMEM(prm_last.shape, bf16),
+            pltpu.VMEM((1, value_head.shape[0]), jnp.float32),
+            pltpu.VMEM((heads, message, HEAD), bf16),
+            pltpu.SemaphoreType.DMA((local,)),
+            pltpu.SemaphoreType.DMA((3,)),
+            pltpu.SemaphoreType.DMA((beam_count,)),
+        ],
         name="pack",
-    )(parents.reshape(1, children), step_kv, prm_last, value_head.reshape(1, -1))
+    )(in_hbm(parents.reshape(1, children)), in_hbm(step_kv), in_hbm(prm_last), in_hbm(value_head.reshape(1, -1)))
     table = lax.all_to_all(packed, "beam", 0, 0)
 
     cost = lambda f, t, b: pl.CostEstimate(flops=f, transcendentals=t, bytes_accessed=b)
@@ -413,7 +442,6 @@
     item = owner * KEEP + jnp.any(earlier, axis=1).astype(jnp.int32)
     near = lax.dynamic_slice_in_dim(item, group_index // heads * (heads * local), heads * local)
     anywhere = pl.BlockSpec(memory_space=pl.ANY)
-    hbm = pl.BlockSpec(memory_space=pltpu.HBM)
 
     def picked(ms, after):
         return pl.pallas_call(
@@ -426,21 +454,20 @@
             name="pick",
         )(near, table, after)
 
-    def pass_on(piece, after):
+    def pass_on(sent, after):
         passed = pl.pallas_call(
             forward,
-            out_shape=jax.ShapeDtypeStruct((local * rows, HEAD), bf16),
-            in_specs=[vmem, anywhere],
+            out_shape=jax.ShapeDtypeStruct((len(sent) * local * rows, HEAD), bf16),
+            in_specs=[vmem] * len(sent) + [anywhere],
             out_specs=vmem,
             compiler_params=params(2),
             cost_estimate=small,
             name="forward",
-        )(piece, after)
+        )(*sent, after)
         return swap(passed, 1)
 
     far = tuple(range(2, chips))
-    pieces = picked(far, in_hbm(stat))
-    pieces = picked((0, 1), pieces[0]) + pieces
+    pieces = picked(range(chips), in_hbm(stat))
     own = [pieces[0]] + [swap(pieces[m], 2 * m) for m in range(1, chips)]
     wide = width // chips
     result = jax.ShapeDtypeStruct((local, new, width), bf16)
@@ -458,13 +485,15 @@
             pltpu.VMEM(stat.shape, bf16),
             token,
         ],
-        in_specs=[smem, vmem, hbm, hbm, hbm, vmem, vmem],
+        in_specs=[hbm, vmem, hbm, hbm, hbm, vmem, vmem],
         out_specs=[hbm] + [vmem] * 5,
-        scratch_shapes=[later] * 2 + [held(1), many((2, local)), many((2, local)), many, many((1, local))],
+        scratch_shapes=[pltpu.SMEM((children,), jnp.int32)]
+        + [later] * 2
+        + [held(1), many((2, local)), many((2, local)), many, many, many((1, local))],
         compiler_params=params(16),
         cost_estimate=small,
         name="attend_first",
-    )(item, table, in_hbm(queries), in_hbm(part), in_hbm(stat), own[0], pass_on(own[0], near))
+    )(in_hbm(item), table, in_hbm(queries), in_hbm(part), in_hbm(stat), own[0], pass_on(own[:1], near))
     attended, done, *staged = pl.pallas_call(
         functools.partial(attend_second, chips),
         out_shape=[result, token] + [later] * (2 * len(far)),
@@ -482,12 +511,13 @@
         in_vmem(next_part),
         in_vmem(stat_held),
         own[1],
-        pass_on(own[1], done),
+        pass_on(own[1:2], done),
         attended,
     )
     operands = []
     for n, m in enumerate(far):
-        operands += [in_vmem(staged[2 * n]), in_vmem(staged[2 * n + 1]), own[m], pass_on(own[m], done)]
+        operands += [in_vmem(staged[2 * n]), in_vmem(staged[2 * n + 1]), own[m]]
+    operands.append(pass_on(own[2:], done))
     attended = pl.pallas_call(
         functools.partial(attend_last, chips),
         out_shape=result,

time: 107 us -> 105 us (0.981)
  Pallas kernels: 91.9 us -> 89.4 us
    pallas_call x1, Pallas kernels: 16.7 us -> 15.5 us  [body(): pl.pallas_call(functools.partial(attend_first, chips), out_shape=[result,...]
    pallas_call x5 -> x4, Pallas kernels: 3.14 us -> 2.51 us  [the longest x1 2.47 us: body(): pl.pallas_call(pack, out_shape=jax.ShapeDtypeStruct((beam_count, message,...]
    ppermute x7 -> x6, starting transfers between devices: 4.45 us -> 4.02 us  [swap(): return lax.ppermute(a, 'beam', [(i, i ^ distance) for i in range(count)])]
    ppermute x7 -> x6, waiting for transfers between devices: 2.31 us -> 2.73 us  [swap(): return lax.ppermute(a, 'beam', [(i, i ^ distance) for i in range(count)])]
  transfers between devices with their start and end apart: 8 -> 7, of which waited for: 3 -> 2; matrix products, arithmetic and copies ran while one was open for 0% -> 0% of each run, Pallas kernels for 59% -> 59%
where the time goes in v4:
time: 105 us
  Pallas kernels  89.4 us (85%)
  starting transfers between devices  11.4 us (11%)
  waiting for transfers between devices  2.73 us (3%)
    pallas_call x1, Pallas kernels, body(): pl.pallas_call(attend_new, grid=(local,), out_shape=[jax.ShapeDtypeStruct...  33.6 us
    pallas_call x1, Pallas kernels, body(): pl.pallas_call(functools.partial(attend_last, chips), out_shape=result, i...  24.1 us
    pallas_call x1, Pallas kernels, body(): pl.pallas_call(functools.partial(attend_first, chips), out_shape=[result,...  15.5 us
    pallas_call x1, Pallas kernels, body(): pl.pallas_call(functools.partial(attend_second, chips), out_shape=[result...  13 us
    all_to_all x1, starting transfers between devices, body(): table = lax.all_to_all(packed, 'beam', 0, 0)  7.4 us
    ppermute x6, starting transfers between devices, swap(): return lax.ppermute(a, 'beam', [(i, i ^ distance) for i in range(count)])  4.02 us
    ppermute x6, waiting for transfers between devices, swap(): return lax.ppermute(a, 'beam', [(i, i ^ distance) for i in range(count)])  2.73 us
    pallas_call x1, Pallas kernels, body(): pl.pallas_call(pack, out_shape=jax.ShapeDtypeStruct((beam_count, message,...  2.47 us
  transfers between devices with their start and end apart: 7, of which 2 were waited for; matrix products, arithmetic and copies ran while one was open for 0% of the time, Pallas kernels for 59%

profile of v4, /device:TPU:0, one launch (start us, length us, event | category | flops | bytes accessed | tf_op | source)
XLA Modules:
  0.0 104.7 jit_solution(454035248483334964)
XLA Ops:
  0.6 0.0 copy-start
  0.6 2.5 %pack.1 = bf16[16,272,128]{2,1,0:T(8,128)(2,1)} custom-call(s32[1,64]{1,0:T(1,128)} %bitcast.4, bf16[4,2,64,1024]{3,2,1,0:T(8,128)(2,1)} %kv_hbm.1, bf16[4,4096]{1,0:T(4,128)(2,1)} %last_hbm.1, f32[1,4096]{1,0:T(1,128)} %bitcast.3), custom_call_target="tpu_custom_call" | custom-call | tf_op jit(solution)/shard_map/pack/pallas_call | solution.py:403
  3.1 7.4 %all-to-all-start = ((bf16[16,272,128]{2,1,0:T(8,128)(2,1)}), bf16[16,272,128]{2,1,0:T(8,128)(2,1)S(1)}, u32[]{:S(2)}, u32[]{:S(2)}) async-start(bf16[16,272,128]{2,1,0:T(8,128)(2,1)} %pack.1), calls=%async_computation | async-start | bytes 2228224 | tf_op jit(solution)/shard_map/all_to_all | solution.py:420
  10.5 0.0 copy-done
  10.6 0.2 and_reduce_fusion
  10.8 0.0 copy-start.1
  10.8 0.1 dynamic_slice.3.item_ref.refs_1_
  10.9 33.6 %attend_new.1 = (bf16[4,256,4096]{2,1,0:T(8,128)(2,1)}, bf16[4,256,128]{2,1,0:T(8,128)(2,1)}) custom-call(bf16[4,256,4096]{2,1,0:T(8,128)(2,1)} %q_ref.5, bf16[4,256,1024]{2,1,0:T(8,128)(2,1)} %k_ref.1, bf16[4,256,1024]{2,1,0:T(8,128)(2,1)} %v_ref.1), custom_call_target="tpu_custom_call" | custom-call | flops 4294967296 | bytes 25165824 | tf_op jit(solution)/shard_map/attend_new/pallas_call | solution.py:425
  44.4 0.0 copy-done.1
  44.4 0.0 all-to-all-done.table_ref
  44.4 0.8 pick.1
  45.2 2.0 %collective-permute-start.1 = (bf16[1024,128]{1,0:T(8,128)(2,1)S(1)}, bf16[1024,128]{1,0:T(8,128)(2,1)S(1)}, u32[]{:S(2)}, u32[]{:S(2)}) collective-permute-start(bf16[1024,128]{1,0:T(8,128)(2,1)S(1)} %get-tuple-element.26), channel_id=1, source_target_pairs={{0,2},{1,3},{2,0},{3,1},{4,6},{5,7},{6,4},{7,5},{8,10},{9,11},{10,... | collective-permute-start | bytes 786440 | tf_op jit(solution)/shard_map/ppermute | solution.py:382
  47.2 0.1 collective-permute-start
  47.3 1.5 %collective-permute-start.3 = (bf16[1024,128]{1,0:T(8,128)(2,1)S(1)}, bf16[1024,128]{1,0:T(8,128)(2,1)S(1)}, u32[]{:S(2)}, u32[]{:S(2)}) collective-permute-start(bf16[1024,128]{1,0:T(8,128)(2,1)S(1)} %get-tuple-element.31), channel_id=1, source_target_pairs={{0,4},{1,5},{2,6},{3,7},{4,0},{5,1},{6,2},{7,3},{8,12},{9,13},{10,... | collective-permute-start | bytes 786440 | tf_op jit(solution)/shard_map/ppermute | solution.py:382
  48.8 0.1 collective-permute-start.4
  49.0 0.0 collective-permute-done.other_ref
  49.0 15.5 %attend_first.1 = (bf16[4,256,4096]{2,1,0:T(8,128)(2,1)}, f32[1,4]{1,0:T(1,128)}, bf16[4,256,1024]{2,1,0:T(8,128)(2,1)S(1)}, bf16[4,256,1024]{2,1,0:T(8,128)(2,1...) custom-call(s32[64]{0:T(128)} %copy-done.1, bf16[16,272,128]{2,1,0:T(8,128)(2,1)S(1)} %all-to-all-done.table_ref, ...), custom_call_target="tpu_custom_call" | custom-call | flops 1024 | bytes 1024 | tf_op jit(solution)/shard_map/attend_first/pallas_call | solution.py:478
  64.5 0.0 collective-permute-done.1.refs_0_.own_ref
  64.5 0.1 collective-permute-start.2
  64.6 1.3 %collective-permute-done.2.other_ref = bf16[512,128]{1,0:T(8,128)(2,1)S(1)} collective-permute-done((bf16[512,128]{1,0:T(8,128)(2,1)S(1)}, bf16[512,128]{1,0:T(8,128)(2,1)S(1)}, u32[]{:S(2)}, u32[]{:S(2)}) %collective-permute-start.2) | collective-permute-done | bytes 131104 | tf_op jit(solution)/shard_map/ppermute | solution.py:382
  65.9 13.0 %attend_second.1 = (bf16[4,256,4096]{2,1,0:T(8,128)(2,1)}, f32[8,128]{1,0:T(8,128)S(1)}, bf16[4,256,1024]{2,1,0:T(8,128)(2,1)S(1)}, bf16[4,256,1024]{2,1,0:T(8,1...) custom-call(bf16[4,256,4096]{2,1,0:T(8,128)(2,1)} %q_ref.5, ...), custom_call_target="tpu_custom_call", output_to_operand_aliasing={{0}: (7, {})} | custom-call | flops 1024 | bytes 1024 | tf_op jit(solution)/shard_map/attend_second/pallas_call | solution.py:497
  78.9 0.0 collective-permute-done.3.refs_0_.refs_2_
  78.9 0.0 collective-permute-done.4.refs_1_.refs_5_
  79.0 0.2 collective-permute-start.5
  79.2 1.4 %collective-permute-done.5.refs_6_ = bf16[1024,128]{1,0:T(8,128)(2,1)S(1)} collective-permute-done((bf16[1024,128]{1,0:T(8,128)(2,1)S(1)}, bf16[1024,128]{1,0:T(8,128)(2,1)S(1)}, u32[]{:S(2)}, u32[]{:S(2)}) %collective-permute-start.5) | collective-permute-done | bytes 262176 | tf_op jit(solution)/shard_map/ppermute | solution.py:382
  80.6 24.1 %attend_last.1 = bf16[4,256,4096]{2,1,0:T(8,128)(2,1)} custom-call(bf16[4,256,128]{2,1,0:T(8,128)(2,1)S(1)} %get-tuple-element.23.stat_ref, bf16[4,256,1024]{2,1,0:T(8,128)(2,1)S(1)} %get-tuple-element.29.refs_0_, bf16[4,256,1024]{2,1,0:T(8,128)(2,1)S(1)} %get-tuple-element.30.refs_1_, ...), custom_call_target="tpu_custom_call", output_to_operand_aliasing={{}: (8, {})} | custom-call | flops 1024 | bytes 1024 | tf_op jit(solution)/shard_map/attend_last/pallas_call | solution.py:521
  (5 shorter events, 0.1 us)
Async XLA Ops:
  0.6 9.9 %copy-start = (s32[64]{0:T(128)S(1)}, s32[64]{0:T(128)}, u32[]{:S(2)}) copy-start(s32[64]{0:T(128)} %param.13) | copy-start | bytes 772
  3.1 41.3 %all-to-all-start = ((bf16[16,272,128]{2,1,0:T(8,128)(2,1)}), bf16[16,272,128]{2,1,0:T(8,128)(2,1)S(1)}, u32[]{:S(2)}, u32[]{:S(2)}) async-start(bf16[16,272,128]{2,1,0:T(8,128)(2,1)} %pack.1), calls=%async_computation | async-start | bytes 2228224 | tf_op jit(solution)/shard_map/all_to_all | solution.py:420
  10.8 33.7 %copy-start.1 = (s32[64]{0:T(128)}, s32[64]{0:T(128)S(1)}, u32[]{:S(2)}) copy-start(s32[64]{0:T(128)S(1)} %convert_add_fusion.item_ref) | copy-start | bytes 772
  45.2 19.3 %collective-permute-start.1 = (bf16[1024,128]{1,0:T(8,128)(2,1)S(1)}, bf16[1024,128]{1,0:T(8,128)(2,1)S(1)}, u32[]{:S(2)}, u32[]{:S(2)}) collective-permute-start(bf16[1024,128]{1,0:T(8,128)(2,1)S(1)} %get-tuple-element.26), channel_id=1, source_target_pairs={{0,2},{1,3},{2,0},{3,1},{4,6},{5,7},{6,4},{7,5},{8,10},{9,11},{10,... | collective-permute-start | bytes 786440 | tf_op jit(solution)/shard_map/ppermute | solution.py:382
  47.2 1.8 %collective-permute-start = (bf16[512,128]{1,0:T(8,128)(2,1)S(1)}, bf16[512,128]{1,0:T(8,128)(2,1)S(1)}, u32[]{:S(2)}, u32[]{:S(2)}) collective-permute-start(bf16[512,128]{1,0:T(8,128)(2,1)S(1)} %forward.3), channel_id=1, source_target_pairs={{0,1},{1,0},{2,3},{3,2},{4,5},{5,4},{6,7},{7,6},{8,9},{9,8},{10,11... | collective-permute-start | bytes 393224 | tf_op jit(solution)/shard_map/ppermute | solution.py:382
  47.3 31.6 %collective-permute-start.3 = (bf16[1024,128]{1,0:T(8,128)(2,1)S(1)}, bf16[1024,128]{1,0:T(8,128)(2,1)S(1)}, u32[]{:S(2)}, u32[]{:S(2)}) collective-permute-start(bf16[1024,128]{1,0:T(8,128)(2,1)S(1)} %get-tuple-element.31), channel_id=1, source_target_pairs={{0,4},{1,5},{2,6},{3,7},{4,0},{5,1},{6,2},{7,3},{8,12},{9,13},{10,... | collective-permute-start | bytes 786440 | tf_op jit(solution)/shard_map/ppermute | solution.py:382
  48.8 30.1 %collective-permute-start.4 = (bf16[1024,128]{1,0:T(8,128)(2,1)S(1)}, bf16[1024,128]{1,0:T(8,128)(2,1)S(1)}, u32[]{:S(2)}, u32[]{:S(2)}) collective-permute-start(bf16[1024,128]{1,0:T(8,128)(2,1)S(1)} %get-tuple-element.34), channel_id=1, source_target_pairs={{0,6},{1,7},{2,4},{3,5},{4,2},{5,3},{6,0},{7,1},{8,14},{9,15},{10,... | collective-permute-start | bytes 786440 | tf_op jit(solution)/shard_map/ppermute | solution.py:382
  64.5 1.4 %collective-permute-start.2 = (bf16[512,128]{1,0:T(8,128)(2,1)S(1)}, bf16[512,128]{1,0:T(8,128)(2,1)S(1)}, u32[]{:S(2)}, u32[]{:S(2)}) collective-permute-start(bf16[512,128]{1,0:T(8,128)(2,1)S(1)} %forward.4), channel_id=1, source_target_pairs={{0,1},{1,0},{2,3},{3,2},{4,5},{5,4},{6,7},{7,6},{8,9},{9,8},{10,11... | collective-permute-start | bytes 393224 | tf_op jit(solution)/shard_map/ppermute | solution.py:382
  79.0 1.6 %collective-permute-start.5 = (bf16[1024,128]{1,0:T(8,128)(2,1)S(1)}, bf16[1024,128]{1,0:T(8,128)(2,1)S(1)}, u32[]{:S(2)}, u32[]{:S(2)}) collective-permute-start(bf16[1024,128]{1,0:T(8,128)(2,1)S(1)} %forward.5), channel_id=1, source_target_pairs={{0,1},{1,0},{2,3},{3,2},{4,5},{5,4},{6,7},{7,6},{8,9},{9,8},{10,11... | collective-permute-start | bytes 786440 | tf_op jit(solution)/shard_map/ppermute | solution.py:382

commit v5 on v4

--- a/solution.py
+++ b/solution.py
@@ -12,6 +12,8 @@
 KEEP = 2
 MARK = 16
 LIMIT = 100.0
+SECOND = 1
+LAST = (2, 3)
 LOG2E = math.log2(math.e)
 MIB = 1 << 20
 NT = (((1,), (1,)), ((), ()))
@@ -250,7 +252,7 @@
         self.store(part * rest + mm(weights, values), mm(weights, ones) + mm(sums, spread) * rest)
 
 
-def attend_blocks(works, stat_ref, held_ref, out_ref, sems, ready):
+def attend_blocks(works, stat_ref, held_ref, out_ref, sems, ready=None, rolled=False):
     local, _, width = works[0][0].shape
     count = out_ref.shape[2] // HEAD
 
@@ -263,18 +265,6 @@
         return pltpu.make_async_copy(held_ref.at[n, i], out_ref.at[i, :, lanes], sems.at[n, i])
 
     lane = lax.broadcasted_iota(jnp.int32, stat_ref.shape[1:], 1)
-
-    def work(n, i, carry):
-        most, weights = carry
-        later, top = block(n, i, 1).weigh()
-        block(n, i, 0).finish(weights)
-        most = jnp.maximum(most, top)
-        following = jnp.minimum(i + 1, local - 1)
-        ready(following, i + 1 < local)
-        weights, top = block(n, following, 0).weigh()
-        block(n, i, 1).finish(later)
-        send(n, i).start()
-        return jnp.maximum(most, top), weights
 
     def moved(i, most):
         tops = jnp.where(lane >= 2 * count, stat_ref[i].astype(jnp.float32), 0.0)
@@ -282,16 +272,34 @@
         return jnp.maximum(most, jnp.max(tops.reshape(-1, 8, HEAD), axis=0))
 
     most = jnp.full((8, HEAD), -jnp.inf, jnp.float32)
-    ready(0, True)
-    for n in range(len(works)):
-        weights, top = block(n, 0, 0).weigh()
-        most, _ = lax.fori_loop(0, local, functools.partial(work, n), (jnp.maximum(most, top), weights))
-    most = lax.fori_loop(0, local, moved, most)
+
+    def run(order, most):
+        held = None
+        for t in range(len(order) + 1):
+            last, held = held, None
+            if t < len(order):
+                n, i, f = order[t]
+                if ready is not None and f == 0:
+                    ready(i)
+                held, top = block(n, i, f).weigh()
+                most = jnp.maximum(most, top)
+            if t > 0:
+                n, i, f = order[t - 1]
+                block(n, i, f).finish(last)
+                if f == 1:
+                    send(n, i).start()
+        return most
+
+    if rolled:
+        most = lax.fori_loop(0, local, lambda i, most: run([(0, i, 0), (0, i, 1)], most), most)
+    else:
+        most = run([(n, i, f) for n in range(len(works)) for i in range(local) for f in range(2)], most)
+    largest = jnp.max(lax.fori_loop(0, local, moved, most))
     every = [(n, i) for n in range(len(works)) for i in range(local)]
     for n, i in every:
         send(n, i).wait()
 
-    @pl.when(jnp.max(most) > LIMIT)
+    @pl.when(largest > LIMIT)
     def _():
         for n in range(len(works)):
             lax.fori_loop(0, 2 * local, lambda t, c: (block(n, t // 2, t % 2).shifted(), c)[1], 0)
@@ -315,7 +323,7 @@
     local = held_q.shape[0]
     chip = lax.axis_index("beam") % (2 * chips) // 2
     mine = lambda i: stage(q_ref, part_ref, 0, i, held_q, held_part, sems, chips)
-    following = lambda i: stage(q_ref, part_ref, 1, i, next_q, next_part, next_sems, chips)
+    following = lambda i: stage(q_ref, part_ref, SECOND, i, next_q, next_part, next_sems, chips)
     stat_copy = pltpu.make_async_copy(stat_ref, stat_out, stat_sem)
     stat_copy.start()
     item_copy = pltpu.make_async_copy(item_ref, items, item_sem)
@@ -327,13 +335,11 @@
     item_copy.wait()
     share_rewards(items, table_ref, share_ref)
 
-    def ready(i, due):
-        @pl.when(due)
-        def _():
-            for copy in mine(i):
-                copy.wait()
-            for copy in following(i):
-                copy.start()
+    def ready(i):
+        for copy in mine(i):
+            copy.wait()
+        for copy in following(i):
+            copy.start()
 
     stat_copy.wait()
     attend_blocks([(held_q, held_part, own_ref, other_ref, chip)], stat_out, held, out_ref, out_sems, ready)
@@ -343,34 +349,34 @@
 
 
 def attend_second(chips, q_ref, part_ref, next_q, next_part, stat_ref, own_ref, other_ref, _, *refs):
-    out_ref, token_ref, *later = refs[: 2 + 2 * (chips - 2)]
-    held, sems, next_sems = refs[2 + 2 * (chips - 2) :]
+    out_ref, token_ref, *later = refs[: 2 + 2 * len(LAST)]
+    held, sems, next_sems = refs[2 + 2 * len(LAST) :]
     local = held.shape[1]
     chip = lax.axis_index("beam") % (2 * chips) // 2
 
     def staged():
-        for n, m in enumerate(range(2, chips)):
+        for n, m in enumerate(LAST):
             for i in range(local):
                 yield from stage(q_ref, part_ref, m, i, later[2 * n], later[2 * n + 1], next_sems.at[n], chips)
 
     for copy in staged():
         copy.start()
     token_ref[...] = jnp.zeros_like(token_ref)
-    works = [(next_q, next_part, own_ref, other_ref, chip ^ 1)]
-    attend_blocks(works, stat_ref, held, out_ref, sems, lambda i, due: None)
+    works = [(next_q, next_part, own_ref, other_ref, chip ^ SECOND)]
+    attend_blocks(works, stat_ref, held, out_ref, sems, rolled=True)
     for copy in staged():
         copy.wait()
 
 
 def attend_last(chips, stat_ref, *refs):
     *operands, other_ref, _, out_ref, held, sems = refs
-    count = other_ref.shape[0] // (chips - 2)
+    count = other_ref.shape[0] // len(LAST)
     chip = lax.axis_index("beam") % (2 * chips) // 2
     works = [
         (*operands[3 * n : 3 * n + 3], other_ref.at[pl.ds(n * count, count), :], chip ^ m)
-        for n, m in enumerate(range(2, chips))
+        for n, m in enumerate(LAST)
     ]
-    attend_blocks(works, stat_ref, held, out_ref, sems, lambda i, due: None)
+    attend_blocks(works, stat_ref, held, out_ref, sems)
 
 
 def params(mib):
@@ -466,7 +472,6 @@
         )(*sent, after)
         return swap(passed, 1)
 
-    far = tuple(range(2, chips))
     pieces = picked(range(chips), in_hbm(stat))
     own = [pieces[0]] + [swap(pieces[m], 2 * m) for m in range(1, chips)]
     wide = width // chips
@@ -496,10 +501,10 @@
     )(in_hbm(item), table, in_hbm(queries), in_hbm(part), in_hbm(stat), own[0], pass_on(own[:1], near))
     attended, done, *staged = pl.pallas_call(
         functools.partial(attend_second, chips),
-        out_shape=[result, token] + [later] * (2 * len(far)),
+        out_shape=[result, token] + [later] * (2 * len(LAST)),
         in_specs=[hbm, hbm] + [vmem] * 5 + [hbm],
-        out_specs=[hbm, vmem] + [vmem] * (2 * len(far)),
-        scratch_shapes=[held(1), many((1, local)), many((len(far), 2, local))],
+        out_specs=[hbm, vmem] + [vmem] * (2 * len(LAST)),
+        scratch_shapes=[held(1), many((1, local)), many((len(LAST), 2, local))],
         input_output_aliases={7: 0},
         compiler_params=params(12),
         cost_estimate=small,
@@ -510,20 +515,20 @@
         in_vmem(next_q),
         in_vmem(next_part),
         in_vmem(stat_held),
-        own[1],
-        pass_on(own[1:2], done),
+        own[SECOND],
+        pass_on([own[SECOND]], done),
         attended,
     )
     operands = []
-    for n, m in enumerate(far):
+    for n, m in enumerate(LAST):
         operands += [in_vmem(staged[2 * n]), in_vmem(staged[2 * n + 1]), own[m]]
-    operands.append(pass_on(own[2:], done))
+    operands.append(pass_on([own[m] for m in LAST], done))
     attended = pl.pallas_call(
         functools.partial(attend_last, chips),
         out_shape=result,
         in_specs=[vmem] * (1 + len(operands)) + [hbm],
         out_specs=hbm,
-        scratch_shapes=[held(len(far)), many((len(far), local))],
+        scratch_shapes=[held(len(LAST)), many((len(LAST), local))],
         input_output_aliases={1 + len(operands): 0},
         compiler_params=params(12),
         cost_estimate=small,

time: 105 us -> 103 us (0.981)
  Pallas kernels: 89.4 us -> 87.8 us
  transfers between devices with their start and end apart: 7 -> 7, of which waited for: 2 -> 2; matrix products, arithmetic and copies ran while one was open for 0% -> 0% of each run, Pallas kernels for 59% -> 60%
where the time goes in v5:
time: 103 us
  Pallas kernels  87.8 us (85%)
  starting transfers between devices  11.4 us (11%)
  waiting for transfers between devices  2.74 us (3%)
    pallas_call x1, Pallas kernels, body(): pl.pallas_call(attend_new, grid=(local,), out_shape=[jax.ShapeDtypeStruct...  33.6 us
    pallas_call x1, Pallas kernels, body(): pl.pallas_call(functools.partial(attend_last, chips), out_shape=result, i...  23.1 us
    pallas_call x1, Pallas kernels, body(): pl.pallas_call(functools.partial(attend_first, chips), out_shape=[result,...  14.7 us
    pallas_call x1, Pallas kernels, body(): pl.pallas_call(functools.partial(attend_second, chips), out_shape=[result...  13.1 us
    all_to_all x1, starting transfers between devices, body(): table = lax.all_to_all(packed, 'beam', 0, 0)  7.4 us
    ppermute x6, starting transfers between devices, swap(): return lax.ppermute(a, 'beam', [(i, i ^ distance) for i in range(count)])  4.01 us
    ppermute x6, waiting for transfers between devices, swap(): return lax.ppermute(a, 'beam', [(i, i ^ distance) for i in range(count)])  2.74 us
    pallas_call x1, Pallas kernels, body(): pl.pallas_call(pack, out_shape=jax.ShapeDtypeStruct((beam_count, message,...  2.47 us
  transfers between devices with their start and end apart: 7, of which 2 were waited for; matrix products, arithmetic and copies ran while one was open for 0% of the time, Pallas kernels for 60%

profile of v5, /device:TPU:0, one launch (start us, length us, event | category | flops | bytes accessed | tf_op | source)
XLA Modules:
  0.0 103.2 jit_solution(11737364081520714152)
XLA Ops:
  0.6 0.0 copy-start
  0.6 2.5 %pack.1 = bf16[16,272,128]{2,1,0:T(8,128)(2,1)} custom-call(s32[1,64]{1,0:T(1,128)} %bitcast.4, bf16[4,2,64,1024]{3,2,1,0:T(8,128)(2,1)} %kv_hbm.1, bf16[4,4096]{1,0:T(4,128)(2,1)} %last_hbm.1, f32[1,4096]{1,0:T(1,128)} %bitcast.3), custom_call_target="tpu_custom_call" | custom-call | tf_op jit(solution)/shard_map/pack/pallas_call | solution.py:409
  3.1 7.4 %all-to-all-start = ((bf16[16,272,128]{2,1,0:T(8,128)(2,1)}), bf16[16,272,128]{2,1,0:T(8,128)(2,1)S(1)}, u32[]{:S(2)}, u32[]{:S(2)}) async-start(bf16[16,272,128]{2,1,0:T(8,128)(2,1)} %pack.1), calls=%async_computation | async-start | bytes 2228224 | tf_op jit(solution)/shard_map/all_to_all | solution.py:426
  10.5 0.0 copy-done
  10.6 0.2 and_reduce_fusion
  10.8 0.0 copy-start.1
  10.8 0.1 dynamic_slice.3.item_ref.refs_1_
  10.9 33.6 %attend_new.1 = (bf16[4,256,4096]{2,1,0:T(8,128)(2,1)}, bf16[4,256,128]{2,1,0:T(8,128)(2,1)}) custom-call(bf16[4,256,4096]{2,1,0:T(8,128)(2,1)} %q_ref.5, bf16[4,256,1024]{2,1,0:T(8,128)(2,1)} %k_ref.1, bf16[4,256,1024]{2,1,0:T(8,128)(2,1)} %v_ref.1), custom_call_target="tpu_custom_call" | custom-call | flops 4294967296 | bytes 25165824 | tf_op jit(solution)/shard_map/attend_new/pallas_call | solution.py:431
  44.4 0.0 copy-done.1
  44.4 0.0 all-to-all-done.table_ref
  44.4 0.8 pick.1
  45.2 2.0 %collective-permute-start.1 = (bf16[1024,128]{1,0:T(8,128)(2,1)S(1)}, bf16[1024,128]{1,0:T(8,128)(2,1)S(1)}, u32[]{:S(2)}, u32[]{:S(2)}) collective-permute-start(bf16[1024,128]{1,0:T(8,128)(2,1)S(1)} %get-tuple-element.26), channel_id=1, source_target_pairs={{0,2},{1,3},{2,0},{3,1},{4,6},{5,7},{6,4},{7,5},{8,10},{9,11},{10,... | collective-permute-start | bytes 786440 | tf_op jit(solution)/shard_map/ppermute | solution.py:388
  47.2 0.1 collective-permute-start
  47.3 1.5 %collective-permute-start.3 = (bf16[1024,128]{1,0:T(8,128)(2,1)S(1)}, bf16[1024,128]{1,0:T(8,128)(2,1)S(1)}, u32[]{:S(2)}, u32[]{:S(2)}) collective-permute-start(bf16[1024,128]{1,0:T(8,128)(2,1)S(1)} %get-tuple-element.31), channel_id=1, source_target_pairs={{0,4},{1,5},{2,6},{3,7},{4,0},{5,1},{6,2},{7,3},{8,12},{9,13},{10,... | collective-permute-start | bytes 786440 | tf_op jit(solution)/shard_map/ppermute | solution.py:388
  48.8 0.2 collective-permute-start.4
  49.0 0.0 collective-permute-done.other_ref
  49.0 14.7 %attend_first.1 = (bf16[4,256,4096]{2,1,0:T(8,128)(2,1)}, f32[1,4]{1,0:T(1,128)}, bf16[4,256,1024]{2,1,0:T(8,128)(2,1)S(1)}, bf16[4,256,1024]{2,1,0:T(8,128)(2,1...) custom-call(s32[64]{0:T(128)} %copy-done.1, bf16[16,272,128]{2,1,0:T(8,128)(2,1)S(1)} %all-to-all-done.table_ref, ...), custom_call_target="tpu_custom_call" | custom-call | flops 1024 | bytes 1024 | tf_op jit(solution)/shard_map/attend_first/pallas_call | solution.py:483
  63.7 0.0 collective-permute-done.1.refs_0_.own_ref
  63.8 0.1 collective-permute-start.2
  63.8 1.3 %collective-permute-done.2.other_ref = bf16[512,128]{1,0:T(8,128)(2,1)S(1)} collective-permute-done((bf16[512,128]{1,0:T(8,128)(2,1)S(1)}, bf16[512,128]{1,0:T(8,128)(2,1)S(1)}, u32[]{:S(2)}, u32[]{:S(2)}) %collective-permute-start.2) | collective-permute-done | bytes 131104 | tf_op jit(solution)/shard_map/ppermute | solution.py:388
  65.2 13.1 %attend_second.1 = (bf16[4,256,4096]{2,1,0:T(8,128)(2,1)}, f32[8,128]{1,0:T(8,128)S(1)}, bf16[4,256,1024]{2,1,0:T(8,128)(2,1)S(1)}, bf16[4,256,1024]{2,1,0:T(8,1...) custom-call(bf16[4,256,4096]{2,1,0:T(8,128)(2,1)} %q_ref.5, ...), custom_call_target="tpu_custom_call", output_to_operand_aliasing={{0}: (7, {})} | custom-call | flops 1024 | bytes 1024 | tf_op jit(solution)/shard_map/attend_second/pallas_call | solution.py:502
  78.3 0.0 collective-permute-done.3.refs_0_.refs_2_
  78.3 0.0 collective-permute-done.4.refs_1_.refs_5_
  78.3 0.2 collective-permute-start.5
  78.5 1.4 %collective-permute-done.5.refs_6_ = bf16[1024,128]{1,0:T(8,128)(2,1)S(1)} collective-permute-done((bf16[1024,128]{1,0:T(8,128)(2,1)S(1)}, bf16[1024,128]{1,0:T(8,128)(2,1)S(1)}, u32[]{:S(2)}, u32[]{:S(2)}) %collective-permute-start.5) | collective-permute-done | bytes 262176 | tf_op jit(solution)/shard_map/ppermute | solution.py:388
  79.9 23.1 %attend_last.1 = bf16[4,256,4096]{2,1,0:T(8,128)(2,1)} custom-call(bf16[4,256,128]{2,1,0:T(8,128)(2,1)S(1)} %get-tuple-element.23.stat_ref, bf16[4,256,1024]{2,1,0:T(8,128)(2,1)S(1)} %get-tuple-element.29.refs_0_, bf16[4,256,1024]{2,1,0:T(8,128)(2,1)S(1)} %get-tuple-element.30.refs_1_, ...), custom_call_target="tpu_custom_call", output_to_operand_aliasing={{}: (8, {})} | custom-call | flops 1024 | bytes 1024 | tf_op jit(solution)/shard_map/attend_last/pallas_call | solution.py:526
  (5 shorter events, 0.1 us)
Async XLA Ops:
  0.6 9.9 %copy-start = (s32[64]{0:T(128)S(1)}, s32[64]{0:T(128)}, u32[]{:S(2)}) copy-start(s32[64]{0:T(128)} %param.13) | copy-start | bytes 772
  3.1 41.3 %all-to-all-start = ((bf16[16,272,128]{2,1,0:T(8,128)(2,1)}), bf16[16,272,128]{2,1,0:T(8,128)(2,1)S(1)}, u32[]{:S(2)}, u32[]{:S(2)}) async-start(bf16[16,272,128]{2,1,0:T(8,128)(2,1)} %pack.1), calls=%async_computation | async-start | bytes 2228224 | tf_op jit(solution)/shard_map/all_to_all | solution.py:426
  10.8 33.7 %copy-start.1 = (s32[64]{0:T(128)}, s32[64]{0:T(128)S(1)}, u32[]{:S(2)}) copy-start(s32[64]{0:T(128)S(1)} %convert_add_fusion.item_ref) | copy-start | bytes 772
  45.2 18.5 %collective-permute-start.1 = (bf16[1024,128]{1,0:T(8,128)(2,1)S(1)}, bf16[1024,128]{1,0:T(8,128)(2,1)S(1)}, u32[]{:S(2)}, u32[]{:S(2)}) collective-permute-start(bf16[1024,128]{1,0:T(8,128)(2,1)S(1)} %get-tuple-element.26), channel_id=1, source_target_pairs={{0,2},{1,3},{2,0},{3,1},{4,6},{5,7},{6,4},{7,5},{8,10},{9,11},{10,... | collective-permute-start | bytes 786440 | tf_op jit(solution)/shard_map/ppermute | solution.py:388
  47.2 1.8 %collective-permute-start = (bf16[512,128]{1,0:T(8,128)(2,1)S(1)}, bf16[512,128]{1,0:T(8,128)(2,1)S(1)}, u32[]{:S(2)}, u32[]{:S(2)}) collective-permute-start(bf16[512,128]{1,0:T(8,128)(2,1)S(1)} %forward.3), channel_id=1, source_target_pairs={{0,1},{1,0},{2,3},{3,2},{4,5},{5,4},{6,7},{7,6},{8,9},{9,8},{10,11... | collective-permute-start | bytes 393224 | tf_op jit(solution)/shard_map/ppermute | solution.py:388
  47.3 31.0 %collective-permute-start.3 = (bf16[1024,128]{1,0:T(8,128)(2,1)S(1)}, bf16[1024,128]{1,0:T(8,128)(2,1)S(1)}, u32[]{:S(2)}, u32[]{:S(2)}) collective-permute-start(bf16[1024,128]{1,0:T(8,128)(2,1)S(1)} %get-tuple-element.31), channel_id=1, source_target_pairs={{0,4},{1,5},{2,6},{3,7},{4,0},{5,1},{6,2},{7,3},{8,12},{9,13},{10,... | collective-permute-start | bytes 786440 | tf_op jit(solution)/shard_map/ppermute | solution.py:388
  48.8 29.5 %collective-permute-start.4 = (bf16[1024,128]{1,0:T(8,128)(2,1)S(1)}, bf16[1024,128]{1,0:T(8,128)(2,1)S(1)}, u32[]{:S(2)}, u32[]{:S(2)}) collective-permute-start(bf16[1024,128]{1,0:T(8,128)(2,1)S(1)} %get-tuple-element.34), channel_id=1, source_target_pairs={{0,6},{1,7},{2,4},{3,5},{4,2},{5,3},{6,0},{7,1},{8,14},{9,15},{10,... | collective-permute-start | bytes 786440 | tf_op jit(solution)/shard_map/ppermute | solution.py:388
  63.8 1.4 %collective-permute-start.2 = (bf16[512,128]{1,0:T(8,128)(2,1)S(1)}, bf16[512,128]{1,0:T(8,128)(2,1)S(1)}, u32[]{:S(2)}, u32[]{:S(2)}) collective-permute-start(bf16[512,128]{1,0:T(8,128)(2,1)S(1)} %forward.4), channel_id=1, source_target_pairs={{0,1},{1,0},{2,3},{3,2},{4,5},{5,4},{6,7},{7,6},{8,9},{9,8},{10,11... | collective-permute-start | bytes 393224 | tf_op jit(solution)/shard_map/ppermute | solution.py:388
  78.3 1.6 %collective-permute-start.5 = (bf16[1024,128]{1,0:T(8,128)(2,1)S(1)}, bf16[1024,128]{1,0:T(8,128)(2,1)S(1)}, u32[]{:S(2)}, u32[]{:S(2)}) collective-permute-start(bf16[1024,128]{1,0:T(8,128)(2,1)S(1)} %forward.5), channel_id=1, source_target_pairs={{0,1},{1,0},{2,3},{3,2},{4,5},{5,4},{6,7},{7,6},{8,9},{9,8},{10,11... | collective-permute-start | bytes 786440 | tf_op jit(solution)/shard_map/ppermute | solution.py:388

commit v6 on v5

--- a/solution.py
+++ b/solution.py
@@ -182,7 +182,7 @@
 class Block:
     def __init__(self, q_ref, part_ref, stat_ref, own_ref, other_ref, out_ref, count, place, i, f):
         new, width = q_ref.shape[1:]
-        rows = own_ref.shape[0] // (2 * q_ref.shape[0])
+        rows = other_ref.shape[0] // q_ref.shape[0]
         self.step = rows // 2
         pairs = width // (2 * HEAD)
         core = lax.axis_index("beam") % 2
@@ -252,18 +252,23 @@
         self.store(part * rest + mm(weights, values), mm(weights, ones) + mm(sums, spread) * rest)
 
 
-def attend_blocks(works, stat_ref, held_ref, out_ref, sems, ready=None, rolled=False):
-    local, _, width = works[0][0].shape
-    count = out_ref.shape[2] // HEAD
-
-    def block(n, i, f):
-        q_ref, part_ref, own_ref, other_ref, place = works[n]
-        return Block(q_ref, part_ref, stat_ref, own_ref, other_ref, held_ref.at[n], count, place, i, f)
-
-    def send(n, i):
-        lanes = pl.ds(pl.multiple_of(works[n][4] * width, width), width)
-        return pltpu.make_async_copy(held_ref.at[n, i], out_ref.at[i, :, lanes], sems.at[n, i])
-
+def run_blocks(block, order, most, ready=None, after=None):
+    held = None
+    for t in range(len(order) + 1):
+        last, held = held, None
+        if t < len(order):
+            if ready is not None:
+                ready(*order[t])
+            held, top = block(*order[t]).weigh()
+            most = jnp.maximum(most, top)
+        if t > 0:
+            block(*order[t - 1]).finish(last)
+            if after is not None:
+                after(*order[t - 1])
+    return most
+
+
+def shifted_rows(stat_ref, count):
     lane = lax.broadcasted_iota(jnp.int32, stat_ref.shape[1:], 1)
 
     def moved(i, most):
@@ -271,42 +276,42 @@
         tops = jnp.where(tops == 0.0, -jnp.inf, jnp.inf)
         return jnp.maximum(most, jnp.max(tops.reshape(-1, 8, HEAD), axis=0))
 
-    most = jnp.full((8, HEAD), -jnp.inf, jnp.float32)
-
-    def run(order, most):
-        held = None
-        for t in range(len(order) + 1):
-            last, held = held, None
-            if t < len(order):
-                n, i, f = order[t]
-                if ready is not None and f == 0:
-                    ready(i)
-                held, top = block(n, i, f).weigh()
-                most = jnp.maximum(most, top)
-            if t > 0:
-                n, i, f = order[t - 1]
-                block(n, i, f).finish(last)
-                if f == 1:
-                    send(n, i).start()
-        return most
-
+    return lax.fori_loop(0, stat_ref.shape[0], moved, jnp.full((8, HEAD), -jnp.inf, jnp.float32))
+
+
+def attend_blocks(work, stat_ref, held_ref, out_ref, sems, ready=None, rolled=False):
+    q_ref, part_ref, own_ref, other_ref, place = work
+    local, _, width = q_ref.shape
+    count = out_ref.shape[2] // HEAD
+
+    def block(i, f):
+        return Block(q_ref, part_ref, stat_ref, own_ref, other_ref, held_ref, count, place, i, f)
+
+    def send(i):
+        lanes = pl.ds(pl.multiple_of(place * width, width), width)
+        return pltpu.make_async_copy(held_ref.at[i], out_ref.at[i, :, lanes], sems.at[i])
+
+    def after(i, f):
+        if f == 1:
+            send(i).start()
+
+    most = shifted_rows(stat_ref, count)
     if rolled:
-        most = lax.fori_loop(0, local, lambda i, most: run([(0, i, 0), (0, i, 1)], most), most)
+        run = lambda i, most: run_blocks(block, [(i, 0), (i, 1)], most, after=after)
+        most = lax.fori_loop(0, local, run, most)
     else:
-        most = run([(n, i, f) for n in range(len(works)) for i in range(local) for f in range(2)], most)
-    largest = jnp.max(lax.fori_loop(0, local, moved, most))
-    every = [(n, i) for n in range(len(works)) for i in range(local)]
-    for n, i in every:
-        send(n, i).wait()
+        most = run_blocks(block, [(i, f) for i in range(local) for f in range(2)], most, ready, after)
+    largest = jnp.max(most)
+    for i in range(local):
+        send(i).wait()
 
     @pl.when(largest > LIMIT)
     def _():
-        for n in range(len(works)):
-            lax.fori_loop(0, 2 * local, lambda t, c: (block(n, t // 2, t % 2).shifted(), c)[1], 0)
-        for n, i in every:
-            send(n, i).start()
-        for n, i in every:
-            send(n, i).wait()
+        lax.fori_loop(0, 2 * local, lambda t, c: (block(t // 2, t % 2).shifted(), c)[1], 0)
+        for i in range(local):
+            send(i).start()
+        for i in range(local):
+            send(i).wait()
 
 
 def stage(q_ref, part_ref, m, i, to_q, to_part, sems, chips):
@@ -335,14 +340,15 @@
     item_copy.wait()
     share_rewards(items, table_ref, share_ref)
 
-    def ready(i):
-        for copy in mine(i):
-            copy.wait()
-        for copy in following(i):
-            copy.start()
+    def ready(i, f):
+        if f == 0:
+            for copy in mine(i):
+                copy.wait()
+            for copy in following(i):
+                copy.start()
 
     stat_copy.wait()
-    attend_blocks([(held_q, held_part, own_ref, other_ref, chip)], stat_out, held, out_ref, out_sems, ready)
+    attend_blocks((held_q, held_part, own_ref, other_ref, chip), stat_out, held, out_ref, out_sems, ready)
     for i in range(local):
         for copy in following(i):
             copy.wait()
@@ -351,7 +357,7 @@
 def attend_second(chips, q_ref, part_ref, next_q, next_part, stat_ref, own_ref, other_ref, _, *refs):
     out_ref, token_ref, *later = refs[: 2 + 2 * len(LAST)]
     held, sems, next_sems = refs[2 + 2 * len(LAST) :]
-    local = held.shape[1]
+    local = held.shape[0]
     chip = lax.axis_index("beam") % (2 * chips) // 2
 
     def staged():
@@ -362,21 +368,74 @@
     for copy in staged():
         copy.start()
     token_ref[...] = jnp.zeros_like(token_ref)
-    works = [(next_q, next_part, own_ref, other_ref, chip ^ SECOND)]
-    attend_blocks(works, stat_ref, held, out_ref, sems, rolled=True)
+    work = (next_q, next_part, own_ref, other_ref, chip ^ SECOND)
+    attend_blocks(work, stat_ref, held, out_ref, sems, rolled=True)
     for copy in staged():
         copy.wait()
 
 
+def attend_half(chips, same, stat_ref, operands, held_ref, count, after=None):
+    chip = lax.axis_index("beam") % (2 * chips) // 2
+    f = lax.axis_index("beam") % 2 if same else 1 - lax.axis_index("beam") % 2
+    local = stat_ref.shape[0]
+
+    def block(n, i):
+        q_ref, part_ref, piece_ref = operands[n]
+        return Block(q_ref, part_ref, stat_ref, piece_ref, piece_ref, held_ref.at[n], count, chip ^ LAST[n], i, f)
+
+    order = [(n, i) for n in range(len(LAST)) for i in range(local)]
+    most = jnp.max(run_blocks(block, order, shifted_rows(stat_ref, count), after=after))
+
+    def redo():
+        for n in range(len(LAST)):
+            lax.fori_loop(0, local, lambda i, c: (block(n, i).shifted(), c)[1], 0)
+
+    return most > LIMIT, redo
+
+
+def attend_own(chips, count, stat_ref, *refs):
+    *operands, held_ref = refs
+    rows = operands[2].shape[0] // 2
+    works = [(*operands[3 * n : 3 * n + 2], operands[3 * n + 2].at[pl.ds(0, rows), :]) for n in range(len(LAST))]
+    large, redo = attend_half(chips, True, stat_ref, works, held_ref, count)
+
+    @pl.when(large)
+    def _():
+        redo()
+
+
 def attend_last(chips, stat_ref, *refs):
-    *operands, other_ref, _, out_ref, held, sems = refs
-    count = other_ref.shape[0] // len(LAST)
+    *operands, other_ref, made_ref, _, out_ref, held_ref, sems = refs
+    local, _, width = operands[0].shape
+    half = width // 2
+    rows = other_ref.shape[0] // len(LAST)
+    works = [(*operands[2 * n : 2 * n + 2], other_ref.at[pl.ds(n * rows, rows), :]) for n in range(len(LAST))]
     chip = lax.axis_index("beam") % (2 * chips) // 2
-    works = [
-        (*operands[3 * n : 3 * n + 3], other_ref.at[pl.ds(n * count, count), :], chip ^ m)
-        for n, m in enumerate(LAST)
-    ]
-    attend_blocks(works, stat_ref, held, out_ref, sems)
+    core = lax.axis_index("beam") % 2
+
+    def send(k, n, i):
+        f = core if k == 0 else 1 - core
+        there = pl.ds(pl.multiple_of((chip ^ LAST[n]) * width + f * half, half), half)
+        here = pl.ds(pl.multiple_of(f * half, half), half)
+        source = (made_ref, held_ref)[k].at[n, i, :, here]
+        return pltpu.make_async_copy(source, out_ref.at[i, :, there], sems.at[k, n, i])
+
+    every = [(n, i) for n in range(len(LAST)) for i in range(local)]
+    for n, i in every:
+        send(0, n, i).start()
+    after = lambda n, i: send(1, n, i).start()
+    large, redo = attend_half(chips, False, stat_ref, works, held_ref, out_ref.shape[2] // HEAD, after)
+    for k in range(2):
+        for n, i in every:
+            send(k, n, i).wait()
+
+    @pl.when(large)
+    def _():
+        redo()
+        for n, i in every:
+            send(1, n, i).start()
+        for n, i in every:
+            send(1, n, i).wait()
 
 
 def params(mib):
@@ -478,7 +537,7 @@
     result = jax.ShapeDtypeStruct((local, new, width), bf16)
     token = jax.ShapeDtypeStruct((8, HEAD), jnp.float32)
     later = pltpu.VMEM((local, new, wide), bf16)
-    held = lambda n: pltpu.VMEM((n, local, new, wide), bf16)
+    halves = pltpu.VMEM((len(LAST), local, new, wide), bf16)
     many = pltpu.SemaphoreType.DMA
     attended, child_share, next_q, next_part, stat_held, done = pl.pallas_call(
         functools.partial(attend_first, chips),
@@ -494,7 +553,7 @@
         out_specs=[hbm] + [vmem] * 5,
         scratch_shapes=[pltpu.SMEM((children,), jnp.int32)]
         + [later] * 2
-        + [held(1), many((2, local)), many((2, local)), many, many, many((1, local))],
+        + [later, many((2, local)), many((2, local)), many, many, many((local,))],
         compiler_params=params(16),
         cost_estimate=small,
         name="attend_first",
@@ -504,7 +563,7 @@
         out_shape=[result, token] + [later] * (2 * len(LAST)),
         in_specs=[hbm, hbm] + [vmem] * 5 + [hbm],
         out_specs=[hbm, vmem] + [vmem] * (2 * len(LAST)),
-        scratch_shapes=[held(1), many((1, local)), many((len(LAST), 2, local))],
+        scratch_shapes=[later, many((local,)), many((len(LAST), 2, local))],
         input_output_aliases={7: 0},
         compiler_params=params(12),
         cost_estimate=small,
@@ -519,21 +578,31 @@
         pass_on([own[SECOND]], done),
         attended,
     )
+    others = pass_on([own[m] for m in LAST], done)
+    staged = [in_vmem(a) for a in staged]
     operands = []
     for n, m in enumerate(LAST):
-        operands += [in_vmem(staged[2 * n]), in_vmem(staged[2 * n + 1]), own[m]]
-    operands.append(pass_on([own[m] for m in LAST], done))
+        operands += [staged[2 * n], staged[2 * n + 1], own[m]]
+    made = pl.pallas_call(
+        functools.partial(attend_own, chips, width // HEAD),
+        out_shape=halves,
+        in_specs=[vmem] * (1 + len(operands)),
+        out_specs=vmem,
+        compiler_params=params(8),
+        cost_estimate=small,
+        name="attend_own",
+    )(in_vmem(stat_held), *operands)
     attended = pl.pallas_call(
         functools.partial(attend_last, chips),
         out_shape=result,
-        in_specs=[vmem] * (1 + len(operands)) + [hbm],
+        in_specs=[vmem] * (3 + len(staged)) + [hbm],
         out_specs=hbm,
-        scratch_shapes=[held(len(LAST)), many((len(LAST), local))],
-        input_output_aliases={1 + len(operands): 0},
+        scratch_shapes=[halves, many((2, len(LAST), local))],
+        input_output_aliases={3 + len(staged): 0},
         compiler_params=params(12),
         cost_estimate=small,
         name="attend_last",
-    )(in_vmem(stat_held), *operands, attended)
+    )(in_vmem(stat_held), *staged, others, in_vmem(made), attended)
     child_share = child_share.reshape(local)
     return (attended, child_share)
 

time: 103 us -> 102 us (level)
  waiting for transfers between devices: 2.74 us -> 1.35 us
    pallas_call x0 -> x1, Pallas kernels: none -> 10.5 us  [body(): pl.pallas_call(functools.partial(attend_own, chips, width // HEAD), out_s...]
    pallas_call x1, Pallas kernels: 23.1 us -> 12.6 us  [body(): pl.pallas_call(functools.partial(attend_last, chips), out_shape=result, i...]
    ppermute x6, waiting for transfers between devices: 2.74 us -> 1.35 us  [swap(): return lax.ppermute(a, 'beam', [(i, i ^ distance) for i in range(count)])]
  transfers between devices with their start and end apart: 7 -> 7, of which waited for: 2 -> 1; matrix products, arithmetic and copies ran while one was open for 0% -> 0% of each run, Pallas kernels for 60% -> 71%
where the time goes in v6:
time: 102 us
  Pallas kernels  88.1 us (86%)
  starting transfers between devices  11.4 us (11%)
  waiting for transfers between devices  1.35 us (1%)
    pallas_call x1, Pallas kernels, body(): pl.pallas_call(attend_new, grid=(local,), out_shape=[jax.ShapeDtypeStruct...  33.6 us
    pallas_call x1, Pallas kernels, body(): pl.pallas_call(functools.partial(attend_first, chips), out_shape=[result,...  14.9 us
    pallas_call x1, Pallas kernels, body(): pl.pallas_call(functools.partial(attend_second, chips), out_shape=[result...  13.2 us
    pallas_call x1, Pallas kernels, body(): pl.pallas_call(functools.partial(attend_last, chips), out_shape=result, i...  12.6 us
    pallas_call x1, Pallas kernels, body(): pl.pallas_call(functools.partial(attend_own, chips, width // HEAD), out_s...  10.5 us
    all_to_all x1, starting transfers between devices, body(): table = lax.all_to_all(packed, 'beam', 0, 0)  7.4 us
    ppermute x6, starting transfers between devices, swap(): return lax.ppermute(a, 'beam', [(i, i ^ distance) for i in range(count)])  4.01 us
    pallas_call x1, Pallas kernels, body(): pl.pallas_call(pack, out_shape=jax.ShapeDtypeStruct((beam_count, message,...  2.47 us
  transfers between devices with their start and end apart: 7, of which 1 were waited for; matrix products, arithmetic and copies ran while one was open for 0% of the time, Pallas kernels for 71%

profile of v6, /device:TPU:0, one launch (start us, length us, event | category | flops | bytes accessed | tf_op | source)
XLA Modules:
  0.0 102.1 jit_solution(12166282965227287807)
XLA Ops:
  0.6 0.0 copy-start
  0.6 2.5 %pack.1 = bf16[16,272,128]{2,1,0:T(8,128)(2,1)} custom-call(s32[1,64]{1,0:T(1,128)} %bitcast.4, bf16[4,2,64,1024]{3,2,1,0:T(8,128)(2,1)} %kv_hbm.1, bf16[4,4096]{1,0:T(4,128)(2,1)} %last_hbm.1, f32[1,4096]{1,0:T(1,128)} %bitcast.3), custom_call_target="tpu_custom_call" | custom-call | tf_op jit(solution)/shard_map/pack/pallas_call | solution.py:468
  3.1 7.4 %all-to-all-start = ((bf16[16,272,128]{2,1,0:T(8,128)(2,1)}), bf16[16,272,128]{2,1,0:T(8,128)(2,1)S(1)}, u32[]{:S(2)}, u32[]{:S(2)}) async-start(bf16[16,272,128]{2,1,0:T(8,128)(2,1)} %pack.1), calls=%async_computation | async-start | bytes 2228224 | tf_op jit(solution)/shard_map/all_to_all | solution.py:485
  10.5 0.0 copy-done
  10.6 0.2 and_reduce_fusion
  10.8 0.0 copy-start.1
  10.8 0.1 dynamic_slice.3.item_ref.refs_1_
  10.9 33.6 %attend_new.1 = (bf16[4,256,4096]{2,1,0:T(8,128)(2,1)}, bf16[4,256,128]{2,1,0:T(8,128)(2,1)}) custom-call(bf16[4,256,4096]{2,1,0:T(8,128)(2,1)} %q_ref.5, bf16[4,256,1024]{2,1,0:T(8,128)(2,1)} %k_ref.1, bf16[4,256,1024]{2,1,0:T(8,128)(2,1)} %v_ref.1), custom_call_target="tpu_custom_call" | custom-call | flops 4294967296 | bytes 25165824 | tf_op jit(solution)/shard_map/attend_new/pallas_call | solution.py:490
  44.4 0.0 copy-done.1
  44.4 0.0 all-to-all-done.table_ref
  44.4 0.8 pick.1
  45.2 2.0 %collective-permute-start.1 = (bf16[1024,128]{1,0:T(8,128)(2,1)S(1)}, bf16[1024,128]{1,0:T(8,128)(2,1)S(1)}, u32[]{:S(2)}, u32[]{:S(2)}) collective-permute-start(bf16[1024,128]{1,0:T(8,128)(2,1)S(1)} %get-tuple-element.26), channel_id=1, source_target_pairs={{0,2},{1,3},{2,0},{3,1},{4,6},{5,7},{6,4},{7,5},{8,10},{9,11},{10,... | collective-permute-start | bytes 786440 | tf_op jit(solution)/shard_map/ppermute | solution.py:447
  47.2 0.1 collective-permute-start
  47.3 1.5 %collective-permute-start.3 = (bf16[1024,128]{1,0:T(8,128)(2,1)S(1)}, bf16[1024,128]{1,0:T(8,128)(2,1)S(1)}, u32[]{:S(2)}, u32[]{:S(2)}) collective-permute-start(bf16[1024,128]{1,0:T(8,128)(2,1)S(1)} %get-tuple-element.33), channel_id=1, source_target_pairs={{0,4},{1,5},{2,6},{3,7},{4,0},{5,1},{6,2},{7,3},{8,12},{9,13},{10,... | collective-permute-start | bytes 786440 | tf_op jit(solution)/shard_map/ppermute | solution.py:447
  48.8 0.2 collective-permute-start.4
  49.0 0.0 collective-permute-done.other_ref
  49.0 14.9 %attend_first.1 = (bf16[4,256,4096]{2,1,0:T(8,128)(2,1)}, f32[1,4]{1,0:T(1,128)}, bf16[4,256,1024]{2,1,0:T(8,128)(2,1)S(1)}, bf16[4,256,1024]{2,1,0:T(8,128)(2,1...) custom-call(s32[64]{0:T(128)} %copy-done.1, bf16[16,272,128]{2,1,0:T(8,128)(2,1)S(1)} %all-to-all-done.table_ref, ...), custom_call_target="tpu_custom_call" | custom-call | flops 1024 | bytes 1024 | tf_op jit(solution)/shard_map/attend_first/pallas_call | solution.py:542
  63.9 0.0 collective-permute-done.1.refs_0_.own_ref
  63.9 0.1 collective-permute-start.2
  64.0 1.3 %collective-permute-done.2.other_ref = bf16[512,128]{1,0:T(8,128)(2,1)S(1)} collective-permute-done((bf16[512,128]{1,0:T(8,128)(2,1)S(1)}, bf16[512,128]{1,0:T(8,128)(2,1)S(1)}, u32[]{:S(2)}, u32[]{:S(2)}) %collective-permute-start.2) | collective-permute-done | bytes 131104 | tf_op jit(solution)/shard_map/ppermute | solution.py:447
  65.3 13.2 %attend_second.1 = (bf16[4,256,4096]{2,1,0:T(8,128)(2,1)}, f32[8,128]{1,0:T(8,128)S(1)}, bf16[4,256,1024]{2,1,0:T(8,128)(2,1)S(1)}, bf16[4,256,1024]{2,1,0:T(8,1...) custom-call(bf16[4,256,4096]{2,1,0:T(8,128)(2,1)} %q_ref.5, ...), custom_call_target="tpu_custom_call", output_to_operand_aliasing={{0}: (7, {})} | custom-call | flops 1024 | bytes 1024 | tf_op jit(solution)/shard_map/attend_second/pallas_call | solution.py:561
  78.5 0.0 collective-permute-done.3.refs_0_.refs_2_
  78.5 0.0 collective-permute-done.4.refs_1_.refs_5_
  78.6 0.2 collective-permute-start.5
  78.8 10.5 %attend_own.1.refs_5_ = bf16[2,4,256,1024]{3,2,1,0:T(8,128)(2,1)S(1)} custom-call(bf16[4,256,128]{2,1,0:T(8,128)(2,1)S(1)} %get-tuple-element.23.stat_ref, bf16[4,256,1024]{2,1,0:T(8,128)(2,1)S(1)} %get-tuple-element.29.refs_0_, bf16[4,256,1024]{2,1,0:T(8,128)(2,1)S(1)} %get-tuple-element.30.refs_1_, ...), custom_call_target="tpu_custom_call" | custom-call | flops 1024 | bytes 1024 | tf_op jit(solution)/shard_map/attend_own/pallas_call | solution.py:586
  89.3 0.0 collective-permute-done.5.refs_4_
  89.3 12.6 %attend_last.1 = bf16[4,256,4096]{2,1,0:T(8,128)(2,1)} custom-call(bf16[4,256,128]{2,1,0:T(8,128)(2,1)S(1)} %get-tuple-element.23.stat_ref, bf16[4,256,1024]{2,1,0:T(8,128)(2,1)S(1)} %get-tuple-element.29.refs_0_, bf16[4,256,1024]{2,1,0:T(8,128)(2,1)S(1)} %get-tuple-element.30.refs_1_, ...), custom_call_target="tpu_custom_call", output_to_operand_aliasing={{}: (7, {})} | custom-call | flops 1024 | bytes 1024 | tf_op jit(solution)/shard_map/attend_last/pallas_call | solution.py:595
  (5 shorter events, 0.1 us)
Async XLA Ops:
  0.6 9.9 %copy-start = (s32[64]{0:T(128)S(1)}, s32[64]{0:T(128)}, u32[]{:S(2)}) copy-start(s32[64]{0:T(128)} %param.13) | copy-start | bytes 772
  3.1 41.3 %all-to-all-start = ((bf16[16,272,128]{2,1,0:T(8,128)(2,1)}), bf16[16,272,128]{2,1,0:T(8,128)(2,1)S(1)}, u32[]{:S(2)}, u32[]{:S(2)}) async-start(bf16[16,272,128]{2,1,0:T(8,128)(2,1)} %pack.1), calls=%async_computation | async-start | bytes 2228224 | tf_op jit(solution)/shard_map/all_to_all | solution.py:485
  10.8 33.7 %copy-start.1 = (s32[64]{0:T(128)}, s32[64]{0:T(128)S(1)}, u32[]{:S(2)}) copy-start(s32[64]{0:T(128)S(1)} %convert_add_fusion.item_ref) | copy-start | bytes 772
  45.2 18.6 %collective-permute-start.1 = (bf16[1024,128]{1,0:T(8,128)(2,1)S(1)}, bf16[1024,128]{1,0:T(8,128)(2,1)S(1)}, u32[]{:S(2)}, u32[]{:S(2)}) collective-permute-start(bf16[1024,128]{1,0:T(8,128)(2,1)S(1)} %get-tuple-element.26), channel_id=1, source_target_pairs={{0,2},{1,3},{2,0},{3,1},{4,6},{5,7},{6,4},{7,5},{8,10},{9,11},{10,... | collective-permute-start | bytes 786440 | tf_op jit(solution)/shard_map/ppermute | solution.py:447
  47.2 1.8 %collective-permute-start = (bf16[512,128]{1,0:T(8,128)(2,1)S(1)}, bf16[512,128]{1,0:T(8,128)(2,1)S(1)}, u32[]{:S(2)}, u32[]{:S(2)}) collective-permute-start(bf16[512,128]{1,0:T(8,128)(2,1)S(1)} %forward.3), channel_id=1, source_target_pairs={{0,1},{1,0},{2,3},{3,2},{4,5},{5,4},{6,7},{7,6},{8,9},{9,8},{10,11... | collective-permute-start | bytes 393224 | tf_op jit(solution)/shard_map/ppermute | solution.py:447
  47.3 31.2 %collective-permute-start.3 = (bf16[1024,128]{1,0:T(8,128)(2,1)S(1)}, bf16[1024,128]{1,0:T(8,128)(2,1)S(1)}, u32[]{:S(2)}, u32[]{:S(2)}) collective-permute-start(bf16[1024,128]{1,0:T(8,128)(2,1)S(1)} %get-tuple-element.33), channel_id=1, source_target_pairs={{0,4},{1,5},{2,6},{3,7},{4,0},{5,1},{6,2},{7,3},{8,12},{9,13},{10,... | collective-permute-start | bytes 786440 | tf_op jit(solution)/shard_map/ppermute | solution.py:447
  48.8 29.7 %collective-permute-start.4 = (bf16[1024,128]{1,0:T(8,128)(2,1)S(1)}, bf16[1024,128]{1,0:T(8,128)(2,1)S(1)}, u32[]{:S(2)}, u32[]{:S(2)}) collective-permute-start(bf16[1024,128]{1,0:T(8,128)(2,1)S(1)} %get-tuple-element.34), channel_id=1, source_target_pairs={{0,6},{1,7},{2,4},{3,5},{4,2},{5,3},{6,0},{7,1},{8,14},{9,15},{10,... | collective-permute-start | bytes 786440 | tf_op jit(solution)/shard_map/ppermute | solution.py:447
  63.9 1.4 %collective-permute-start.2 = (bf16[512,128]{1,0:T(8,128)(2,1)S(1)}, bf16[512,128]{1,0:T(8,128)(2,1)S(1)}, u32[]{:S(2)}, u32[]{:S(2)}) collective-permute-start(bf16[512,128]{1,0:T(8,128)(2,1)S(1)} %forward.4), channel_id=1, source_target_pairs={{0,1},{1,0},{2,3},{3,2},{4,5},{5,4},{6,7},{7,6},{8,9},{9,8},{10,11... | collective-permute-start | bytes 393224 | tf_op jit(solution)/shard_map/ppermute | solution.py:447
  78.6 10.8 %collective-permute-start.5 = (bf16[1024,128]{1,0:T(8,128)(2,1)S(1)}, bf16[1024,128]{1,0:T(8,128)(2,1)S(1)}, u32[]{:S(2)}, u32[]{:S(2)}) collective-permute-start(bf16[1024,128]{1,0:T(8,128)(2,1)S(1)} %forward.5), channel_id=1, source_target_pairs={{0,1},{1,0},{2,3},{3,2},{4,5},{5,4},{6,7},{7,6},{8,9},{9,8},{10,11... | collective-permute-start | bytes 786440 | tf_op jit(solution)/shard_map/ppermute | solution.py:447

commit v7 on v6

--- a/solution.py
+++ b/solution.py
@@ -279,7 +279,7 @@
     return lax.fori_loop(0, stat_ref.shape[0], moved, jnp.full((8, HEAD), -jnp.inf, jnp.float32))
 
 
-def attend_blocks(work, stat_ref, held_ref, out_ref, sems, ready=None, rolled=False):
+def attend_blocks(work, stat_ref, most, held_ref, out_ref, sems, ready=None, rolled=False):
     q_ref, part_ref, own_ref, other_ref, place = work
     local, _, width = q_ref.shape
     count = out_ref.shape[2] // HEAD
@@ -295,7 +295,6 @@
         if f == 1:
             send(i).start()
 
-    most = shifted_rows(stat_ref, count)
     if rolled:
         run = lambda i, most: run_blocks(block, [(i, 0), (i, 1)], most, after=after)
         most = lax.fori_loop(0, local, run, most)
@@ -336,7 +335,6 @@
     for i in range(local):
         for copy in mine(i):
             copy.start()
-    token_ref[...] = jnp.zeros_like(token_ref)
     item_copy.wait()
     share_rewards(items, table_ref, share_ref)
 
@@ -348,13 +346,15 @@
                 copy.start()
 
     stat_copy.wait()
-    attend_blocks((held_q, held_part, own_ref, other_ref, chip), stat_out, held, out_ref, out_sems, ready)
+    most = shifted_rows(stat_out, out_ref.shape[2] // HEAD)
+    token_ref[...] = most
+    attend_blocks((held_q, held_part, own_ref, other_ref, chip), stat_out, most, held, out_ref, out_sems, ready)
     for i in range(local):
         for copy in following(i):
             copy.wait()
 
 
-def attend_second(chips, q_ref, part_ref, next_q, next_part, stat_ref, own_ref, other_ref, _, *refs):
+def attend_second(chips, q_ref, part_ref, next_q, next_part, stat_ref, own_ref, other_ref, moved_ref, _, *refs):
     out_ref, token_ref, *later = refs[: 2 + 2 * len(LAST)]
     held, sems, next_sems = refs[2 + 2 * len(LAST) :]
     local = held.shape[0]
@@ -369,12 +369,12 @@
         copy.start()
     token_ref[...] = jnp.zeros_like(token_ref)
     work = (next_q, next_part, own_ref, other_ref, chip ^ SECOND)
-    attend_blocks(work, stat_ref, held, out_ref, sems, rolled=True)
+    attend_blocks(work, stat_ref, moved_ref[...], held, out_ref, sems, rolled=True)
     for copy in staged():
         copy.wait()
 
 
-def attend_half(chips, same, stat_ref, operands, held_ref, count, after=None):
+def attend_half(chips, same, stat_ref, moved_ref, operands, held_ref, count, after=None):
     chip = lax.axis_index("beam") % (2 * chips) // 2
     f = lax.axis_index("beam") % 2 if same else 1 - lax.axis_index("beam") % 2
     local = stat_ref.shape[0]
@@ -384,7 +384,7 @@
         return Block(q_ref, part_ref, stat_ref, piece_ref, piece_ref, held_ref.at[n], count, chip ^ LAST[n], i, f)
 
     order = [(n, i) for n in range(len(LAST)) for i in range(local)]
-    most = jnp.max(run_blocks(block, order, shifted_rows(stat_ref, count), after=after))
+    most = jnp.max(run_blocks(block, order, moved_ref[...], after=after))
 
     def redo():
         for n in range(len(LAST)):
@@ -393,18 +393,18 @@
     return most > LIMIT, redo
 
 
-def attend_own(chips, count, stat_ref, *refs):
+def attend_own(chips, count, stat_ref, moved_ref, *refs):
     *operands, held_ref = refs
     rows = operands[2].shape[0] // 2
     works = [(*operands[3 * n : 3 * n + 2], operands[3 * n + 2].at[pl.ds(0, rows), :]) for n in range(len(LAST))]
-    large, redo = attend_half(chips, True, stat_ref, works, held_ref, count)
+    large, redo = attend_half(chips, True, stat_ref, moved_ref, works, held_ref, count)
 
     @pl.when(large)
     def _():
         redo()
 
 
-def attend_last(chips, stat_ref, *refs):
+def attend_last(chips, stat_ref, moved_ref, *refs):
     *operands, other_ref, made_ref, _, out_ref, held_ref, sems = refs
     local, _, width = operands[0].shape
     half = width // 2
@@ -424,7 +424,7 @@
     for n, i in every:
         send(0, n, i).start()
     after = lambda n, i: send(1, n, i).start()
-    large, redo = attend_half(chips, False, stat_ref, works, held_ref, out_ref.shape[2] // HEAD, after)
+    large, redo = attend_half(chips, False, stat_ref, moved_ref, works, held_ref, out_ref.shape[2] // HEAD, after)
     for k in range(2):
         for n, i in every:
             send(k, n, i).wait()
@@ -558,13 +558,14 @@
         cost_estimate=small,
         name="attend_first",
     )(in_hbm(item), table, in_hbm(queries), in_hbm(part), in_hbm(stat), own[0], pass_on(own[:1], near))
+    moved = done
     attended, done, *staged = pl.pallas_call(
         functools.partial(attend_second, chips),
         out_shape=[result, token] + [later] * (2 * len(LAST)),
-        in_specs=[hbm, hbm] + [vmem] * 5 + [hbm],
+        in_specs=[hbm, hbm] + [vmem] * 6 + [hbm],
         out_specs=[hbm, vmem] + [vmem] * (2 * len(LAST)),
         scratch_shapes=[later, many((local,)), many((len(LAST), 2, local))],
-        input_output_aliases={7: 0},
+        input_output_aliases={8: 0},
         compiler_params=params(12),
         cost_estimate=small,
         name="attend_second",
@@ -576,6 +577,7 @@
         in_vmem(stat_held),
         own[SECOND],
         pass_on([own[SECOND]], done),
+        moved,
         attended,
     )
     others = pass_on([own[m] for m in LAST], done)
@@ -586,23 +588,23 @@
     made = pl.pallas_call(
         functools.partial(attend_own, chips, width // HEAD),
         out_shape=halves,
-        in_specs=[vmem] * (1 + len(operands)),
+        in_specs=[vmem] * (2 + len(operands)),
         out_specs=vmem,
         compiler_params=params(8),
         cost_estimate=small,
         name="attend_own",
-    )(in_vmem(stat_held), *operands)
+    )(in_vmem(stat_held), moved, *operands)
     attended = pl.pallas_call(
         functools.partial(attend_last, chips),
         out_shape=result,
-        in_specs=[vmem] * (3 + len(staged)) + [hbm],
+        in_specs=[vmem] * (4 + len(staged)) + [hbm],
         out_specs=hbm,
         scratch_shapes=[halves, many((2, len(LAST), local))],
-        input_output_aliases={3 + len(staged): 0},
+        input_output_aliases={4 + len(staged): 0},
         compiler_params=params(12),
         cost_estimate=small,
         name="attend_last",
-    )(in_vmem(stat_held), *staged, others, in_vmem(made), attended)
+    )(in_vmem(stat_held), moved, *staged, others, in_vmem(made), attended)
     child_share = child_share.reshape(local)
     return (attended, child_share)
 

time: 102 us -> 102 us (level)
  no operation moved by 1% of the time
where the time goes in v7:
time: 102 us
  Pallas kernels  87.8 us (86%)
  starting transfers between devices  11.4 us (11%)
  waiting for transfers between devices  1.35 us (1%)
    pallas_call x1, Pallas kernels, body(): pl.pallas_call(attend_new, grid=(local,), out_shape=[jax.ShapeDtypeStruct...  33.6 us
    pallas_call x1, Pallas kernels, body(): pl.pallas_call(functools.partial(attend_first, chips), out_shape=[result,...  14.9 us
    pallas_call x1, Pallas kernels, body(): pl.pallas_call(functools.partial(attend_second, chips), out_shape=[result...  13.1 us
    pallas_call x1, Pallas kernels, body(): pl.pallas_call(functools.partial(attend_last, chips), out_shape=result, i...  12.4 us
    pallas_call x1, Pallas kernels, body(): pl.pallas_call(functools.partial(attend_own, chips, width // HEAD), out_s...  10.5 us
    all_to_all x1, starting transfers between devices, body(): table = lax.all_to_all(packed, 'beam', 0, 0)  7.4 us
    ppermute x6, starting transfers between devices, swap(): return lax.ppermute(a, 'beam', [(i, i ^ distance) for i in range(count)])  4.01 us
    pallas_call x1, Pallas kernels, body(): pl.pallas_call(pack, out_shape=jax.ShapeDtypeStruct((beam_count, message,...  2.47 us
  transfers between devices with their start and end apart: 7, of which 1 were waited for; matrix products, arithmetic and copies ran while one was open for 0% of the time, Pallas kernels for 71%

profile of v7, /device:TPU:0, one launch (start us, length us, event | category | flops | bytes accessed | tf_op | source)
XLA Modules:
  0.0 101.8 jit_solution(16952617809712984320)
XLA Ops:
  0.6 0.0 copy-start
  0.6 2.5 %pack.1 = bf16[16,272,128]{2,1,0:T(8,128)(2,1)} custom-call(s32[1,64]{1,0:T(1,128)} %bitcast.4, bf16[4,2,64,1024]{3,2,1,0:T(8,128)(2,1)} %kv_hbm.1, bf16[4,4096]{1,0:T(4,128)(2,1)} %last_hbm.1, f32[1,4096]{1,0:T(1,128)} %bitcast.3), custom_call_target="tpu_custom_call" | custom-call | tf_op jit(solution)/shard_map/pack/pallas_call | solution.py:468
  3.1 7.4 %all-to-all-start = ((bf16[16,272,128]{2,1,0:T(8,128)(2,1)}), bf16[16,272,128]{2,1,0:T(8,128)(2,1)S(1)}, u32[]{:S(2)}, u32[]{:S(2)}) async-start(bf16[16,272,128]{2,1,0:T(8,128)(2,1)} %pack.1), calls=%async_computation | async-start | bytes 2228224 | tf_op jit(solution)/shard_map/all_to_all | solution.py:485
  10.5 0.0 copy-done
  10.6 0.2 and_reduce_fusion
  10.8 0.0 copy-start.1
  10.8 0.1 dynamic_slice.3.item_ref.refs_1_
  10.9 33.6 %attend_new.1 = (bf16[4,256,4096]{2,1,0:T(8,128)(2,1)}, bf16[4,256,128]{2,1,0:T(8,128)(2,1)}) custom-call(bf16[4,256,4096]{2,1,0:T(8,128)(2,1)} %q_ref.5, bf16[4,256,1024]{2,1,0:T(8,128)(2,1)} %k_ref.1, bf16[4,256,1024]{2,1,0:T(8,128)(2,1)} %v_ref.1), custom_call_target="tpu_custom_call" | custom-call | flops 4294967296 | bytes 25165824 | tf_op jit(solution)/shard_map/attend_new/pallas_call | solution.py:490
  44.4 0.0 copy-done.1
  44.4 0.0 all-to-all-done.table_ref
  44.4 0.8 pick.1
  45.2 2.0 %collective-permute-start.1 = (bf16[1024,128]{1,0:T(8,128)(2,1)S(1)}, bf16[1024,128]{1,0:T(8,128)(2,1)S(1)}, u32[]{:S(2)}, u32[]{:S(2)}) collective-permute-start(bf16[1024,128]{1,0:T(8,128)(2,1)S(1)} %get-tuple-element.27), channel_id=1, source_target_pairs={{0,2},{1,3},{2,0},{3,1},{4,6},{5,7},{6,4},{7,5},{8,10},{9,11},{10,... | collective-permute-start | bytes 786440 | tf_op jit(solution)/shard_map/ppermute | solution.py:447
  47.2 0.1 collective-permute-start
  47.3 1.5 %collective-permute-start.3 = (bf16[1024,128]{1,0:T(8,128)(2,1)S(1)}, bf16[1024,128]{1,0:T(8,128)(2,1)S(1)}, u32[]{:S(2)}, u32[]{:S(2)}) collective-permute-start(bf16[1024,128]{1,0:T(8,128)(2,1)S(1)} %get-tuple-element.33), channel_id=1, source_target_pairs={{0,4},{1,5},{2,6},{3,7},{4,0},{5,1},{6,2},{7,3},{8,12},{9,13},{10,... | collective-permute-start | bytes 786440 | tf_op jit(solution)/shard_map/ppermute | solution.py:447
  48.8 0.2 collective-permute-start.4
  49.0 0.0 collective-permute-done.other_ref
  49.0 14.9 %attend_first.1 = (bf16[4,256,4096]{2,1,0:T(8,128)(2,1)}, f32[1,4]{1,0:T(1,128)}, bf16[4,256,1024]{2,1,0:T(8,128)(2,1)S(1)}, bf16[4,256,1024]{2,1,0:T(8,128)(2,1...) custom-call(s32[64]{0:T(128)} %copy-done.1, bf16[16,272,128]{2,1,0:T(8,128)(2,1)S(1)} %all-to-all-done.table_ref, ...), custom_call_target="tpu_custom_call" | custom-call | flops 1024 | bytes 1024 | tf_op jit(solution)/shard_map/attend_first/pallas_call | solution.py:542
  63.9 0.0 collective-permute-done.1.refs_0_.own_ref
  63.9 0.1 collective-permute-start.2
  64.0 1.3 %collective-permute-done.2.other_ref = bf16[512,128]{1,0:T(8,128)(2,1)S(1)} collective-permute-done((bf16[512,128]{1,0:T(8,128)(2,1)S(1)}, bf16[512,128]{1,0:T(8,128)(2,1)S(1)}, u32[]{:S(2)}, u32[]{:S(2)}) %collective-permute-start.2) | collective-permute-done | bytes 131104 | tf_op jit(solution)/shard_map/ppermute | solution.py:447
  65.3 13.1 %attend_second.1 = (bf16[4,256,4096]{2,1,0:T(8,128)(2,1)}, f32[8,128]{1,0:T(8,128)S(1)}, bf16[4,256,1024]{2,1,0:T(8,128)(2,1)S(1)}, bf16[4,256,1024]{2,1,0:T(8,1...) custom-call(bf16[4,256,4096]{2,1,0:T(8,128)(2,1)} %q_ref.5, ...), custom_call_target="tpu_custom_call", output_to_operand_aliasing={{0}: (8, {})} | custom-call | flops 1024 | bytes 1024 | tf_op jit(solution)/shard_map/attend_second/pallas_call | solution.py:562
  78.4 0.0 collective-permute-done.3.refs_0_.refs_2_
  78.4 0.0 collective-permute-done.4.refs_1_.refs_5_
  78.5 0.2 collective-permute-start.5
  78.7 10.5 %attend_own.1.refs_5_ = bf16[2,4,256,1024]{3,2,1,0:T(8,128)(2,1)S(1)} custom-call(bf16[4,256,128]{2,1,0:T(8,128)(2,1)S(1)} %get-tuple-element.23.stat_ref, f32[8,128]{1,0:T(8,128)S(1)} %get-tuple-element.24.refs_1_.moved_ref, bf16[4,256,1024]{2,1,0:T(8,128)(2,1)S(1)} %get-tuple-element.29.refs_0_, bf16[4,256,1024]{2,1,0:T(8,128)(2,1)S(1)} %get-tuple-element.30.refs_1_, ...), custom_call_target="tpu_custom_call" | custom-call | flops 1024 | bytes 1024 | tf_op jit(solution)/shard_map/attend_own/pallas_call | solution.py:588
  89.2 0.0 collective-permute-done.5.refs_4_
  89.2 12.4 %attend_last.1 = bf16[4,256,4096]{2,1,0:T(8,128)(2,1)} custom-call(bf16[4,256,128]{2,1,0:T(8,128)(2,1)S(1)} %get-tuple-element.23.stat_ref, f32[8,128]{1,0:T(8,128)S(1)} %get-tuple-element.24.refs_1_.moved_ref, bf16[4,256,1024]{2,1,0:T(8,128)(2,1)S(1)} %get-tuple-element.29.refs_0_, ...), custom_call_target="tpu_custom_call", output_to_operand_aliasing={{}: (8, {})} | custom-call | flops 1024 | bytes 1024 | tf_op jit(solution)/shard_map/attend_last/pallas_call | solution.py:597
  (5 shorter events, 0.1 us)
Async XLA Ops:
  0.6 9.9 %copy-start = (s32[64]{0:T(128)S(1)}, s32[64]{0:T(128)}, u32[]{:S(2)}) copy-start(s32[64]{0:T(128)} %param.13) | copy-start | bytes 772
  3.1 41.3 %all-to-all-start = ((bf16[16,272,128]{2,1,0:T(8,128)(2,1)}), bf16[16,272,128]{2,1,0:T(8,128)(2,1)S(1)}, u32[]{:S(2)}, u32[]{:S(2)}) async-start(bf16[16,272,128]{2,1,0:T(8,128)(2,1)} %pack.1), calls=%async_computation | async-start | bytes 2228224 | tf_op jit(solution)/shard_map/all_to_all | solution.py:485
  10.8 33.7 %copy-start.1 = (s32[64]{0:T(128)}, s32[64]{0:T(128)S(1)}, u32[]{:S(2)}) copy-start(s32[64]{0:T(128)S(1)} %convert_add_fusion.item_ref) | copy-start | bytes 772
  45.2 18.6 %collective-permute-start.1 = (bf16[1024,128]{1,0:T(8,128)(2,1)S(1)}, bf16[1024,128]{1,0:T(8,128)(2,1)S(1)}, u32[]{:S(2)}, u32[]{:S(2)}) collective-permute-start(bf16[1024,128]{1,0:T(8,128)(2,1)S(1)} %get-tuple-element.27), channel_id=1, source_target_pairs={{0,2},{1,3},{2,0},{3,1},{4,6},{5,7},{6,4},{7,5},{8,10},{9,11},{10,... | collective-permute-start | bytes 786440 | tf_op jit(solution)/shard_map/ppermute | solution.py:447
  47.2 1.8 %collective-permute-start = (bf16[512,128]{1,0:T(8,128)(2,1)S(1)}, bf16[512,128]{1,0:T(8,128)(2,1)S(1)}, u32[]{:S(2)}, u32[]{:S(2)}) collective-permute-start(bf16[512,128]{1,0:T(8,128)(2,1)S(1)} %forward.3), channel_id=1, source_target_pairs={{0,1},{1,0},{2,3},{3,2},{4,5},{5,4},{6,7},{7,6},{8,9},{9,8},{10,11... | collective-permute-start | bytes 393224 | tf_op jit(solution)/shard_map/ppermute | solution.py:447
  47.3 31.1 %collective-permute-start.3 = (bf16[1024,128]{1,0:T(8,128)(2,1)S(1)}, bf16[1024,128]{1,0:T(8,128)(2,1)S(1)}, u32[]{:S(2)}, u32[]{:S(2)}) collective-permute-start(bf16[1024,128]{1,0:T(8,128)(2,1)S(1)} %get-tuple-element.33), channel_id=1, source_target_pairs={{0,4},{1,5},{2,6},{3,7},{4,0},{5,1},{6,2},{7,3},{8,12},{9,13},{10,... | collective-permute-start | bytes 786440 | tf_op jit(solution)/shard_map/ppermute | solution.py:447
  48.8 29.6 %collective-permute-start.4 = (bf16[1024,128]{1,0:T(8,128)(2,1)S(1)}, bf16[1024,128]{1,0:T(8,128)(2,1)S(1)}, u32[]{:S(2)}, u32[]{:S(2)}) collective-permute-start(bf16[1024,128]{1,0:T(8,128)(2,1)S(1)} %get-tuple-element.34), channel_id=1, source_target_pairs={{0,6},{1,7},{2,4},{3,5},{4,2},{5,3},{6,0},{7,1},{8,14},{9,15},{10,... | collective-permute-start | bytes 786440 | tf_op jit(solution)/shard_map/ppermute | solution.py:447
  63.9 1.4 %collective-permute-start.2 = (bf16[512,128]{1,0:T(8,128)(2,1)S(1)}, bf16[512,128]{1,0:T(8,128)(2,1)S(1)}, u32[]{:S(2)}, u32[]{:S(2)}) collective-permute-start(bf16[512,128]{1,0:T(8,128)(2,1)S(1)} %forward.4), channel_id=1, source_target_pairs={{0,1},{1,0},{2,3},{3,2},{4,5},{5,4},{6,7},{7,6},{8,9},{9,8},{10,11... | collective-permute-start | bytes 393224 | tf_op jit(solution)/shard_map/ppermute | solution.py:447
  78.5 10.7 %collective-permute-start.5 = (bf16[1024,128]{1,0:T(8,128)(2,1)S(1)}, bf16[1024,128]{1,0:T(8,128)(2,1)S(1)}, u32[]{:S(2)}, u32[]{:S(2)}) collective-permute-start(bf16[1024,128]{1,0:T(8,128)(2,1)S(1)} %forward.5), channel_id=1, source_target_pairs={{0,1},{1,0},{2,3},{3,2},{4,5},{5,4},{6,7},{7,6},{8,9},{9,8},{10,11... | collective-permute-start | bytes 786440 | tf_op jit(solution)/shard_map/ppermute | solution.py:447

commit v8 on v7

--- a/solution.py
+++ b/solution.py
@@ -421,9 +421,12 @@
         return pltpu.make_async_copy(source, out_ref.at[i, :, there], sems.at[k, n, i])
 
     every = [(n, i) for n in range(len(LAST)) for i in range(local)]
-    for n, i in every:
-        send(0, n, i).start()
-    after = lambda n, i: send(1, n, i).start()
+    def after(n, i):
+        t = every.index((n, i))
+        for e in every[2 * t : 2 * t + 2]:
+            send(0, *e).start()
+        send(1, n, i).start()
+
     large, redo = attend_half(chips, False, stat_ref, moved_ref, works, held_ref, out_ref.shape[2] // HEAD, after)
     for k in range(2):
         for n, i in every:

time: 102 us -> 102 us (level)
  no operation moved by 1% of the time
where the time goes in v8:
time: 102 us
  Pallas kernels  87.8 us (86%)
  starting transfers between devices  11.4 us (11%)
  waiting for transfers between devices  1.35 us (1%)
    pallas_call x1, Pallas kernels, body(): pl.pallas_call(attend_new, grid=(local,), out_shape=[jax.ShapeDtypeStruct...  33.6 us
    pallas_call x1, Pallas kernels, body(): pl.pallas_call(functools.partial(attend_first, chips), out_shape=[result,...  14.9 us
    pallas_call x1, Pallas kernels, body(): pl.pallas_call(functools.partial(attend_second, chips), out_shape=[result...  13.1 us
    pallas_call x1, Pallas kernels, body(): pl.pallas_call(functools.partial(attend_last, chips), out_shape=result, i...  12.4 us
    pallas_call x1, Pallas kernels, body(): pl.pallas_call(functools.partial(attend_own, chips, width // HEAD), out_s...  10.5 us
    all_to_all x1, starting transfers between devices, body(): table = lax.all_to_all(packed, 'beam', 0, 0)  7.4 us
    ppermute x6, starting transfers between devices, swap(): return lax.ppermute(a, 'beam', [(i, i ^ distance) for i in range(count)])  4.01 us
    pallas_call x1, Pallas kernels, body(): pl.pallas_call(pack, out_shape=jax.ShapeDtypeStruct((beam_count, message,...  2.47 us
  transfers between devices with their start and end apart: 7, of which 1 were waited for; matrix products, arithmetic and copies ran while one was open for 0% of the time, Pallas kernels for 71%

profile of v8, /device:TPU:0, one launch (start us, length us, event | category | flops | bytes accessed | tf_op | source)
XLA Modules:
  0.0 101.8 jit_solution(448695503799015493)
XLA Ops:
  0.6 0.0 copy-start
  0.6 2.5 %pack.1 = bf16[16,272,128]{2,1,0:T(8,128)(2,1)} custom-call(s32[1,64]{1,0:T(1,128)} %bitcast.4, bf16[4,2,64,1024]{3,2,1,0:T(8,128)(2,1)} %kv_hbm.1, bf16[4,4096]{1,0:T(4,128)(2,1)} %last_hbm.1, f32[1,4096]{1,0:T(1,128)} %bitcast.3), custom_call_target="tpu_custom_call" | custom-call | tf_op jit(solution)/shard_map/pack/pallas_call | solution.py:471
  3.1 7.4 %all-to-all-start = ((bf16[16,272,128]{2,1,0:T(8,128)(2,1)}), bf16[16,272,128]{2,1,0:T(8,128)(2,1)S(1)}, u32[]{:S(2)}, u32[]{:S(2)}) async-start(bf16[16,272,128]{2,1,0:T(8,128)(2,1)} %pack.1), calls=%async_computation | async-start | bytes 2228224 | tf_op jit(solution)/shard_map/all_to_all | solution.py:488
  10.5 0.0 copy-done
  10.6 0.2 and_reduce_fusion
  10.8 0.0 copy-start.1
  10.8 0.1 dynamic_slice.3.item_ref.refs_1_
  10.9 33.6 %attend_new.1 = (bf16[4,256,4096]{2,1,0:T(8,128)(2,1)}, bf16[4,256,128]{2,1,0:T(8,128)(2,1)}) custom-call(bf16[4,256,4096]{2,1,0:T(8,128)(2,1)} %q_ref.5, bf16[4,256,1024]{2,1,0:T(8,128)(2,1)} %k_ref.1, bf16[4,256,1024]{2,1,0:T(8,128)(2,1)} %v_ref.1), custom_call_target="tpu_custom_call" | custom-call | flops 4294967296 | bytes 25165824 | tf_op jit(solution)/shard_map/attend_new/pallas_call | solution.py:493
  44.4 0.0 copy-done.1
  44.4 0.0 all-to-all-done.table_ref
  44.4 0.8 pick.1
  45.2 2.0 %collective-permute-start.1 = (bf16[1024,128]{1,0:T(8,128)(2,1)S(1)}, bf16[1024,128]{1,0:T(8,128)(2,1)S(1)}, u32[]{:S(2)}, u32[]{:S(2)}) collective-permute-start(bf16[1024,128]{1,0:T(8,128)(2,1)S(1)} %get-tuple-element.27), channel_id=1, source_target_pairs={{0,2},{1,3},{2,0},{3,1},{4,6},{5,7},{6,4},{7,5},{8,10},{9,11},{10,... | collective-permute-start | bytes 786440 | tf_op jit(solution)/shard_map/ppermute | solution.py:450
  47.2 0.1 collective-permute-start
  47.3 1.5 %collective-permute-start.3 = (bf16[1024,128]{1,0:T(8,128)(2,1)S(1)}, bf16[1024,128]{1,0:T(8,128)(2,1)S(1)}, u32[]{:S(2)}, u32[]{:S(2)}) collective-permute-start(bf16[1024,128]{1,0:T(8,128)(2,1)S(1)} %get-tuple-element.33), channel_id=1, source_target_pairs={{0,4},{1,5},{2,6},{3,7},{4,0},{5,1},{6,2},{7,3},{8,12},{9,13},{10,... | collective-permute-start | bytes 786440 | tf_op jit(solution)/shard_map/ppermute | solution.py:450
  48.8 0.2 collective-permute-start.4
  49.0 0.0 collective-permute-done.other_ref
  49.0 14.9 %attend_first.1 = (bf16[4,256,4096]{2,1,0:T(8,128)(2,1)}, f32[1,4]{1,0:T(1,128)}, bf16[4,256,1024]{2,1,0:T(8,128)(2,1)S(1)}, bf16[4,256,1024]{2,1,0:T(8,128)(2,1...) custom-call(s32[64]{0:T(128)} %copy-done.1, bf16[16,272,128]{2,1,0:T(8,128)(2,1)S(1)} %all-to-all-done.table_ref, ...), custom_call_target="tpu_custom_call" | custom-call | flops 1024 | bytes 1024 | tf_op jit(solution)/shard_map/attend_first/pallas_call | solution.py:545
  63.9 0.0 collective-permute-done.1.refs_0_.own_ref
  63.9 0.1 collective-permute-start.2
  64.0 1.3 %collective-permute-done.2.other_ref = bf16[512,128]{1,0:T(8,128)(2,1)S(1)} collective-permute-done((bf16[512,128]{1,0:T(8,128)(2,1)S(1)}, bf16[512,128]{1,0:T(8,128)(2,1)S(1)}, u32[]{:S(2)}, u32[]{:S(2)}) %collective-permute-start.2) | collective-permute-done | bytes 131104 | tf_op jit(solution)/shard_map/ppermute | solution.py:450
  65.3 13.1 %attend_second.1 = (bf16[4,256,4096]{2,1,0:T(8,128)(2,1)}, f32[8,128]{1,0:T(8,128)S(1)}, bf16[4,256,1024]{2,1,0:T(8,128)(2,1)S(1)}, bf16[4,256,1024]{2,1,0:T(8,1...) custom-call(bf16[4,256,4096]{2,1,0:T(8,128)(2,1)} %q_ref.5, ...), custom_call_target="tpu_custom_call", output_to_operand_aliasing={{0}: (8, {})} | custom-call | flops 1024 | bytes 1024 | tf_op jit(solution)/shard_map/attend_second/pallas_call | solution.py:565
  78.4 0.0 collective-permute-done.3.refs_0_.refs_2_
  78.4 0.0 collective-permute-done.4.refs_1_.refs_5_
  78.5 0.2 collective-permute-start.5
  78.7 10.5 %attend_own.1.refs_5_ = bf16[2,4,256,1024]{3,2,1,0:T(8,128)(2,1)S(1)} custom-call(bf16[4,256,128]{2,1,0:T(8,128)(2,1)S(1)} %get-tuple-element.23.stat_ref, f32[8,128]{1,0:T(8,128)S(1)} %get-tuple-element.24.refs_1_.moved_ref, bf16[4,256,1024]{2,1,0:T(8,128)(2,1)S(1)} %get-tuple-element.29.refs_0_, bf16[4,256,1024]{2,1,0:T(8,128)(2,1)S(1)} %get-tuple-element.30.refs_1_, ...), custom_call_target="tpu_custom_call" | custom-call | flops 1024 | bytes 1024 | tf_op jit(solution)/shard_map/attend_own/pallas_call | solution.py:591
  89.2 0.0 collective-permute-done.5.refs_4_
  89.2 12.4 %attend_last.1 = bf16[4,256,4096]{2,1,0:T(8,128)(2,1)} custom-call(bf16[4,256,128]{2,1,0:T(8,128)(2,1)S(1)} %get-tuple-element.23.stat_ref, f32[8,128]{1,0:T(8,128)S(1)} %get-tuple-element.24.refs_1_.moved_ref, bf16[4,256,1024]{2,1,0:T(8,128)(2,1)S(1)} %get-tuple-element.29.refs_0_, ...), custom_call_target="tpu_custom_call", output_to_operand_aliasing={{}: (8, {})} | custom-call | flops 1024 | bytes 1024 | tf_op jit(solution)/shard_map/attend_last/pallas_call | solution.py:600
  (5 shorter events, 0.1 us)
Async XLA Ops:
  0.6 9.9 %copy-start = (s32[64]{0:T(128)S(1)}, s32[64]{0:T(128)}, u32[]{:S(2)}) copy-start(s32[64]{0:T(128)} %param.13) | copy-start | bytes 772
  3.1 41.3 %all-to-all-start = ((bf16[16,272,128]{2,1,0:T(8,128)(2,1)}), bf16[16,272,128]{2,1,0:T(8,128)(2,1)S(1)}, u32[]{:S(2)}, u32[]{:S(2)}) async-start(bf16[16,272,128]{2,1,0:T(8,128)(2,1)} %pack.1), calls=%async_computation | async-start | bytes 2228224 | tf_op jit(solution)/shard_map/all_to_all | solution.py:488
  10.8 33.7 %copy-start.1 = (s32[64]{0:T(128)}, s32[64]{0:T(128)S(1)}, u32[]{:S(2)}) copy-start(s32[64]{0:T(128)S(1)} %convert_add_fusion.item_ref) | copy-start | bytes 772
  45.2 18.6 %collective-permute-start.1 = (bf16[1024,128]{1,0:T(8,128)(2,1)S(1)}, bf16[1024,128]{1,0:T(8,128)(2,1)S(1)}, u32[]{:S(2)}, u32[]{:S(2)}) collective-permute-start(bf16[1024,128]{1,0:T(8,128)(2,1)S(1)} %get-tuple-element.27), channel_id=1, source_target_pairs={{0,2},{1,3},{2,0},{3,1},{4,6},{5,7},{6,4},{7,5},{8,10},{9,11},{10,... | collective-permute-start | bytes 786440 | tf_op jit(solution)/shard_map/ppermute | solution.py:450
  47.2 1.8 %collective-permute-start = (bf16[512,128]{1,0:T(8,128)(2,1)S(1)}, bf16[512,128]{1,0:T(8,128)(2,1)S(1)}, u32[]{:S(2)}, u32[]{:S(2)}) collective-permute-start(bf16[512,128]{1,0:T(8,128)(2,1)S(1)} %forward.3), channel_id=1, source_target_pairs={{0,1},{1,0},{2,3},{3,2},{4,5},{5,4},{6,7},{7,6},{8,9},{9,8},{10,11... | collective-permute-start | bytes 393224 | tf_op jit(solution)/shard_map/ppermute | solution.py:450
  47.3 31.1 %collective-permute-start.3 = (bf16[1024,128]{1,0:T(8,128)(2,1)S(1)}, bf16[1024,128]{1,0:T(8,128)(2,1)S(1)}, u32[]{:S(2)}, u32[]{:S(2)}) collective-permute-start(bf16[1024,128]{1,0:T(8,128)(2,1)S(1)} %get-tuple-element.33), channel_id=1, source_target_pairs={{0,4},{1,5},{2,6},{3,7},{4,0},{5,1},{6,2},{7,3},{8,12},{9,13},{10,... | collective-permute-start | bytes 786440 | tf_op jit(solution)/shard_map/ppermute | solution.py:450
  48.8 29.6 %collective-permute-start.4 = (bf16[1024,128]{1,0:T(8,128)(2,1)S(1)}, bf16[1024,128]{1,0:T(8,128)(2,1)S(1)}, u32[]{:S(2)}, u32[]{:S(2)}) collective-permute-start(bf16[1024,128]{1,0:T(8,128)(2,1)S(1)} %get-tuple-element.34), channel_id=1, source_target_pairs={{0,6},{1,7},{2,4},{3,5},{4,2},{5,3},{6,0},{7,1},{8,14},{9,15},{10,... | collective-permute-start | bytes 786440 | tf_op jit(solution)/shard_map/ppermute | solution.py:450
  63.9 1.4 %collective-permute-start.2 = (bf16[512,128]{1,0:T(8,128)(2,1)S(1)}, bf16[512,128]{1,0:T(8,128)(2,1)S(1)}, u32[]{:S(2)}, u32[]{:S(2)}) collective-permute-start(bf16[512,128]{1,0:T(8,128)(2,1)S(1)} %forward.4), channel_id=1, source_target_pairs={{0,1},{1,0},{2,3},{3,2},{4,5},{5,4},{6,7},{7,6},{8,9},{9,8},{10,11... | collective-permute-start | bytes 393224 | tf_op jit(solution)/shard_map/ppermute | solution.py:450
  78.5 10.7 %collective-permute-start.5 = (bf16[1024,128]{1,0:T(8,128)(2,1)S(1)}, bf16[1024,128]{1,0:T(8,128)(2,1)S(1)}, u32[]{:S(2)}, u32[]{:S(2)}) collective-permute-start(bf16[1024,128]{1,0:T(8,128)(2,1)S(1)} %forward.5), channel_id=1, source_target_pairs={{0,1},{1,0},{2,3},{3,2},{4,5},{5,4},{6,7},{7,6},{8,9},{9,8},{10,11... | collective-permute-start | bytes 786440 | tf_op jit(solution)/shard_map/ppermute | solution.py:450
